TPU v7x, 128 devices: a whole 4x4x4 slice. The times are simulated.
128 devices in a mesh: dp: 32 (over x_lo, z, y), tensor: 4 (over x_hi, core).
Axes of the slice: x: 4 (x_hi: 2, x_lo: 2; x = x_hi * 2 + x_lo), y: 4, z: 4, core: 2. Of those that a mesh axis runs over, the one named last changes fastest.
Arguments:
- x_in: bfloat16 [32, 1024, 768], P('dp', 'tensor'), may hold values from -6 to 6
- segments: int32 [32, 1024], P('dp'), may hold values from 0 to 7, never falling along the last dimension, each value on 1 to 800 neighbouring positions
- attn_w: float32 [2, 4, 768, 768], P(None, None, 'dp', 'tensor'), may hold values from -0.21875 to 0.21875
- mlp_w: float32 [2, 2, 768, 4, 768], P(None, None, 'dp', None, 'tensor'), may hold values from -0.21875 to 0.21875
- in_bias: float32 [2, 7, 768], P(None, None, 'tensor'), may hold values from -3 to 3
- vectors: float32 [2, 6, 768], replicated, may hold values from 0.1 to 1.9
- mom_attn: float32 [2, 4, 768, 768], P(None, None, 'dp', 'tensor'), may hold values from -320 to 320
- mom_mlp: float32 [2, 2, 768, 4, 768], P(None, None, 'dp', None, 'tensor'), may hold values from -320 to 320
- mom_bias: float32 [2, 7, 768], P(None, None, 'tensor'), may hold values from -320 to 320
- mom_vec: float32 [2, 6, 768], replicated, may hold values from -512 to 512
- cotangent: float32 [32, 1024, 768], P('dp', 'tensor'), may hold values from -6 to 6
Outputs:
- out_act: float32 [32, 1024, 768], P('dp', 'tensor')
- grad_in: float32 [32, 1024, 768], P('dp', 'tensor')
- new_mom_attn: float32 [2, 4, 768, 768], P(None, None, 'dp', 'tensor')
- new_attn_w: float32 [2, 4, 768, 768], P(None, None, 'dp', 'tensor')
- new_mom_mlp: float32 [2, 2, 768, 4, 768], P(None, None, 'dp', None, 'tensor')
- new_mlp_w: float32 [2, 2, 768, 4, 768], P(None, None, 'dp', None, 'tensor')
- new_mom_bias: float32 [2, 7, 768], P(None, None, 'tensor')
- new_in_bias: float32 [2, 7, 768], P(None, None, 'tensor')
- new_mom_vec: float32 [2, 6, 768], replicated
- new_vectors: float32 [2, 6, 768], replicated
Inputs may be any that keep to these rules, and one draw needn't show every extreme that they name: `segments`: in every sequence segment numbers never fall, every document has 1 to 800 tokens, and one has exactly 800.
All inputs are finite; a program needn't handle non-finite values.
Results may differ from a plain program's by a relative error of at most 0.018.
The roundings to bfloat16 on the way count: a program that leaves them out, or rounds other values in their place, can miss the bound.
Values may be sent and summed in bfloat16 or wider, within the bound.
No kernel may reach another device: no remote copies, remote signals or barrier semaphores. Data moves between devices by JAX's collectives and lax.ppermute only.
A program may use at most 192 MiB of HBM per device.

v0:
```python
import math

import jax
import jax.numpy as jnp
from jax import lax
from jax.sharding import PartitionSpec as P

D = 768
FF = 3072
HD = 64
ROT = 16
NS_STEPS = 5


EPS_NORM = 1e-05
EPS_ORTH = 1e-07
COEF_A = 3.4445
COEF_B = -4.775
COEF_C = 2.0315
MOMENTUM = 0.95
STEP_SCALE = 0.4
RATE_VEC = 0.5
NEG_FILL = -1e30
PRECISE = lax.Precision.HIGHEST


def normalize(stream, gain_row, shift_row):
    center = stream - jnp.mean(stream, -1, keepdims=True)
    inverse = lax.rsqrt(jnp.mean(center * center, -1, keepdims=True) + EPS_NORM)
    scaled = center * inverse
    return (scaled * gain_row + shift_row, scaled, inverse)


def norm_back(upstream, scaled, inverse, gain_row):
    weighted = upstream * gain_row
    return inverse * (
        weighted
        - jnp.mean(weighted, -1, keepdims=True)
        - scaled * jnp.mean(weighted * scaled, -1, keepdims=True)
    )


def rope_tables(segments):
    length = segments.shape[-1]
    earlier = jnp.sum((segments[:, None, :] < segments[:, :, None]).astype(jnp.int32), -1)
    places = jnp.arange(length, dtype=jnp.int32)[None, :] - earlier
    frequency = 10000.0 ** (jnp.arange(ROT // 2, dtype=jnp.float32) * (-2.0 / ROT))
    angles = places.astype(jnp.float32)[:, :, None] * frequency
    return (jnp.cos(angles)[:, :, None, :], jnp.sin(angles)[:, :, None, :])


def rotate(heads_in, cosine_table, sine_table):
    half_rot = ROT // 2
    leading = heads_in[..., :half_rot]
    trailing = heads_in[..., half_rot:ROT]
    return jnp.concatenate(
        [
            leading * cosine_table - trailing * sine_table,
            trailing * cosine_table + leading * sine_table,
            heads_in[..., ROT:],
        ],
        -1,
    )


def rotate_back(upstream, cosine_table, sine_table):
    half_rot = ROT // 2
    leading = upstream[..., :half_rot]
    trailing = upstream[..., half_rot:ROT]
    return jnp.concatenate(
        [
            leading * cosine_table + trailing * sine_table,
            trailing * cosine_table - leading * sine_table,
            upstream[..., ROT:],
        ],
        -1,
    )


def gelu_slope(pre_act):
    return (
        0.5 * (1.0 + jax.scipy.special.erf(pre_act * 0.7071067811865476))
        + pre_act * jnp.exp(-0.5 * pre_act * pre_act) * 0.3989422804014327
    )


def regroup(stacked, local_len):
    batch_size, span_rows = (stacked.shape[0], stacked.shape[1])
    trailing_shape = stacked.shape[2:]
    split_view = stacked.reshape((batch_size, span_rows // local_len, local_len) + trailing_shape)
    return jnp.swapaxes(split_view, 0, 1).reshape((span_rows * batch_size,) + trailing_shape)


def attend_forward(queries, key_rows, values, allowed):
    length = queries.shape[1]
    factor = queries.shape[-1] ** (-0.5)
    block_rows = min(512, length)
    out_blocks = []
    total_blocks = []
    for start_row in range(0, length, block_rows):
        end_row = start_row + block_rows
        scores = (
            jnp.einsum(
                "bqhd,bkhd->bhqk",
                queries[:, start_row:end_row],
                key_rows,
                preferred_element_type=jnp.float32,
            )
            * factor
        )
        scores = jnp.where(allowed[:, None, start_row:end_row], scores, NEG_FILL)
        row_max = jnp.max(scores, -1, keepdims=True)
        shifted = jnp.exp(scores - row_max)
        row_total = jnp.sum(shifted, -1, keepdims=True)
        probability = (shifted / row_total).astype(jnp.bfloat16)
        out_blocks.append(
            jnp.einsum("bhqk,bkhd->bqhd", probability, values, preferred_element_type=jnp.float32)
        )
        total_blocks.append(row_max + jnp.log(row_total))
    return (jnp.concatenate(out_blocks, 1), jnp.concatenate(total_blocks, 2))


def attend_backward(queries, key_rows, values, allowed, log_total, d_mixed):
    length = queries.shape[1]
    factor = queries.shape[-1] ** (-0.5)
    block_rows = min(512, length)
    query_grads = []
    key_grad = jnp.zeros(key_rows.shape, jnp.float32)
    value_grad = jnp.zeros(values.shape, jnp.float32)
    for start_row in range(0, length, block_rows):
        end_row = start_row + block_rows
        query_block = queries[:, start_row:end_row]
        grad_block = d_mixed[:, start_row:end_row]
        scores = (
            jnp.einsum("bqhd,bkhd->bhqk", query_block, key_rows, preferred_element_type=jnp.float32)
            * factor
        )
        probability = jnp.where(
            allowed[:, None, start_row:end_row],
            jnp.exp(scores - log_total[:, :, start_row:end_row]),
            0.0,
        )
        prob_grad = jnp.einsum(
            "bqhd,bkhd->bhqk", grad_block, values, preferred_element_type=jnp.float32
        )
        score_grad = (
            probability * (prob_grad - jnp.sum(probability * prob_grad, -1, keepdims=True))
        ).astype(jnp.bfloat16)
        query_grads.append(
            jnp.einsum("bhqk,bkhd->bqhd", score_grad, key_rows, preferred_element_type=jnp.float32)
            * factor
        )
        key_grad = (
            key_grad
            + jnp.einsum(
                "bhqk,bqhd->bkhd", score_grad, query_block, preferred_element_type=jnp.float32
            )
            * factor
        )
        value_grad = value_grad + jnp.einsum(
            "bhqk,bqhd->bkhd",
            probability.astype(jnp.bfloat16),
            grad_block,
            preferred_element_type=jnp.float32,
        )
    return (jnp.concatenate(query_grads, 1), key_grad, value_grad)


def forward_layer(stream, weight_pair, bias_rows, vector_rows, cosine_table, sine_table, allowed):
    attn_full, mlp_full = weight_pair
    batch_size, local_len, model_width = stream.shape
    normed_one = normalize(stream, vector_rows[0], vector_rows[1])[0].astype(jnp.bfloat16)
    normed_two = normalize(stream, vector_rows[2], vector_rows[3])[0].astype(jnp.bfloat16)
    first_normed, second_normed = (
        lax.all_gather(normed_one, "tensor", axis=1, tiled=True),
        lax.all_gather(normed_two, "tensor", axis=1, tiled=True),
    )
    length = first_normed.shape[1]
    local_cols = attn_full.shape[2]
    projected = (
        jnp.einsum("bsd,mdh->bsmh", first_normed, attn_full[:3], preferred_element_type=jnp.float32)
        + bias_rows[:3]
    )
    head_view = projected.reshape(batch_size, length, 3, local_cols // HD, HD)
    queries = rotate(head_view[:, :, 0], cosine_table, sine_table).astype(jnp.bfloat16)
    key_rows = rotate(head_view[:, :, 1], cosine_table, sine_table).astype(jnp.bfloat16)
    values = head_view[:, :, 2].astype(jnp.bfloat16)
    mixed_heads, log_total = attend_forward(queries, key_rows, values, allowed)
    mixed_heads = mixed_heads.reshape(batch_size, length, local_cols).astype(jnp.bfloat16)
    pre_act = (
        jnp.einsum("bsd,drc->bsrc", second_normed, mlp_full[0], preferred_element_type=jnp.float32)
        + bias_rows[3:]
    )
    hidden = jax.nn.gelu(pre_act, approximate=False).astype(jnp.bfloat16)
    output_part = jnp.einsum(
        "bsh,dh->bsd", mixed_heads, attn_full[3], preferred_element_type=jnp.float32
    ) + jnp.einsum("bsrc,drc->bsd", hidden, mlp_full[1], preferred_element_type=jnp.float32)
    branch = lax.psum_scatter(
        regroup(output_part, local_len), "tensor", scatter_dimension=0, tiled=True
    )
    branch = branch.reshape(batch_size, local_len, model_width)
    record = (
        stream,
        first_normed,
        second_normed,
        queries,
        key_rows,
        values,
        log_total,
        mixed_heads,
        pre_act,
        hidden,
    )
    return (record, stream + branch + vector_rows[4] + vector_rows[5])


def backward_layer(upstream, record, weight_pair, vector_rows, cosine_table, sine_table, allowed):
    (
        stream,
        first_normed,
        second_normed,
        queries,
        key_rows,
        values,
        log_total,
        mixed_heads,
        pre_act,
        hidden,
    ) = record
    attn_full, mlp_full = weight_pair
    batch_size, local_len, model_width = upstream.shape
    length = queries.shape[1]
    local_cols = attn_full.shape[2]
    outer_grad = lax.all_gather(upstream.astype(jnp.bfloat16), "tensor", axis=1, tiled=True)
    d_mixed = jnp.einsum(
        "bsd,dh->bsh", outer_grad, attn_full[3], preferred_element_type=jnp.float32
    ).astype(jnp.bfloat16)
    grad_out = jnp.einsum(
        "bsd,bsh->dh", outer_grad, mixed_heads, preferred_element_type=jnp.float32
    )
    d_hidden = jnp.einsum(
        "bsd,drc->bsrc", outer_grad, mlp_full[1], preferred_element_type=jnp.float32
    )
    grad_down = jnp.einsum("bsd,bsrc->drc", outer_grad, hidden, preferred_element_type=jnp.float32)
    d_pre = (d_hidden * gelu_slope(pre_act)).astype(jnp.bfloat16)
    grad_up = jnp.einsum("bsd,bsrc->drc", second_normed, d_pre, preferred_element_type=jnp.float32)
    query_grad, key_grad, value_grad = attend_backward(
        queries,
        key_rows,
        values,
        allowed,
        log_total,
        d_mixed.reshape(batch_size, length, local_cols // HD, HD),
    )
    query_grad = rotate_back(query_grad, cosine_table, sine_table).reshape(
        batch_size, length, local_cols
    )
    key_grad = rotate_back(key_grad, cosine_table, sine_table).reshape(
        batch_size, length, local_cols
    )
    value_grad = value_grad.reshape(batch_size, length, local_cols)
    d_proj = jnp.stack([query_grad, key_grad, value_grad], 2).astype(jnp.bfloat16)
    grad_qkv = jnp.einsum("bsd,bsmh->mdh", first_normed, d_proj, preferred_element_type=jnp.float32)
    grad_bias = jnp.concatenate(
        [jnp.sum(d_proj.astype(jnp.float32), (0, 1)), jnp.sum(d_pre.astype(jnp.float32), (0, 1))], 0
    )
    back_first = jnp.einsum(
        "bsmh,mdh->bsd", d_proj, attn_full[:3], preferred_element_type=jnp.float32
    )
    back_second = jnp.einsum(
        "bsrc,drc->bsd", d_pre, mlp_full[0], preferred_element_type=jnp.float32
    )
    d_norm = lax.psum_scatter(
        regroup(jnp.stack([back_first, back_second], 2), local_len),
        "tensor",
        scatter_dimension=0,
        tiled=True,
    )
    d_norm = d_norm.reshape(batch_size, local_len, 2, model_width)
    norm_one, scaled_one, inverse_one = normalize(stream, vector_rows[0], vector_rows[1])
    norm_two, scaled_two, inverse_two = normalize(stream, vector_rows[2], vector_rows[3])
    d_first = d_norm[:, :, 0]
    d_second = d_norm[:, :, 1]
    new_upstream = (
        upstream
        + norm_back(d_first, scaled_one, inverse_one, vector_rows[0])
        + norm_back(d_second, scaled_two, inverse_two, vector_rows[2])
    )
    token_sum = jnp.sum(upstream, (0, 1))
    grad_vector = jnp.stack(
        [
            jnp.sum(d_first * scaled_one, (0, 1)),
            jnp.sum(d_first, (0, 1)),
            jnp.sum(d_second * scaled_two, (0, 1)),
            jnp.sum(d_second, (0, 1)),
            token_sum,
            token_sum,
        ]
    )
    grad_attn = jnp.concatenate([grad_qkv, grad_out[None]], 0)
    grad_mlp = jnp.stack([grad_up, grad_down])
    shard_attn, shard_mlp = (
        lax.psum_scatter(grad_attn, "dp", scatter_dimension=1, tiled=True),
        lax.psum_scatter(grad_mlp, "dp", scatter_dimension=1, tiled=True),
    )
    return (new_upstream, shard_attn, shard_mlp, grad_vector, grad_bias)


def gram_of(current):
    return lax.psum(jnp.dot(current, current.T, precision=PRECISE), "tensor")


def orthogonalize(matrix):
    gram_matrix = gram_of(matrix)
    frob_norm = jnp.sqrt(jnp.trace(gram_matrix)) + EPS_ORTH
    current = matrix / frob_norm
    gram_matrix = gram_matrix / (frob_norm * frob_norm)
    for ns_step in range(NS_STEPS):
        if ns_step > 0:
            gram_matrix = gram_of(current)
        polynomial = COEF_B * gram_matrix + COEF_C * jnp.dot(
            gram_matrix, gram_matrix, precision=PRECISE
        )
        current = COEF_A * current + jnp.dot(polynomial, current, precision=PRECISE)
    return current


def per_device(
    x_in, segments, attn_w, mlp_w, in_bias, vectors, mom_attn, mom_mlp, mom_bias, mom_vec, cotangent
):
    batch_size, local_len, model_width = x_in.shape
    groups = lax.axis_size("dp")
    layer_count = attn_w.shape[0]
    local_cols = attn_w.shape[3]
    full_len = segments.shape[1]
    cosine_table, sine_table = rope_tables(segments)
    places = jnp.arange(full_len, dtype=jnp.int32)
    allowed = (segments[:, :, None] == segments[:, None, :]) & (
        places[None, :, None] >= places[None, None, :]
    )
    stream = x_in.astype(jnp.float32)
    saved = []
    for layer_index in range(layer_count):
        weight_pair = (
            lax.all_gather(attn_w[layer_index].astype(jnp.bfloat16), "dp", axis=1, tiled=True),
            lax.all_gather(mlp_w[layer_index].astype(jnp.bfloat16), "dp", axis=1, tiled=True),
        )
        record, stream = forward_layer(
            stream,
            weight_pair,
            in_bias[layer_index],
            vectors[layer_index],
            cosine_table,
            sine_table,
            allowed,
        )
        saved.append((record, weight_pair))
    upstream = cotangent
    attn_grads, mlp_grads, vector_grads, bias_grads = ([], [], [], [])
    for layer_index in reversed(range(layer_count)):
        record, weight_pair = saved[layer_index]
        weight_pair = (
            lax.all_gather(attn_w[layer_index].astype(jnp.bfloat16), "dp", axis=1, tiled=True),
            lax.all_gather(mlp_w[layer_index].astype(jnp.bfloat16), "dp", axis=1, tiled=True),
        )
        upstream, shard_attn, shard_mlp, grad_vector, grad_bias = backward_layer(
            upstream, record, weight_pair, vectors[layer_index], cosine_table, sine_table, allowed
        )
        attn_grads.insert(0, shard_attn)
        mlp_grads.insert(0, shard_mlp)
        vector_grads.insert(0, grad_vector)
        bias_grads.insert(0, grad_bias)
    bias_local = jnp.stack(bias_grads)
    spread_bias = jnp.zeros((layer_count, bias_local.shape[1], model_width), jnp.float32)
    spread_bias = lax.dynamic_update_slice_in_dim(
        spread_bias, bias_local, lax.axis_index("tensor") * local_cols, 2
    )
    vector_total, bias_total = lax.psum((jnp.stack(vector_grads), spread_bias), ("dp", "tensor"))
    bias_total = lax.dynamic_slice_in_dim(
        bias_total, lax.axis_index("tensor") * local_cols, local_cols, 2
    )
    new_mom_attn = MOMENTUM * mom_attn + jnp.stack(attn_grads)
    new_mom_mlp = MOMENTUM * mom_mlp + jnp.stack(mlp_grads)
    new_mom_bias = MOMENTUM * mom_bias + bias_total
    new_mom_vec = MOMENTUM * mom_vec + vector_total
    row_count = attn_w.shape[2]
    wide_cols = mlp_w.shape[3] * mlp_w.shape[4]
    pieces = []
    for layer_index in range(layer_count):
        for matrix_index in range(4):
            pieces.append(
                jnp.pad(
                    new_mom_attn[layer_index, matrix_index], ((0, 0), (0, wide_cols - local_cols))
                )
            )
        for matrix_index in range(2):
            pieces.append(new_mom_mlp[layer_index, matrix_index].reshape(row_count, wide_cols))
    stacked = jnp.stack(pieces)
    matrix_count = stacked.shape[0]
    whole = lax.all_gather(stacked, "dp", axis=1, tiled=True)
    my_group = lax.axis_index("dp")
    labels = jnp.arange(matrix_count, dtype=jnp.int32)
    result = jnp.zeros(whole.shape, jnp.float32)
    picked = my_group + 0
    chosen = lax.dynamic_index_in_dim(
        whole, jnp.minimum(picked, matrix_count - 1), 0, keepdims=False
    )
    chosen = jnp.where(picked < matrix_count, chosen, 0.0)
    finished = orthogonalize(chosen)
    result = result + jnp.where((labels == picked)[:, None, None], finished[None], 0.0)
    returned = lax.psum_scatter(result, "dp", scatter_dimension=1, tiled=True)
    attn_orth = jnp.stack(
        [
            jnp.stack(
                [
                    returned[layer_index * 6 + matrix_index][:, :local_cols]
                    for matrix_index in range(4)
                ]
            )
            for layer_index in range(layer_count)
        ]
    )
    mlp_orth = jnp.stack(
        [
            jnp.stack(
                [
                    returned[layer_index * 6 + 4 + matrix_index].reshape(mlp_w.shape[2:])
                    for matrix_index in range(2)
                ]
            )
            for layer_index in range(layer_count)
        ]
    )
    new_attn_w = attn_w - STEP_SCALE * math.sqrt(D) * attn_orth
    new_mlp_w = mlp_w - STEP_SCALE * math.sqrt(FF) * mlp_orth
    tokens_all = groups * batch_size * full_len
    vec_rate = RATE_VEC / math.sqrt(tokens_all)
    new_in_bias = in_bias - vec_rate * new_mom_bias
    new_vectors = vectors - vec_rate * new_mom_vec
    return (
        stream,
        upstream,
        new_mom_attn,
        new_attn_w,
        new_mom_mlp,
        new_mlp_w,
        new_mom_bias,
        new_in_bias,
        new_mom_vec,
        new_vectors,
    )


def solution(mesh):
    placed = (
        P("dp", "tensor", None),
        P("dp", None),
        P(None, None, "dp", "tensor"),
        P(None, None, "dp", None, "tensor"),
        P(None, None, "tensor"),
        P(),
        P(None, None, "dp", "tensor"),
        P(None, None, "dp", None, "tensor"),
        P(None, None, "tensor"),
        P(),
        P("dp", "tensor", None),
    )
    return jax.shard_map(
        per_device,
        mesh=mesh,
        in_specs=placed,
        out_specs=(
            P("dp", "tensor", None),
            P("dp", "tensor", None),
            P(None, None, "dp", "tensor"),
            P(None, None, "dp", "tensor"),
            P(None, None, "dp", None, "tensor"),
            P(None, None, "dp", None, "tensor"),
            P(None, None, "tensor"),
            P(None, None, "tensor"),
            P(),
            P(),
        ),
        check_vma=False,
    )
```

profile of v0, /device:TPU:1, one launch (start us, length us, event | category | flops | bytes accessed | tf_op | source)
XLA Modules:
  0.0 2720.5 jit_solution(5844644376128212627)
XLA Ops:
  18.2 126.7 %all-gather.30.cloned.1.call-done = bf16[1,4,768,192]{3,1,0,2:T(4,128)(2,1)} async-done(((bf16[1,4,24,192]{3,1,0,2:T(4,128)(2,1)}), bf16[1,4,768,192]{3,1,0,2:T(4,128)(2,1)}) %all-gather.30.cloned.1.call-update) | async-done | bytes 1179664 | tf_op jit(solution)/shard_map/all_gather | solution.py:345
  152.6 39.8 %all-gather.16.cloned.1.call-done = bf16[1,1024,768]{2,1,0:T(8,128)(2,1)} async-done(((bf16[1,256,768]{2,1,0:T(8,128)(2,1)}), bf16[1,1024,768]{2,1,0:T(8,128)(2,1)}) %all-gather.16.cloned.1.call-update) | async-done | bytes 1572880 | tf_op jit(solution)/shard_map/all_gather | solution.py:175
  206.6 122.2 %all-gather.32.cloned.1.call-done = bf16[1,2,768,4,192]{4,3,1,0,2:T(4,128)(2,1)} async-done(((bf16[1,2,24,4,192]{4,3,1,0,2:T(4,128)(2,1)}), bf16[1,2,768,4,192]{4,3,1,0,2:T(4,128)(2,1)}) %all-gather.32.cloned.1.call-update) | async-done | bytes 2359312 | tf_op jit(solution)/shard_map/all_gather | solution.py:346
  339.1 36.6 %all-gather.18.cloned.1.call-done = bf16[1,1024,768]{2,1,0:T(8,128)(2,1)} async-done(((bf16[1,256,768]{2,1,0:T(8,128)(2,1)}), bf16[1,1024,768]{2,1,0:T(8,128)(2,1)}) %all-gather.18.cloned.1.call-update) | async-done | bytes 1572880 | tf_op jit(solution)/shard_map/all_gather | solution.py:176
  378.9 7.4 fusion.11
  391.5 42.6 %reduce-scatter.6.cloned.1.call-done = f32[256,768]{1,0:T(8,128)} async-done(((f32[1024,768]{1,0:T(8,128)}), f32[256,768]{1,0:T(8,128)}) %reduce-scatter.6.cloned.1.call-update) | async-done | bytes 786448 | tf_op jit(solution)/shard_map/reduce_scatter | solution.py:198
  440.1 126.5 %all-gather.34.cloned.1.call-done = bf16[1,4,768,192]{3,1,0,2:T(4,128)(2,1)} async-done(((bf16[1,4,24,192]{3,1,0,2:T(4,128)(2,1)}), bf16[1,4,768,192]{3,1,0,2:T(4,128)(2,1)}) %all-gather.34.cloned.1.call-update) | async-done | bytes 1179664 | tf_op jit(solution)/shard_map/all_gather | solution.py:345
  573.0 152.2 %all-gather.36.cloned.1.call-done = bf16[1,2,768,4,192]{4,3,1,0,2:T(4,128)(2,1)} async-done(((bf16[1,2,24,4,192]{4,3,1,0,2:T(4,128)(2,1)}), bf16[1,2,768,4,192]{4,3,1,0,2:T(4,128)(2,1)}) %all-gather.36.cloned.1.call-update) | async-done | bytes 2359312 | tf_op jit(solution)/shard_map/all_gather | solution.py:346
  737.8 34.5 %all-gather.20.cloned.1.call-done = bf16[1,1024,768]{2,1,0:T(8,128)(2,1)} async-done(((bf16[1,256,768]{2,1,0:T(8,128)(2,1)}), bf16[1,1024,768]{2,1,0:T(8,128)(2,1)}) %all-gather.20.cloned.1.call-update) | async-done | bytes 1572880 | tf_op jit(solution)/shard_map/all_gather | solution.py:175
  785.1 12.8 all-gather.24.cloned.1.call-done
  800.0 5.0 multiply_reduce_fusion.3
  817.0 5.5 multiply_reduce_fusion.2
  826.5 10.2 convert_reduce_fusion.1
  857.7 8.3 copy.89
  866.1 48.8 %reduce-scatter.10.cloned.1.call-done = f32[256,2,768]{2,0,1:T(8,128)} async-done(((f32[1024,2,768]{2,0,1:T(8,128)}), f32[256,2,768]{2,0,1:T(8,128)}) %reduce-scatter.10.cloned.1.call-update) | async-done | bytes 1572880 | tf_op jit(solution)/shard_map/reduce_scatter | solution.py:273
  920.2 5.0 fusion.185
  925.3 5.2 fusion.186
  933.7 4.8 copy.84
  938.5 5.3 all-gather.26.cloned.1.call-done
  973.8 7.3 copy.88
  981.1 5.6 multiply_convert_fusion
  996.7 429.4 %all-reduce.34.cloned.1.call-done = (f32[4,768,192]{2,0,1:T(4,128)}, f32[4,768,192]{2,0,1:T(4,128)}, f32[2,768,4,192]{3,2,0,1:T(4,128)}, f32[2,768,4,192]{3,2,0,1:T(4,128)}) async-done(((f32[4,768,192]{2,0,1:T(4,128)}, f32[4,768,192]{2,0,1:T(4,128)}, f32[2,768,4,192]{3,2,0,1:T(4,128)}, f32[2,768,4,192]{3,2,0,1:T(4,128)}), (f32[4,768,192]{2,0,1:T(4,128)}, f32[4,768,192]{2,0,1:T(4,128)}, ...) | async-done | bytes 14155792
  1433.4 308.0 %all-gather.28.cloned.1.call-done = f32[12,768,768]{2,1,0:T(8,128)} async-done(((f32[12,24,768]{2,1,0:T(8,128)}), f32[12,768,768]{2,1,0:T(8,128)}) %all-gather.28.cloned.1.call-update) | async-done | bytes 28311568 | tf_op jit(solution)/shard_map/all_gather | solution.py:400
  1741.5 9.6 fusion.60
  1751.6 59.6 %all-reduce.22.cloned.1.call-done = f32[768,768]{1,0:T(8,128)} async-done(((f32[768,768]{1,0:T(8,128)}), f32[768,768]{1,0:T(8,128)}) %all-reduce.22.cloned.1.call-update) | async-done | bytes 2359312 | tf_op jit(solution)/shard_map/psum | solution.py:310
  1814.4 8.5 fusion.189
  1822.9 8.7 fusion.59
  1833.0 7.4 fusion.316
  1840.5 62.7 %all-reduce.24.cloned.1.call-done = f32[768,768]{1,0:T(8,128)} async-done(((f32[768,768]{1,0:T(8,128)}), f32[768,768]{1,0:T(8,128)}) %all-reduce.24.cloned.1.call-update) | async-done | bytes 2359312 | tf_op jit(solution)/shard_map/psum | solution.py:310
  1903.2 8.5 fusion.317
  1911.7 8.4 multiply_add_fusion.3
  1920.1 7.7 fusion.318
  1927.9 62.7 %all-reduce.26.cloned.1.call-done = f32[768,768]{1,0:T(8,128)} async-done(((f32[768,768]{1,0:T(8,128)}), f32[768,768]{1,0:T(8,128)}) %all-reduce.26.cloned.1.call-update) | async-done | bytes 2359312 | tf_op jit(solution)/shard_map/psum | solution.py:310
  1990.5 8.5 fusion.319
  1999.1 6.2 multiply_add_fusion.2
  2006.7 7.5 fusion.320
  2021.9 55.1 %all-reduce.28.cloned.1.call-done = f32[768,768]{1,0:T(8,128)} async-done(((f32[768,768]{1,0:T(8,128)}), f32[768,768]{1,0:T(8,128)}) %all-reduce.28.cloned.1.call-update) | async-done | bytes 2359312 | tf_op jit(solution)/shard_map/psum | solution.py:310
  2077.0 8.5 fusion.321
  2085.5 9.2 multiply_add_fusion.1
  2094.7 7.6 fusion.322
  2119.0 25.0 reduce-scatter.12.cloned.1.call-done
  2149.0 60.4 %all-reduce.30.cloned.1.call-done = f32[768,768]{1,0:T(8,128)} async-done(((f32[768,768]{1,0:T(8,128)}), f32[768,768]{1,0:T(8,128)}) %all-reduce.30.cloned.1.call-update) | async-done | bytes 2359312 | tf_op jit(solution)/shard_map/psum | solution.py:310
  2209.5 8.5 fusion.323
  2218.0 6.2 multiply_add_fusion
  2224.2 9.7 broadcast_select_fusion
  2239.2 17.1 reduce-scatter.8.cloned.1.call-done
  2259.2 140.9 %all-reduce.32.cloned.1.call-done = (f32[2,7,768]{2,0,1:T(2,128)}, f32[2,6,768]{2,1,0:T(8,128)}) async-done(((f32[2,7,768]{2,0,1:T(2,128)}, f32[2,6,768]{2,1,0:T(8,128)}), (f32[2,7,768]{2,0,1:T(2,128)}, f32[2,6,768]{2,1,0:T(8,128)})) %all-reduce.32.cloned.1.call-update) | async-done | bytes 79888 | tf_op jit(solution)/shard_map/psum | solution.py:378
  2405.6 304.6 %reduce-scatter.14.cloned.1.call-done = f32[12,24,768]{2,1,0:T(8,128)} async-done(((f32[12,768,768]{2,1,0:T(8,128)}), f32[12,24,768]{2,1,0:T(8,128)}) %reduce-scatter.14.cloned.1.call-update) | async-done | bytes 884752 | tf_op jit(solution)/shard_map/reduce_scatter | solution.py:411
  (533 shorter events, 233.9 us)
Async XLA Ops:
  7.2 137.7 %all-gather.30.cloned.1.call-start = ((), (), s32[]{:S(2)}) async-start(), calls=%async_computation.22 | async-start | bytes 1622016 | tf_op jit(solution)/shard_map/all_gather | solution.py:345
  9.0 183.4 %all-gather.16.cloned.1.call-start = ((), (), s32[]{:S(2)}) async-start(), calls=%async_computation.5 | async-start | bytes 1966080 | tf_op jit(solution)/shard_map/all_gather | solution.py:175
  10.6 427.7 %copy-start.87 = (f32[768]{0:T(1024)}, f32[768]{0:T(1024)S(1)}, u32[]{:S(2)}) copy-start(f32[768]{0:T(1024)S(1)} %get-tuple-element.71) | copy-start | bytes 9220
  10.6 427.7 %copy-start.89 = (f32[768]{0:T(1024)}, f32[768]{0:T(1024)S(1)}, u32[]{:S(2)}) copy-start(f32[768]{0:T(1024)S(1)} %get-tuple-element.72) | copy-start | bytes 9220
  11.8 136.4 %copy-start.105 = (f32[256]{0:T(256)}, f32[256]{0:T(256)S(1)}, u32[]{:S(2)}) copy-start(f32[256]{0:T(256)S(1)} %broadcast_multiply_fusion.9) | copy-start | bytes 3076
  13.0 135.2 %copy-start.106 = (f32[256]{0:T(256)}, f32[256]{0:T(256)S(1)}, u32[]{:S(2)}) copy-start(f32[256]{0:T(256)S(1)} %add_rsqrt_fusion.1) | copy-start | bytes 3076
  15.2 313.6 %all-gather.32.cloned.1.call-start = ((), (), s32[]{:S(2)}) async-start(), calls=%async_computation.23 | async-start | bytes 3244032 | tf_op jit(solution)/shard_map/all_gather | solution.py:346
  16.0 359.7 %all-gather.18.cloned.1.call-start = ((), (), s32[]{:S(2)}) async-start(), calls=%async_computation.6 | async-start | bytes 1966080 | tf_op jit(solution)/shard_map/all_gather | solution.py:176
  16.6 417.5 %reduce-scatter.6.cloned.1.call-start = ((), (), s32[]{:S(2)}) async-start(), calls=%async_computation.7 | async-start | bytes 3932160 | tf_op jit(solution)/shard_map/reduce_scatter | solution.py:198
  150.5 237.2 %copy-start.58 = (bf16[1,1,768,192]{2,3,1,0:T(8,128)(2,1)}, bf16[1,1,768,192]{2,3,1,0:T(8,128)(2,1)S(1)}, u32[]{:S(2)}) copy-start(bf16[1,1,768,192]{2,3,1,0:T(8,128)(2,1)S(1)} %copy.107) | copy-start | bytes 884740
  204.4 183.3 %copy-start.66 = (bf16[3,64,512]{2,1,0:T(8,128)(2,1)}, bf16[3,64,512]{2,1,0:T(8,128)(2,1)S(1)}, u32[]{:S(2)}) copy-start(bf16[3,64,512]{2,1,0:T(8,128)(2,1)S(1)} %fusion.187) | copy-start | bytes 589828
  206.6 181.2 %copy-start.68 = (bf16[3,64,512]{2,1,0:T(8,128)(2,1)}, bf16[3,64,512]{2,1,0:T(8,128)(2,1)S(1)}, u32[]{:S(2)}) copy-start(bf16[3,64,512]{2,1,0:T(8,128)(2,1)S(1)} %fusion.188) | copy-start | bytes 589828
  390.1 44.1 %copy-start.4 = (bf16[1,256,768]{2,1,0:T(8,128)(2,1)S(1)}, bf16[1,256,768]{2,1,0:T(8,128)(2,1)}, u32[]{:S(2)}) copy-start(bf16[1,256,768]{2,1,0:T(8,128)(2,1)} %param.11) | copy-start | bytes 1179652
  390.1 44.1 %copy-start.25 = (f32[1,256,768]{2,1,0:T(8,128)S(1)}, f32[1,256,768]{2,1,0:T(8,128)}, u32[]{:S(2)}) copy-start(f32[1,256,768]{2,1,0:T(8,128)} %param.21) | copy-start | bytes 2359300
  390.1 176.5 %all-gather.34.cloned.1.call-start = ((), (), s32[]{:S(2)}) async-start(), calls=%async_computation.24 | async-start | bytes 1622016 | tf_op jit(solution)/shard_map/all_gather | solution.py:345
  390.7 334.5 %all-gather.36.cloned.1.call-start = ((), (), s32[]{:S(2)}) async-start(), calls=%async_computation.25 | async-start | bytes 3244032 | tf_op jit(solution)/shard_map/all_gather | solution.py:346
  391.4 380.9 %all-gather.20.cloned.1.call-start = ((), (), s32[]{:S(2)}) async-start(), calls=%async_computation.8 | async-start | bytes 1966080 | tf_op jit(solution)/shard_map/all_gather | solution.py:175
  438.3 134.7 %copy-start.108 = (f32[256]{0:T(256)}, f32[256]{0:T(256)S(1)}, u32[]{:S(2)}) copy-start(f32[256]{0:T(256)S(1)} %add_rsqrt_fusion) | copy-start | bytes 3076
  439.3 358.5 %all-gather.24.cloned.1.call-start = ((), (), s32[]{:S(2)}) async-start(), calls=%async_computation.11 | async-start | bytes 1966080 | tf_op jit(solution)/shard_map/all_gather | solution.py:234
  440.1 383.1 %all-gather.22.cloned.1.call-start = ((), (), s32[]{:S(2)}) async-start(), calls=%async_computation.9 | async-start | bytes 1966080 | tf_op jit(solution)/shard_map/all_gather | solution.py:176
  569.4 228.4 %copy-start.56 = (bf16[1,1,768,192]{2,3,1,0:T(8,128)(2,1)}, bf16[1,1,768,192]{2,3,1,0:T(8,128)(2,1)S(1)}, u32[]{:S(2)}) copy-start(bf16[1,1,768,192]{2,3,1,0:T(8,128)(2,1)S(1)} %copy.111) | copy-start | bytes 884740
  737.8 177.0 %reduce-scatter.10.cloned.1.call-start = ((), (), s32[]{:S(2)}) async-start(), calls=%async_computation.12 | async-start | bytes 7864320 | tf_op jit(solution)/shard_map/reduce_scatter | solution.py:273
  781.0 28.6 %copy-start.101 = (f32[3,512]{1,0:T(4,128)}, f32[3,512]{1,0:T(4,128)S(1)}, u32[]{:S(2)}) copy-start(f32[3,512]{1,0:T(4,128)S(1)} %get-tuple-element.175) | copy-start | bytes 18436
  844.7 86.3 %copy-start.40 = (bf16[1,1024,3,64]{1,3,2,0:T(8,128)(2,1)}, bf16[1,1024,3,64]{1,3,2,0:T(8,128)(2,1)S(1)}, u32[]{:S(2)}) copy-start(bf16[1,1024,3,64]{1,3,2,0:T(8,128)(2,1)S(1)} %maximum_convert_fusion) | copy-start | bytes 1179652
  850.3 93.5 %all-gather.26.cloned.1.call-start = ((), (), s32[]{:S(2)}) async-start(), calls=%async_computation.13 | async-start | bytes 1966080 | tf_op jit(solution)/shard_map/all_gather | solution.py:234
  857.7 59.7 %copy-start.26 = (f32[1,256,768]{2,1,0:T(8,128)S(1)}, f32[1,256,768]{2,1,0:T(8,128)}, u32[]{:S(2)}) copy-start(f32[1,256,768]{2,1,0:T(8,128)} %param.21) | copy-start | bytes 2359300
  857.7 59.7 %copy-start.109 = (f32[256]{0:T(256)S(1)}, f32[256]{0:T(256)}, u32[]{:S(2)}) copy-start(f32[256]{0:T(256)} %copy-done.108) | copy-start | bytes 3076
  920.1 505.9 %all-reduce.34.cloned.1.call-start = ((), (), s32[]{:S(2)}) async-start(), calls=%async_computation.27 | async-start | bytes 37748736
  988.7 1025.6 %copy-start.48 = (bf16[1,1024,3,64]{1,3,2,0:T(8,128)(2,1)}, bf16[1,1024,3,64]{1,3,2,0:T(8,128)(2,1)S(1)}, u32[]{:S(2)}) copy-start(bf16[1,1024,3,64]{1,3,2,0:T(8,128)(2,1)S(1)} %fusion.220) | copy-start | bytes 1179652
  994.8 435.2 %copy-start.85 = (f32[2,4,24,192]{3,2,1,0:T(8,128)S(1)}, f32[2,4,24,192]{3,2,1,0:T(8,128)}, u32[]{:S(2)}) copy-start(f32[2,4,24,192]{3,2,1,0:T(8,128)} %param.17) | copy-start | bytes 442372
  994.8 435.9 %copy-start.78 = (f32[2,2,24,4,192]{4,3,2,1,0:T(4,128)S(1)}, f32[2,2,24,4,192]{4,3,2,1,0:T(4,128)}, u32[]{:S(2)}) copy-start(f32[2,2,24,4,192]{4,3,2,1,0:T(4,128)} %param.18) | copy-start | bytes 884740
  994.8 746.6 %all-gather.28.cloned.1.call-start = ((), (), s32[]{:S(2)}) async-start(), calls=%async_computation.15 | async-start | bytes 29196288 | tf_op jit(solution)/shard_map/all_gather | solution.py:400
  1433.4 377.9 %all-reduce.22.cloned.1.call-start = ((), (), s32[]{:S(2)}) async-start(), calls=%async_computation.16 | async-start | bytes 4718592 | tf_op jit(solution)/shard_map/psum | solution.py:310
  1751.1 152.0 %all-reduce.24.cloned.1.call-start = ((), (), s32[]{:S(2)}) async-start(), calls=%async_computation.17 | async-start | bytes 4718592 | tf_op jit(solution)/shard_map/psum | solution.py:310
  1840.4 150.1 %all-reduce.26.cloned.1.call-start = ((), (), s32[]{:S(2)}) async-start(), calls=%async_computation.18 | async-start | bytes 4718592 | tf_op jit(solution)/shard_map/psum | solution.py:310
  1927.8 149.2 %all-reduce.28.cloned.1.call-start = ((), (), s32[]{:S(2)}) async-start(), calls=%async_computation.19 | async-start | bytes 4718592 | tf_op jit(solution)/shard_map/psum | solution.py:310
  2014.3 129.7 %reduce-scatter.12.cloned.1.call-start = ((), (), s32[]{:S(2)}) async-start(), calls=%async_computation.14 | async-start | bytes 7864320 | tf_op jit(solution)/shard_map/reduce_scatter | solution.py:273
  2021.6 187.8 %all-reduce.30.cloned.1.call-start = ((), (), s32[]{:S(2)}) async-start(), calls=%async_computation.20 | async-start | bytes 4718592 | tf_op jit(solution)/shard_map/psum | solution.py:310
  2102.4 153.9 %reduce-scatter.8.cloned.1.call-start = ((), (), s32[]{:S(2)}) async-start(), calls=%async_computation.10 | async-start | bytes 3932160 | tf_op jit(solution)/shard_map/reduce_scatter | solution.py:198
  2108.1 37.4 %copy-start.5 = (bf16[1,256,768]{2,1,0:T(8,128)(2,1)S(1)}, bf16[1,256,768]{2,1,0:T(8,128)(2,1)}, u32[]{:S(2)}) copy-start(bf16[1,256,768]{2,1,0:T(8,128)(2,1)} %param.11) | copy-start | bytes 1179652
  2108.1 37.4 %copy-start.92 = (f32[768]{0:T(1024)S(1)}, f32[768]{0:T(1024)}, u32[]{:S(2)}) copy-start(f32[768]{0:T(1024)} %copy-done.91) | copy-start | bytes 9220
  2108.1 37.4 %copy-start.94 = (f32[768]{0:T(1024)S(1)}, f32[768]{0:T(1024)}, u32[]{:S(2)}) copy-start(f32[768]{0:T(1024)} %copy-done.93) | copy-start | bytes 9220
  2108.1 292.1 %all-reduce.32.cloned.1.call-start = ((), (), s32[]{:S(2)}) async-start(), calls=%async_computation.26 | async-start | bytes 184320 | tf_op jit(solution)/shard_map/psum | solution.py:378
  2119.0 29.8 %copy-start.86 = (f32[2,7,768]{2,0,1:T(2,128)}, f32[2,7,768]{2,0,1:T(2,128)S(1)}, u32[]{:S(2)}) copy-start(f32[2,7,768]{2,0,1:T(2,128)S(1)} %dynamic_update_slice.3) | copy-start | bytes 129028
  2148.8 561.3 %reduce-scatter.14.cloned.1.call-start = ((), (), s32[]{:S(2)}) async-start(), calls=%async_computation.21 | async-start | bytes 29196288 | tf_op jit(solution)/shard_map/reduce_scatter | solution.py:411
  2234.0 22.3 copy-start.88
  2259.2 452.9 %copy-start.64 = (f32[2,4,24,192]{3,2,1,0:T(8,128)S(1)}, f32[2,4,24,192]{3,2,1,0:T(8,128)}, u32[]{:S(2)}) copy-start(f32[2,4,24,192]{3,2,1,0:T(8,128)} %param.13) | copy-start | bytes 442372
  2259.2 453.7 %copy-start.63 = (f32[2,2,24,4,192]{4,3,2,1,0:T(4,128)S(1)}, f32[2,2,24,4,192]{4,3,2,1,0:T(4,128)}, u32[]{:S(2)}) copy-start(f32[2,2,24,4,192]{4,3,2,1,0:T(4,128)} %param.14) | copy-start | bytes 884740
  (105 other events, 541.7 us)
Sparse Core Ops, SparseCore 0:
  10.3 134.6 all-gather.29
  147.2 45.1 all-gather.15
  194.6 134.0 all-gather.31
  330.9 44.7 all-gather.17
  390.2 43.8 reduce-scatter.5
  435.7 130.8 all-gather.33
  569.0 156.1 all-gather.35
  727.5 44.7 all-gather.19
  774.7 23.1 all-gather.23
  800.0 23.1 all-gather.21
  850.5 64.2 reduce-scatter.9
  920.2 23.5 all-gather.25
  995.0 431.0 all-reduce.33
  1433.5 307.9 all-gather.27
  1751.2 59.9 all-reduce.21
  1840.6 62.5 all-reduce.23
  1927.9 62.5 all-reduce.25
  2014.4 62.5 all-reduce.27
  2079.6 64.3 reduce-scatter.11
  2146.5 62.9 all-reduce.29
  2212.3 43.9 reduce-scatter.7
  2261.9 138.2 all-reduce.31
  2402.7 307.3 reduce-scatter.13
where the time goes:
time: 2730 us; the launch traced here: 2720 us
  waiting for transfers between devices  2280 us (84%)
  matrix products  227 us (8%)
  other arithmetic  104 us (4%)
  local copies, waits for them, and re-layouts  93.3 us (3%)
    unnamed x24, waiting for transfers between devices  432 us
    all_gather x1, waiting for transfers between devices, per_device(): whole = lax.all_gather(stacked, 'dp', axis=1, tiled=True)  308 us
    reduce_scatter x1, waiting for transfers between devices, per_device(): returned = lax.psum_scatter(result, 'dp', scatter_dimension=1, tiled=True)  305 us
    psum x5, waiting for transfers between devices, gram_of(): return lax.psum(jnp.dot(current, current.T, precision=PRECISE), 'tensor')  300 us
    all_gather x2, waiting for transfers between devices, per_device(): lax.all_gather(mlp_w[layer_index].astype(jnp.bfloat16), 'dp', axis=1, til...  274 us
    all_gather x2, waiting for transfers between devices, per_device(): lax.all_gather(attn_w[layer_index].astype(jnp.bfloat16), 'dp', axis=1, ti...  253 us
    psum x1, waiting for transfers between devices, per_device(): lax.psum((jnp.stack(vector_grads), spread_bias), ('dp', 'tensor'))  141 us
    all_gather x2, waiting for transfers between devices, forward_layer(): lax.all_gather(normed_one, 'tensor', axis=1, tiled=True)  74.3 us
  transfers between devices with their start and end apart: 23, of which 23 were waited for; matrix products, arithmetic and copies ran while one was open for 8% of the time, Pallas kernels for 0%

commit v1 on v0

v1 whole, which is shorter than its diff:
```python
import math

import jax
import jax.numpy as jnp
from jax import lax
from jax.sharding import PartitionSpec as P

D = 768
FF = 3072
HD = 64
ROT = 16
NS_STEPS = 5
HEADS_HERE = 3
COLS = 192
CHUNK = 24
WIDE = 2304

EPS_NORM = 1e-05
EPS_ORTH = 1e-07
COEF_A = 3.4445
COEF_B = -4.775
COEF_C = 2.0315
MOMENTUM = 0.95
STEP_SCALE = 0.4
RATE_VEC = 0.5
NEG_FILL = -1e30

BF = jnp.bfloat16
F32 = jnp.float32


def dp_swap(value, mask):
    return lax.ppermute(value, "dp", [(i, i ^ mask) for i in range(32)])


def tensor_swap(value, mask):
    return lax.ppermute(value, "tensor", [(i, i ^ mask) for i in range(4)])


def dp_place():
    me = lax.axis_index("dp")
    return me // 16, (me // 4) % 4, me % 4


def swap_four(pieces, unit):
    return [pieces[0]] + [dp_swap(pieces[s], s * unit) for s in (1, 2, 3)]


def gather_rows(shard):
    spread = jnp.broadcast_to(shard[None], (32,) + shard.shape)
    return lax.all_to_all(spread, "dp", 0, 0, tiled=True).reshape(D, shard.shape[1])


def scatter_rows(full):
    arrived = lax.all_to_all(full.reshape(32, CHUNK, full.shape[1]), "dp", 0, 0, tiled=True)
    return jnp.sum(arrived.astype(F32), 0)


def gather_tokens(mine):
    far = tensor_swap(mine, 2)
    near = tensor_swap(mine, 1)
    diagonal = tensor_swap(far, 1)
    return jnp.stack([mine, near, far, diagonal])


def scatter_tokens(partial):
    arrived = tensor_swap(partial[1::2].astype(BF), 1)
    pair = partial[0::2] + arrived.astype(F32)
    return pair[0] + tensor_swap(pair[1].astype(BF), 2).astype(F32)


def standardize(stream):
    center = stream - jnp.mean(stream, -1, keepdims=True)
    inverse = lax.rsqrt(jnp.mean(center * center, -1, keepdims=True) + EPS_NORM)
    return center * inverse, inverse


def rope_tables(labels, places):
    kinds = jnp.arange(8, dtype=jnp.int32)
    below = jnp.sum((labels[None, :] < kinds[:, None]).astype(jnp.int32), 1)
    earlier = jnp.sum(jnp.where(labels[None, :] == kinds[:, None], below[:, None], 0), 0)
    frequency = 10000.0 ** (jnp.arange(ROT // 2, dtype=F32) * (-2.0 / ROT))
    angles = (places - earlier).astype(F32)[None, :] * frequency[:, None]
    return jnp.cos(angles).T[:, None, :], jnp.sin(angles).T[:, None, :]


def rotate(heads_in, cosine, sine):
    half = ROT // 2
    leading, trailing = heads_in[..., :half], heads_in[..., half:ROT]
    return jnp.concatenate(
        [leading * cosine - trailing * sine, trailing * cosine + leading * sine, heads_in[..., ROT:]],
        -1,
    )


def gelu_and_slope(pre_act):
    below = 0.5 * (1.0 + jax.scipy.special.erf(pre_act * 0.7071067811865476))
    return (
        (pre_act * below).astype(BF),
        below + pre_act * jnp.exp(-0.5 * pre_act * pre_act) * 0.3989422804014327,
    )


def mm(spec, left, right):
    return jnp.einsum(spec, left, right, preferred_element_type=F32)


def attend_forward(queries, keys, values, allowed):
    factor = HD ** (-0.5)
    outs, totals = [], []
    for start in range(0, 1024, 512):
        rows = slice(start, start + 512)
        scores = mm("qhd,khd->hqk", queries[rows], keys) * factor
        scores = jnp.where(allowed[None, rows], scores, NEG_FILL)
        row_max = jnp.max(scores, -1, keepdims=True)
        shifted = jnp.exp(scores - row_max)
        row_total = jnp.sum(shifted, -1, keepdims=True)
        probability = (shifted / row_total).astype(BF)
        outs.append(mm("hqk,khd->qhd", probability, values))
        totals.append(row_max + jnp.log(row_total))
    return jnp.concatenate(outs, 0), jnp.concatenate(totals, 1)


def attend_backward(queries, keys, values, allowed, log_total, d_mixed):
    factor = HD ** (-0.5)
    query_grads = []
    key_grad = value_grad = 0.0
    for start in range(0, 1024, 512):
        rows = slice(start, start + 512)
        scores = mm("qhd,khd->hqk", queries[rows], keys) * factor
        probability = jnp.where(allowed[None, rows], jnp.exp(scores - log_total[:, rows]), 0.0)
        prob_grad = mm("qhd,khd->hqk", d_mixed[rows], values)
        score_grad = (
            probability * (prob_grad - jnp.sum(probability * prob_grad, -1, keepdims=True))
        ).astype(BF)
        query_grads.append(mm("hqk,khd->qhd", score_grad, keys) * factor)
        key_grad = key_grad + mm("hqk,qhd->khd", score_grad, queries[rows]) * factor
        value_grad = value_grad + mm("hqk,qhd->khd", probability.astype(BF), d_mixed[rows])
    return jnp.concatenate(query_grads, 0), key_grad, value_grad


def forward_layer(stream, weights, bias_rows, vector_rows, cosine, sine, allowed):
    scaled, inverse = standardize(stream)
    scaled_all = gather_tokens(scaled.astype(jnp.float16)).reshape(1024, D).astype(F32)
    first = (scaled_all * vector_rows[0] + vector_rows[1]).astype(BF)
    second = (scaled_all * vector_rows[2] + vector_rows[3]).astype(BF)
    projected = mm("sd,dh->sh", first, weights[0]) + bias_rows[:3].reshape(-1)
    view = projected.reshape(1024, 3, HEADS_HERE, HD)
    queries = rotate(view[:, 0], cosine, sine).astype(BF)
    keys = rotate(view[:, 1], cosine, sine).astype(BF)
    values = view[:, 2].astype(BF)
    mixed, log_total = attend_forward(queries, keys, values, allowed)
    mixed = mixed.reshape(1024, COLS).astype(BF)
    pre_act = mm("sd,dh->sh", second, weights[1]) + bias_rows[3:].reshape(-1)
    hidden, slope = gelu_and_slope(pre_act)
    inner = jnp.concatenate([hidden, mixed], 1)
    branch = scatter_tokens(mm("sh,dh->sd", inner, weights[2]).reshape(4, 256, D))
    record = (scaled, inverse, scaled_all, first, second, queries, keys, values, log_total, slope, inner)
    return record, stream + branch + vector_rows[4] + vector_rows[5]


def backward_layer(upstream, outer, record, weights, vector_rows, cosine, sine, allowed):
    scaled, inverse, scaled_all, first, second, queries, keys, values, log_total, slope, inner = record
    d_inner = mm("sd,dh->sh", outer, weights[2])
    d_mixed = d_inner[:, 768:].astype(BF)
    d_pre = (d_inner[:, :768] * slope).astype(BF)
    grad_rest = jnp.concatenate(
        [mm("sd,sh->dh", outer, inner).astype(BF), mm("sd,sh->dh", second, d_pre).astype(BF)], 1
    )
    rest = scatter_rows(grad_rest)
    query_grad, key_grad, value_grad = attend_backward(
        queries, keys, values, allowed, log_total, d_mixed.reshape(1024, HEADS_HERE, HD)
    )
    d_proj = jnp.stack(
        [rotate(query_grad, cosine, -sine), rotate(key_grad, cosine, -sine), value_grad], 1
    ).astype(BF).reshape(1024, 576)
    grad_proj = mm("sd,sh->dh", first, d_proj).astype(BF)
    d_first = mm("sh,dh->sd", d_proj, weights[0])
    d_second = mm("sh,dh->sd", d_pre, weights[1])
    weighted = scatter_tokens(
        (d_first * vector_rows[0] + d_second * vector_rows[2]).reshape(4, 256, D)
    )
    new_upstream = upstream + inverse * (
        weighted
        - jnp.mean(weighted, -1, keepdims=True)
        - scaled * jnp.mean(weighted * scaled, -1, keepdims=True)
    )
    wide = scaled_all
    small = jnp.concatenate(
        [
            jnp.sum(d_first * wide, 0),
            jnp.sum(d_first, 0),
            jnp.sum(d_second * wide, 0),
            jnp.sum(d_second, 0),
            jnp.sum(upstream, 0),
            jnp.sum(d_proj.astype(F32), 0),
            jnp.sum(d_pre.astype(F32), 0),
            jnp.zeros((192,), F32),
        ]
    ).reshape(7, D)
    near, rest = lax.optimization_barrier(
        (jnp.concatenate([grad_proj, two_terms(small.T)], 1), rest)
    )
    near = scatter_rows(near)
    grads = jnp.concatenate([rest[:, :960], near[:, :576], rest[:, 960:]], 1)
    return new_upstream, grads, near[:, 576:583] + near[:, 583:]


def two_terms(value):
    upper = value.astype(BF)
    return jnp.concatenate([upper, (value - upper.astype(F32)).astype(BF)], 1)


def pack_shard(attn, mlp):
    up = mlp[0].reshape(CHUNK, 768)
    down = mlp[1].reshape(CHUNK, 768)
    return jnp.concatenate([down, attn[3], attn[0], attn[1], attn[2], up], 1)


def unpack_shard(wide):
    attn = jnp.stack([wide[:, 960:1152], wide[:, 1152:1344], wide[:, 1344:1536], wide[:, 768:960]])
    mlp = jnp.stack([wide[:, 1536:], wide[:, :768]]).reshape(2, CHUNK, 4, COLS)
    return attn, mlp


def high(left, right):
    return jnp.dot(left, right, precision=lax.Precision.HIGH)


def orthogonal_blocks(moms, small):
    x, z, y = dp_place()
    sends = []
    for to_x in range(2):
        for to_z in range(4):
            wide = moms[to_z // 2]
            if to_x == 0:
                sends.append(wide[:, 1536:] if to_z % 2 == 0 else wide[:, :768])
            else:
                pair = wide[:, 960:1344] if to_z % 2 == 0 else jnp.concatenate([wide[:, 1344:1536], wide[:, 768:960]], 1)
                sends.append(jnp.pad(pair, ((0, 0), (0, 384))))
    sends = jnp.stack(sends).astype(BF)
    groups = [[i + y_place for i in range(0, 32, 4)] for y_place in range(4)]
    rows = lax.all_to_all(sends, "dp", 0, 0, tiled=True, axis_index_groups=groups)
    rows = rows.reshape(192, 768)
    far = tensor_swap(rows, 2)
    whole = jnp.stack(swap_four([jnp.stack([rows, far])] * 4, 1))
    half = y // 2
    column = jnp.arange(768) // COLS
    whole = jnp.where((x == 0) | (column == half), whole, jnp.zeros((), BF))
    mine = whole[:, 0].reshape(768, 768)
    other = whole[:, 1].reshape(768, 768)
    gram = mm("ac,bc->ab", mine, mine) + mm("ac,bc->ab", other, other)
    gram = gram + tensor_swap(gram, 1)
    scale = 1.0 / (jnp.sqrt(jnp.trace(gram)) + EPS_ORTH)
    which = jnp.where(x == 0, y, half)
    block = jnp.zeros((768, COLS), BF)
    for i in range(4):
        block = jnp.where(which == i, mine[:, i * COLS : (i + 1) * COLS], block)
    current = block.astype(F32) * scale
    gram = gram * (scale * scale)
    for ns_step in range(NS_STEPS):
        mixer = COEF_B * gram + COEF_C * high(gram, gram)
        current = COEF_A * current + high(mixer, current)
        if ns_step < NS_STEPS - 1:
            gram = COEF_A * gram + high(mixer, gram)
            gram = COEF_A * gram + high(gram, mixer)
    result = current.astype(BF).reshape(4, 8, CHUNK, COLS)
    result = jnp.stack([lax.dynamic_index_in_dim(result, y ^ s, 0, keepdims=False) for s in range(4)], 1)
    spread = jnp.broadcast_to(two_terms(small)[None], (32, CHUNK, 28))
    result = jnp.concatenate([result.reshape(32, CHUNK, COLS), spread], 2)
    back = lax.all_to_all(result, "dp", 0, 0, tiled=True).astype(F32)
    small = (back[:, :, 192:206] + back[:, :, 206:]).reshape(D, 14)
    back = back[:, :, :192].reshape(2, 4, 4, CHUNK, COLS)
    wides = []
    for layer in range(2):
        up = [back[0, 2 * layer, i] for i in range(4)]
        down = [back[0, 2 * layer + 1, i] for i in range(4)]
        query, key = back[1, 2 * layer, 0], back[1, 2 * layer, 2]
        value, output = back[1, 2 * layer + 1, 0], back[1, 2 * layer + 1, 2]
        wides.append(jnp.concatenate(down + [output, query, key, value] + up, 1))
    return wides, small


def per_device(
    x_in, segments, attn_w, mlp_w, in_bias, vectors, mom_attn, mom_mlp, mom_bias, mom_vec, cotangent
):
    me = lax.axis_index("tensor")
    order = [me ^ s for s in range(4)]
    places = jnp.concatenate([i * 256 + jnp.arange(256, dtype=jnp.int32) for i in order])
    labels = jnp.concatenate([lax.dynamic_slice(segments[0], (i * 256,), (256,)) for i in order])
    cosine, sine = rope_tables(labels, places)
    allowed = (labels[:, None] == labels[None, :]) & (places[:, None] >= places[None, :])
    shards = [pack_shard(attn_w[layer], mlp_w[layer]).astype(BF) for layer in range(2)]
    near = gather_rows(shards[0][:, 960:1536])
    rest, near = lax.optimization_barrier((jnp.concatenate([shards[0][:, 1536:], shards[0][:, :960]], 1), near))
    rest = gather_rows(rest)
    later, rest = lax.optimization_barrier((shards[1], rest))
    later = gather_rows(later)
    weights = [
        (near, rest[:, :768], rest[:, 768:]),
        (later[:, 960:1536], later[:, 1536:], later[:, :960]),
    ]
    stream = x_in[0].astype(F32)
    upstream = cotangent[0]
    saved = []
    for layer in range(2):
        if layer == 1:
            stream, weights[1] = lax.optimization_barrier((stream, weights[1]))
        record, stream = forward_layer(
            stream, weights[layer], in_bias[layer], vectors[layer], cosine, sine, allowed
        )
        saved.append(record)
    grads, smalls = [None, None], [None, None]
    for layer in (1, 0):
        outer = gather_tokens(upstream.astype(BF)).reshape(1024, D)
        upstream, grads[layer], smalls[layer] = backward_layer(
            upstream, outer, saved[layer], weights[layer], vectors[layer], cosine, sine, allowed
        )
    shared = jnp.concatenate([s[:, :5] for s in smalls], 1)
    for mask in (1, 2):
        shared = shared + tensor_swap(shared, mask)
    small = jnp.concatenate([shared] + [s[:, 5:] for s in smalls], 1)
    moms = [
        MOMENTUM * pack_shard(mom_attn[layer], mom_mlp[layer]) + grads[layer] for layer in range(2)
    ]
    orth, small = orthogonal_blocks(moms, small)
    vec_total = small[:, :10].T.reshape(2, 5, D)
    vec_total = jnp.concatenate([vec_total, vec_total[:, 4:]], 1)
    bias_total = small[:, 10:].T.reshape(2, 2 * D)[:, :1344].reshape(2, 7, COLS)
    new_mom_attn, new_mom_mlp, new_attn_w, new_mlp_w = [], [], [], []
    for layer in range(2):
        a, m = unpack_shard(moms[layer])
        new_mom_attn.append(a)
        new_mom_mlp.append(m)
        a, m = unpack_shard(orth[layer])
        new_attn_w.append(attn_w[layer] - STEP_SCALE * math.sqrt(D) * a)
        new_mlp_w.append(mlp_w[layer] - STEP_SCALE * math.sqrt(FF) * m)
    new_mom_bias = MOMENTUM * mom_bias + bias_total
    new_mom_vec = MOMENTUM * mom_vec + vec_total
    vec_rate = RATE_VEC / math.sqrt(32768)
    return (
        stream[None],
        upstream[None],
        jnp.stack(new_mom_attn),
        jnp.stack(new_attn_w),
        jnp.stack(new_mom_mlp),
        jnp.stack(new_mlp_w),
        new_mom_bias,
        in_bias - vec_rate * new_mom_bias,
        new_mom_vec,
        vectors - vec_rate * new_mom_vec,
    )


def solution(mesh):
    placed = (
        P("dp", "tensor", None),
        P("dp", None),
        P(None, None, "dp", "tensor"),
        P(None, None, "dp", None, "tensor"),
        P(None, None, "tensor"),
        P(),
        P(None, None, "dp", "tensor"),
        P(None, None, "dp", None, "tensor"),
        P(None, None, "tensor"),
        P(),
        P("dp", "tensor", None),
    )
    return jax.shard_map(
        per_device,
        mesh=mesh,
        in_specs=placed,
        out_specs=(
            P("dp", "tensor", None),
            P("dp", "tensor", None),
            P(None, None, "dp", "tensor"),
            P(None, None, "dp", "tensor"),
            P(None, None, "dp", None, "tensor"),
            P(None, None, "dp", None, "tensor"),
            P(None, None, "tensor"),
            P(None, None, "tensor"),
            P(),
            P(),
        ),
        check_vma=False,
    )
```

time: 2730 us -> 580 us (0.21)
  waiting for transfers between devices: 2280 us -> 136 us
  starting transfers between devices: 1.79 us -> 97.1 us
  matrix products: 227 us -> 160 us
    all_gather x11 -> x0, waiting for transfers between devices: 965 us -> none  [the longest x1 308 us: per_device(): whole = lax.all_gather(stacked, 'dp', axis=1, tiled=True)]
    psum x6 -> x0, waiting for transfers between devices: 441 us -> none  [the longest x5 300 us: gram_of(): return lax.psum(jnp.dot(current, current.T, precision=PRECISE), 'tensor')]
    reduce_scatter x5 -> x0, waiting for transfers between devices: 438 us -> none  [the longest x1 305 us: per_device(): returned = lax.psum_scatter(result, 'dp', scatter_dimension=1, tiled=True)]
    unnamed x24 -> x0, waiting for transfers between devices: 432 us -> none
    ppermute x0 -> x27, waiting for transfers between devices: none -> 76.4 us  [the longest x24 51.8 us: tensor_swap(): return lax.ppermute(value, 'tensor', [(i, i ^ mask) for i in range(4)])]
    all_to_all x0 -> x9, starting transfers between devices: none -> 64.6 us  [the longest x4 29.8 us: scatter_rows(): lax.all_to_all(full.reshape(32, CHUNK, full.shape[1]), 'dp', 0, 0, tiled=...]
    all_to_all x0 -> x9, waiting for transfers between devices: none -> 59.8 us  [the longest x3 25 us: gather_rows(): lax.all_to_all(spread, 'dp', 0, 0, tiled=True).reshape(D, shard.shape[1])]
    dot_general x54 -> x62, matrix products: 204 us -> 160 us  [the longest x44 108 us: mm(): return jnp.einsum(spec, left, right, preferred_element_type=F32)]
  transfers between devices with their start and end apart: 23 -> 36, of which waited for: 23 -> 20; matrix products, arithmetic and copies ran while one was open for 8% -> 34% of each run, Pallas kernels for 0% -> 0%
where the time goes in v1:
time: 580 us; the launch traced here: 571 us
  matrix products  160 us (28%)
  waiting for transfers between devices  136 us (23%)
  starting transfers between devices  97.1 us (17%)
  local copies, waits for them, and re-layouts  88.3 us (15%)
  other arithmetic  85.2 us (15%)
    dot_general x44, matrix products, mm(): return jnp.einsum(spec, left, right, preferred_element_type=F32)  108 us
    dot_general x18, matrix products, high(): return jnp.dot(left, right, precision=lax.Precision.HIGH)  52.1 us
    ppermute x24, waiting for transfers between devices, tensor_swap(): return lax.ppermute(value, 'tensor', [(i, i ^ mask) for i in range(4)])  51.8 us
    all_to_all x4, starting transfers between devices, scatter_rows(): lax.all_to_all(full.reshape(32, CHUNK, full.shape[1]), 'dp', 0, 0, tiled=...  29.8 us
    ppermute x24, starting transfers between devices, tensor_swap(): return lax.ppermute(value, 'tensor', [(i, i ^ mask) for i in range(4)])  28.8 us
    all_to_all x3, starting transfers between devices, gather_rows(): lax.all_to_all(spread, 'dp', 0, 0, tiled=True).reshape(D, shard.shape[1])  25.6 us
    unnamed x284, local copies, waits for them, and re-layouts  25.4 us
    all_to_all x3, waiting for transfers between devices, gather_rows(): lax.all_to_all(spread, 'dp', 0, 0, tiled=True).reshape(D, shard.shape[1])  25 us
  transfers between devices with their start and end apart: 36, of which 20 were waited for; matrix products, arithmetic and copies ran while one was open for 34% of the time, Pallas kernels for 0%

profile of v1, /device:TPU:1, one launch (start us, length us, event | category | flops | bytes accessed | tf_op | source)
XLA Modules:
  0.0 571.1 jit_solution(3816250112077511958)
XLA Ops:
  5.1 3.6 collective-permute-start.1
  13.8 9.3 %all-to-all-start = ((bf16[32,24,576]{2,1,0:T(8,128)(2,1)}), bf16[32,24,576]{2,1,0:T(8,128)(2,1)}, u32[]{:S(2)}, u32[]{:S(2)}) async-start(bf16[32,24,576]{2,1,0:T(8,128)(2,1)} %broadcast_in_dim.142), calls=%async_computation | async-start | bytes 1966080 | tf_op jit(solution)/shard_map/all_to_all | solution.py:51
  29.5 3.6 fusion.31
  33.1 7.5 %all-to-all-done = bf16[32,24,576]{2,1,0:T(8,128)(2,1)} async-done(((bf16[32,24,576]{2,1,0:T(8,128)(2,1)}), bf16[32,24,576]{2,1,0:T(8,128)(2,1)}, u32[]{:S(2)}, u32[]{:S(2)}) %all-to-all-start) | async-done | bytes 884768 | tf_op jit(solution)/shard_map/all_to_all | solution.py:51
  42.3 5.5 all-to-all-start.1
  61.4 17.5 %all-to-all-done.1 = bf16[32,24,1728]{2,1,0:T(8,128)(2,1)} async-done(((bf16[32,24,1728]{2,1,0:T(8,128)(2,1)}), bf16[32,24,1728]{2,1,0:T(8,128)(2,1)}, u32[]{:S(2)}, u32[]{:S(2)}) %all-to-all-start.1) | async-done | bytes 2654240 | tf_op jit(solution)/shard_map/all_to_all | solution.py:51
  80.9 10.7 %all-to-all-start.2 = ((bf16[32,24,2304]{2,1,0:T(8,128)(2,1)}), bf16[32,24,2304]{2,1,0:T(8,128)(2,1)}, u32[]{:S(2)}, u32[]{:S(2)}) async-start(bf16[32,24,2304]{2,1,0:T(8,128)(2,1)} %broadcast_in_dim.149), calls=%async_computation.2 | async-start | bytes 7077888 | tf_op jit(solution)/shard_map/all_to_all | solution.py:51
  91.7 5.1 fusion.142
  96.9 4.9 multiply_convert_fusion.5
  101.8 3.9 fusion.84
  117.2 23.6 %collective-permute-done.4 = bf16[256,768]{1,0:T(8,128)(2,1)S(1)} collective-permute-done((bf16[256,768]{1,0:T(8,128)(2,1)S(1)}, bf16[256,768]{1,0:T(8,128)(2,1)S(1)}, u32[]{:S(2)}, u32[]{:S(2)}) %collective-permute-start.4) | collective-permute-done | bytes 393248 | tf_op jit(solution)/shard_map/ppermute | solution.py:37
  152.8 5.6 fusion.300
  158.3 4.8 collective-permute-done.6
  165.4 3.6 fusion.21
  201.2 3.6 convert_reduce_fusion.2
  211.0 4.5 fusion.282
  223.6 8.8 %collective-permute-done.14 = bf16[256,768]{1,0:T(8,128)(2,1)S(1)} collective-permute-done((bf16[256,768]{1,0:T(8,128)(2,1)S(1)}, bf16[256,768]{1,0:T(8,128)(2,1)S(1)}, u32[]{:S(2)}, u32[]{:S(2)}) %collective-permute-start.14) | collective-permute-done | bytes 393248 | tf_op jit(solution)/shard_map/ppermute | solution.py:37
  232.7 8.1 %collective-permute-done.9 = bf16[256,768]{1,0:T(8,128)(2,1)S(1)} collective-permute-done((bf16[256,768]{1,0:T(8,128)(2,1)S(1)}, bf16[256,768]{1,0:T(8,128)(2,1)S(1)}, u32[]{:S(2)}, u32[]{:S(2)}) %collective-permute-start.9) | collective-permute-done | bytes 393248 | tf_op jit(solution)/shard_map/ppermute | solution.py:37
  246.3 4.5 copy.65
  250.9 7.7 %all-to-all-start.5 = ((bf16[32,24,1728]{2,1,0:T(8,128)(2,1)}), bf16[32,24,1728]{2,1,0:T(8,128)(2,1)}, u32[]{:S(2)}, u32[]{:S(2)}) async-start(bf16[32,24,1728]{2,1,0:T(8,128)(2,1)} %bitcast.461), calls=%async_computation.5 | async-start | bytes 5505024 | tf_op jit(solution)/shard_map/all_to_all | solution.py:55
  269.3 3.3 fusion.301
  279.1 4.4 multiply_reduce_fusion.1
  283.6 4.4 multiply_reduce_fusion
  287.9 7.8 %multiply_convert_fusion = (bf16[3,512,1024]{2,1,0:T(8,128)(2,1)S(1)}, bf16[3,512,1024]{2,1,0:T(8,128)(2,1)}) fusion(f32[3,512,1024]{2,1,0:T(8,128)} %get-tuple-element.271, f32[3,512,1024]{2,1,0:T(8,128)S(1)} %bitcast.456, f32[3,512]{1,0:T(4,128)S(1)} %get-tuple-element.270, f32[3,512]{1,0:T(4,128)S(1)} %log_add_fusion, pred[512,1024]{1,0:T(8,128)(4,1)} %copy-done.6, ...), kind=kLoop, calls=%fused_computation | loop fusion | flops 18874368 | bytes 32530432 | tf_op jit(solution)/shard_map/convert_element_type | solution.py:135
  295.7 3.4 pad_maximum_fusion
  299.1 4.6 copy.63
  317.5 8.3 %all-to-all-start.6 = ((bf16[32,24,590]{2,1,0:T(8,128)(2,1)}), bf16[32,24,590]{2,1,0:T(8,128)(2,1)S(1)}, u32[]{:S(2)}, u32[]{:S(2)}) async-start(bf16[32,24,590]{2,1,0:T(8,128)(2,1)} %bitcast.103), calls=%async_computation.6 | async-start | bytes 1966080 | tf_op jit(solution)/shard_map/all_to_all | solution.py:55
  325.9 4.5 fusion.99
  331.6 8.5 %all-to-all-done.6 = bf16[32,24,590]{2,1,0:T(8,128)(2,1)S(1)} async-done(((bf16[32,24,590]{2,1,0:T(8,128)(2,1)}), bf16[32,24,590]{2,1,0:T(8,128)(2,1)S(1)}, u32[]{:S(2)}, u32[]{:S(2)}) %all-to-all-start.6) | async-done | bytes 906272 | tf_op jit(solution)/shard_map/all_to_all | solution.py:55
  341.0 6.1 %all-to-all-start.3 = ((bf16[32,24,1728]{2,1,0:T(8,128)(2,1)}), bf16[32,24,1728]{2,1,0:T(8,128)(2,1)S(1)}, u32[]{:S(2)}, u32[]{:S(2)}) async-start(bf16[32,24,1728]{2,1,0:T(8,128)(2,1)} %bitcast.89), calls=%async_computation.3 | async-start | bytes 5505024 | tf_op jit(solution)/shard_map/all_to_all | solution.py:55
  350.4 4.3 fusion.280
  384.9 7.7 %all-to-all-start.4 = ((bf16[32,24,590]{2,1,0:T(8,128)(2,1)}), bf16[32,24,590]{2,1,0:T(8,128)(2,1)}, u32[]{:S(2)}, u32[]{:S(2)}) async-start(bf16[32,24,590]{2,1,0:T(8,128)(2,1)} %bitcast.90), calls=%async_computation.4 | async-start | bytes 1966080 | tf_op jit(solution)/shard_map/all_to_all | solution.py:55
  394.1 13.0 %all-to-all-done.4 = bf16[32,24,590]{2,1,0:T(8,128)(2,1)} async-done(((bf16[32,24,590]{2,1,0:T(8,128)(2,1)}), bf16[32,24,590]{2,1,0:T(8,128)(2,1)}, u32[]{:S(2)}, u32[]{:S(2)}) %all-to-all-start.4) | async-done | bytes 906272 | tf_op jit(solution)/shard_map/all_to_all | solution.py:55
  414.4 4.3 all-to-all-start.7
  418.7 6.3 %all-to-all-done.7 = bf16[8,24,768]{2,1,0:T(8,128)(2,1)} async-done(((bf16[8,24,768]{2,1,0:T(8,128)(2,1)}), bf16[8,24,768]{2,1,0:T(8,128)(2,1)}, u32[]{:S(2)}, u32[]{:S(2)}) %all-to-all-start.7) | async-done | bytes 294944 | tf_op jit(solution)/shard_map/all_to_all | solution.py:243
  429.0 3.3 collective-permute-done.20
  438.3 7.4 %collective-permute-done.22 = bf16[2,192,768]{2,1,0:T(8,128)(2,1)S(1)} collective-permute-done((bf16[2,192,768]{2,1,0:T(8,128)(2,1)S(1)}, bf16[2,192,768]{2,1,0:T(8,128)(2,1)S(1)}, u32[]{:S(2)}, u32[]{:S(2)}) %collective-permute-start.22) | collective-permute-done | bytes 589856 | tf_op jit(solution)/shard_map/ppermute | solution.py:33
  445.7 11.6 %collective-permute-done.21 = bf16[2,192,768]{2,1,0:T(8,128)(2,1)S(1)} collective-permute-done((bf16[2,192,768]{2,1,0:T(8,128)(2,1)S(1)}, bf16[2,192,768]{2,1,0:T(8,128)(2,1)S(1)}, u32[]{:S(2)}, u32[]{:S(2)}) %collective-permute-start.21) | collective-permute-done | bytes 589856 | tf_op jit(solution)/shard_map/ppermute | solution.py:33
  457.3 5.6 collective-permute-done.23
  492.8 3.9 select_reduce_fusion.4
  497.5 6.4 %multiply_add_fusion.22 = f32[768,768]{1,0:T(8,128)S(1)} fusion(f32[768,768]{1,0:T(8,128)} %get-tuple-element.97, f32[]{:T(128)S(6)} %mul.805), kind=kOutput, calls=%fused_computation.133 | convolution fusion | flops 2720858112 | bytes 4718596 | tf_op jit(solution)/shard_map/dot_general | solution.py:227
  510.0 3.2 fusion.313
  513.3 3.2 multiply_add_fusion.15
  522.5 3.3 fusion.314
  525.8 3.2 multiply_add_fusion.9
  533.6 3.4 fusion.315
  551.0 4.9 all-to-all-start.8
  557.6 7.0 %all-to-all-done.8 = bf16[32,24,220]{2,1,0:T(8,128)(2,1)S(1)} async-done(((bf16[32,24,220]{2,1,0:T(8,128)(2,1)}), bf16[32,24,220]{2,1,0:T(8,128)(2,1)S(1)}, u32[]{:S(2)}, u32[]{:S(2)}) %all-to-all-start.8) | async-done | bytes 337952 | tf_op jit(solution)/shard_map/all_to_all | solution.py:271
  (596 shorter events, 263.4 us)
Async XLA Ops:
  5.1 21.6 %collective-permute-start.1 = (f16[256,768]{1,0:T(8,128)(2,1)}, f16[256,768]{1,0:T(8,128)(2,1)S(1)}, u32[]{:S(2)}, u32[]{:S(2)}) collective-permute-start(f16[256,768]{1,0:T(8,128)(2,1)} %fusion.156), channel_id=1, source_target_pairs={{0,2},{1,3},{2,0},{3,1},{4,6},{5,7},{6,4},{7,5},{8,10},{9,11},{10,... | collective-permute-start | bytes 1179656 | tf_op jit(solution)/shard_map/ppermute | solution.py:37
  8.6 19.5 %collective-permute-start = (f16[256,768]{1,0:T(8,128)(2,1)}, f16[256,768]{1,0:T(8,128)(2,1)}, u32[]{:S(2)}, u32[]{:S(2)}) collective-permute-start(f16[256,768]{1,0:T(8,128)(2,1)} %fusion.156), channel_id=1, source_target_pairs={{0,1},{1,0},{2,3},{3,2},{4,5},{5,4},{6,7},{7,6},{8,9},{9,8},{10,11... | collective-permute-start | bytes 1179656 | tf_op jit(solution)/shard_map/ppermute | solution.py:37
  12.5 96.2 %collective-permute-start.11 = (bf16[256,768]{1,0:T(8,128)(2,1)}, bf16[256,768]{1,0:T(8,128)(2,1)}, u32[]{:S(2)}, u32[]{:S(2)}) collective-permute-start(bf16[256,768]{1,0:T(8,128)(2,1)} %get-tuple-element.182), channel_id=1, source_target_pairs={{0,2},{1,3},{2,0},{3,1},{4,6},{5,7},{6,4},{7,5},{8,10},{9,11},{10,... | collective-permute-start | bytes 1179656 | tf_op jit(solution)/shard_map/ppermute | solution.py:37
  13.8 26.8 %all-to-all-start = ((bf16[32,24,576]{2,1,0:T(8,128)(2,1)}), bf16[32,24,576]{2,1,0:T(8,128)(2,1)}, u32[]{:S(2)}, u32[]{:S(2)}) async-start(bf16[32,24,576]{2,1,0:T(8,128)(2,1)} %broadcast_in_dim.142), calls=%async_computation | async-start | bytes 1966080 | tf_op jit(solution)/shard_map/all_to_all | solution.py:51
  25.9 182.3 %copy-start.33 = (f32[1024,8]{0,1:T(8,128)}, f32[1024,8]{0,1:T(8,128)S(1)}, u32[]{:S(2)}) copy-start(f32[1024,8]{0,1:T(8,128)S(1)} %get-tuple-element.243) | copy-start | bytes 98308
  25.9 182.3 %copy-start.62 = (f32[1024,8]{0,1:T(8,128)}, f32[1024,8]{0,1:T(8,128)S(1)}, u32[]{:S(2)}) copy-start(f32[1024,8]{0,1:T(8,128)S(1)} %get-tuple-element.241) | copy-start | bytes 98308
  26.1 70.8 %copy-start.109 = (f32[768]{0:T(1024)}, f32[768]{0:T(1024)S(1)}, u32[]{:S(2)}) copy-start(f32[768]{0:T(1024)S(1)} %add.460) | copy-start | bytes 9220
  26.7 2.0 collective-permute-start.2
  28.1 250.2 %copy-start.3 = (pred[512,1024]{1,0:T(8,128)(4,1)}, pred[512,1024]{1,0:T(8,128)(4,1)S(1)}, u32[]{:S(2)}) copy-start(pred[512,1024]{1,0:T(8,128)(4,1)S(1)} %get-tuple-element.143) | copy-start | bytes 1572868
  28.1 255.4 %copy-start.6 = (pred[512,1024]{1,0:T(8,128)(4,1)}, pred[512,1024]{1,0:T(8,128)(4,1)S(1)}, u32[]{:S(2)}) copy-start(pred[512,1024]{1,0:T(8,128)(4,1)S(1)} %get-tuple-element.144) | copy-start | bytes 1572868
  42.3 36.7 %all-to-all-start.1 = ((bf16[32,24,1728]{2,1,0:T(8,128)(2,1)}), bf16[32,24,1728]{2,1,0:T(8,128)(2,1)}, u32[]{:S(2)}, u32[]{:S(2)}) async-start(bf16[32,24,1728]{2,1,0:T(8,128)(2,1)} %broadcast_in_dim.143), calls=%async_computation.1 | async-start | bytes 5505024 | tf_op jit(solution)/shard_map/all_to_all | solution.py:51
  80.9 60.0 %all-to-all-start.2 = ((bf16[32,24,2304]{2,1,0:T(8,128)(2,1)}), bf16[32,24,2304]{2,1,0:T(8,128)(2,1)}, u32[]{:S(2)}, u32[]{:S(2)}) async-start(bf16[32,24,2304]{2,1,0:T(8,128)(2,1)} %broadcast_in_dim.149), calls=%async_computation.2 | async-start | bytes 7077888 | tf_op jit(solution)/shard_map/all_to_all | solution.py:51
  107.4 7.0 %collective-permute-start.3 = (bf16[2,256,768]{2,1,0:T(8,128)(2,1)S(1)}, bf16[2,256,768]{2,1,0:T(8,128)(2,1)}, u32[]{:S(2)}, u32[]{:S(2)}) collective-permute-start(bf16[2,256,768]{2,1,0:T(8,128)(2,1)S(1)} %slice.735), channel_id=1, source_target_pairs={{0,1},{1,0},{2,3},{3,2},{4,5},{5,4},{6,7},{7,6},{8,9},{9,8},{10,11... | collective-permute-start | bytes 2359304 | tf_op jit(solution)/shard_map/ppermute | solution.py:37
  108.6 3.1 collective-permute-start.10
  108.7 3.3 collective-permute-start.12
  114.5 26.3 %copy-start.118 = (f32[768]{0:T(1024)S(1)}, f32[768]{0:T(1024)}, u32[]{:S(2)}) copy-start(f32[768]{0:T(1024)} %get-tuple-element.82) | copy-start | bytes 9220
  115.8 24.9 %collective-permute-start.4 = (bf16[256,768]{1,0:T(8,128)(2,1)S(1)}, bf16[256,768]{1,0:T(8,128)(2,1)S(1)}, u32[]{:S(2)}, u32[]{:S(2)}) collective-permute-start(bf16[256,768]{1,0:T(8,128)(2,1)S(1)} %fusion.183), channel_id=1, source_target_pairs={{0,2},{1,3},{2,0},{3,1},{4,6},{5,7},{6,4},{7,5},{8,10},{9,11},{10,... | collective-permute-start | bytes 1179656 | tf_op jit(solution)/shard_map/ppermute | solution.py:37
  149.2 15.0 %collective-permute-start.5 = (f16[256,768]{1,0:T(8,128)(2,1)S(1)}, f16[256,768]{1,0:T(8,128)(2,1)S(1)}, u32[]{:S(2)}, u32[]{:S(2)}) collective-permute-start(f16[256,768]{1,0:T(8,128)(2,1)S(1)} %fusion.179), channel_id=1, source_target_pairs={{0,1},{1,0},{2,3},{3,2},{4,5},{5,4},{6,7},{7,6},{8,9},{9,8},{10,11... | collective-permute-start | bytes 1179656 | tf_op jit(solution)/shard_map/ppermute | solution.py:37
  151.0 12.2 %collective-permute-start.6 = (f16[256,768]{1,0:T(8,128)(2,1)S(1)}, f16[256,768]{1,0:T(8,128)(2,1)S(1)}, u32[]{:S(2)}, u32[]{:S(2)}) collective-permute-start(f16[256,768]{1,0:T(8,128)(2,1)S(1)} %fusion.179), channel_id=1, source_target_pairs={{0,2},{1,3},{2,0},{3,1},{4,6},{5,7},{6,4},{7,5},{8,10},{9,11},{10,... | collective-permute-start | bytes 1179656 | tf_op jit(solution)/shard_map/ppermute | solution.py:37
  163.2 2.2 collective-permute-start.7
  207.0 15.0 %collective-permute-start.8 = (bf16[2,256,768]{2,1,0:T(8,128)(2,1)S(1)}, bf16[2,256,768]{2,1,0:T(8,128)(2,1)S(1)}, u32[]{:S(2)}, u32[]{:S(2)}) collective-permute-start(bf16[2,256,768]{2,1,0:T(8,128)(2,1)S(1)} %slice.761), channel_id=1, source_target_pairs={{0,1},{1,0},{2,3},{3,2},{4,5},{5,4},{6,7},{7,6},{8,9},{9,8},{10,11... | collective-permute-start | bytes 2359304 | tf_op jit(solution)/shard_map/ppermute | solution.py:37
  215.7 4.3 collective-permute-start.13
  220.2 12.2 %collective-permute-start.14 = (bf16[256,768]{1,0:T(8,128)(2,1)S(1)}, bf16[256,768]{1,0:T(8,128)(2,1)S(1)}, u32[]{:S(2)}, u32[]{:S(2)}) collective-permute-start(bf16[256,768]{1,0:T(8,128)(2,1)S(1)} %fusion.186), channel_id=1, source_target_pairs={{0,2},{1,3},{2,0},{3,1},{4,6},{5,7},{6,4},{7,5},{8,10},{9,11},{10,... | collective-permute-start | bytes 1179656 | tf_op jit(solution)/shard_map/ppermute | solution.py:37
  222.3 18.6 %collective-permute-start.9 = (bf16[256,768]{1,0:T(8,128)(2,1)S(1)}, bf16[256,768]{1,0:T(8,128)(2,1)S(1)}, u32[]{:S(2)}, u32[]{:S(2)}) collective-permute-start(bf16[256,768]{1,0:T(8,128)(2,1)S(1)} %fusion.185), channel_id=1, source_target_pairs={{0,2},{1,3},{2,0},{3,1},{4,6},{5,7},{6,4},{7,5},{8,10},{9,11},{10,... | collective-permute-start | bytes 1179656 | tf_op jit(solution)/shard_map/ppermute | solution.py:37
  242.8 21.0 %collective-permute-start.16 = (bf16[256,768]{1,0:T(8,128)(2,1)S(1)}, bf16[256,768]{1,0:T(8,128)(2,1)S(1)}, u32[]{:S(2)}, u32[]{:S(2)}) collective-permute-start(bf16[256,768]{1,0:T(8,128)(2,1)S(1)} %convert_element_type.374), channel_id=1, source_target_pairs={{0,2},{1,3},{2,0},{3,1},{4,6},{5,7},{6,4},{7,5},{8,10},{9,11},{10,... | collective-permute-start | bytes 1179656 | tf_op jit(solution)/shard_map/ppermute | solution.py:37
  250.9 62.3 %all-to-all-start.5 = ((bf16[32,24,1728]{2,1,0:T(8,128)(2,1)}), bf16[32,24,1728]{2,1,0:T(8,128)(2,1)}, u32[]{:S(2)}, u32[]{:S(2)}) async-start(bf16[32,24,1728]{2,1,0:T(8,128)(2,1)} %bitcast.461), calls=%async_computation.5 | async-start | bytes 5505024 | tf_op jit(solution)/shard_map/all_to_all | solution.py:55
  262.2 2.9 collective-permute-start.15
  263.8 1.9 collective-permute-start.17
  317.5 22.6 %all-to-all-start.6 = ((bf16[32,24,590]{2,1,0:T(8,128)(2,1)}), bf16[32,24,590]{2,1,0:T(8,128)(2,1)S(1)}, u32[]{:S(2)}, u32[]{:S(2)}) async-start(bf16[32,24,590]{2,1,0:T(8,128)(2,1)} %bitcast.103), calls=%async_computation.6 | async-start | bytes 1966080 | tf_op jit(solution)/shard_map/all_to_all | solution.py:55
  341.0 41.1 %all-to-all-start.3 = ((bf16[32,24,1728]{2,1,0:T(8,128)(2,1)}), bf16[32,24,1728]{2,1,0:T(8,128)(2,1)S(1)}, u32[]{:S(2)}, u32[]{:S(2)}) async-start(bf16[32,24,1728]{2,1,0:T(8,128)(2,1)} %bitcast.89), calls=%async_computation.3 | async-start | bytes 5505024 | tf_op jit(solution)/shard_map/all_to_all | solution.py:55
  356.4 20.1 %collective-permute-start.18 = (bf16[2,256,768]{2,1,0:T(8,128)(2,1)S(1)}, bf16[2,256,768]{2,1,0:T(8,128)(2,1)}, u32[]{:S(2)}, u32[]{:S(2)}) collective-permute-start(bf16[2,256,768]{2,1,0:T(8,128)(2,1)S(1)} %slice.793), channel_id=1, source_target_pairs={{0,1},{1,0},{2,3},{3,2},{4,5},{5,4},{6,7},{7,6},{8,9},{9,8},{10,11... | collective-permute-start | bytes 2359304 | tf_op jit(solution)/shard_map/ppermute | solution.py:37
  379.9 48.1 %collective-permute-start.19 = (bf16[256,768]{1,0:T(8,128)(2,1)}, bf16[256,768]{1,0:T(8,128)(2,1)S(1)}, u32[]{:S(2)}, u32[]{:S(2)}) collective-permute-start(bf16[256,768]{1,0:T(8,128)(2,1)} %fusion.187), channel_id=1, source_target_pairs={{0,2},{1,3},{2,0},{3,1},{4,6},{5,7},{6,4},{7,5},{8,10},{9,11},{10,... | collective-permute-start | bytes 1179656 | tf_op jit(solution)/shard_map/ppermute | solution.py:37
  384.9 22.3 %all-to-all-start.4 = ((bf16[32,24,590]{2,1,0:T(8,128)(2,1)}), bf16[32,24,590]{2,1,0:T(8,128)(2,1)}, u32[]{:S(2)}, u32[]{:S(2)}) async-start(bf16[32,24,590]{2,1,0:T(8,128)(2,1)} %bitcast.90), calls=%async_computation.4 | async-start | bytes 1966080 | tf_op jit(solution)/shard_map/all_to_all | solution.py:55
  392.6 35.4 %copy-start.9 = (bf16[1,256,768]{2,1,0:T(8,128)(2,1)S(1)}, bf16[1,256,768]{2,1,0:T(8,128)(2,1)}, u32[]{:S(2)}) copy-start(bf16[1,256,768]{2,1,0:T(8,128)(2,1)} %param.11) | copy-start | bytes 1179652
  392.6 35.4 %copy-start.14 = (f32[2,256,768]{2,1,0:T(8,128)S(1)}, f32[2,256,768]{2,1,0:T(8,128)}, u32[]{:S(2)}) copy-start(f32[2,256,768]{2,1,0:T(8,128)} %copy-done.13) | copy-start | bytes 4718596
  392.6 35.4 %copy-start.98 = (f32[256]{0:T(256)S(1)}, f32[256]{0:T(256)}, u32[]{:S(2)}) copy-start(f32[256]{0:T(256)} %copy-done.97) | copy-start | bytes 3076
  392.6 36.4 %copy-start.52 = (f32[24,2304]{1,0:T(8,128)}, f32[24,2304]{1,0:T(8,128)S(1)}, u32[]{:S(2)}) copy-start(f32[24,2304]{1,0:T(8,128)S(1)} %multiply_add_fusion.41) | copy-start | bytes 663556
  409.1 28.0 %copy-start.11 = (f32[256,768]{1,0:T(8,128)S(1)}, f32[256,768]{1,0:T(8,128)}, u32[]{:S(2)}) copy-start(f32[256,768]{1,0:T(8,128)} %copy-done.10) | copy-start | bytes 2359300
  409.2 28.0 %copy-start.108 = (f32[256]{0:T(256)S(1)}, f32[256]{0:T(256)}, u32[]{:S(2)}) copy-start(f32[256]{0:T(256)} %copy-done.107) | copy-start | bytes 3076
  414.4 10.6 %all-to-all-start.7 = ((bf16[8,24,768]{2,1,0:T(8,128)(2,1)}), bf16[8,24,768]{2,1,0:T(8,128)(2,1)}, u32[]{:S(2)}, u32[]{:S(2)}) async-start(bf16[8,24,768]{2,1,0:T(8,128)(2,1)} %fusion.227), calls=%async_computation.7 | async-start | bytes 589824 | tf_op jit(solution)/shard_map/all_to_all | solution.py:243
  425.0 7.3 %collective-permute-start.20 = (bf16[192,768]{1,0:T(8,128)(2,1)}, bf16[192,768]{1,0:T(8,128)(2,1)S(1)}, u32[]{:S(2)}, u32[]{:S(2)}) collective-permute-start(bf16[192,768]{1,0:T(8,128)(2,1)} %bitcast.118), channel_id=1, source_target_pairs={{0,2},{1,3},{2,0},{3,1},{4,6},{5,7},{6,4},{7,5},{8,10},{9,11},{10,... | collective-permute-start | bytes 884744 | tf_op jit(solution)/shard_map/ppermute | solution.py:37
  433.4 12.3 %collective-permute-start.22 = (bf16[2,192,768]{2,1,0:T(8,128)(2,1)S(1)}, bf16[2,192,768]{2,1,0:T(8,128)(2,1)S(1)}, u32[]{:S(2)}, u32[]{:S(2)}) collective-permute-start(bf16[2,192,768]{2,1,0:T(8,128)(2,1)S(1)} %get-tuple-element.186), channel_id=1, source_target_pairs={{0,8},{4,12},{8,0},{12,4},{16,24},{20,28},{24,16},{28,20},{32,40},... | collective-permute-start | bytes 1769480 | tf_op jit(solution)/shard_map/ppermute | solution.py:33
  435.6 21.7 %collective-permute-start.21 = (bf16[2,192,768]{2,1,0:T(8,128)(2,1)S(1)}, bf16[2,192,768]{2,1,0:T(8,128)(2,1)S(1)}, u32[]{:S(2)}, u32[]{:S(2)}) collective-permute-start(bf16[2,192,768]{2,1,0:T(8,128)(2,1)S(1)} %get-tuple-element.186), channel_id=1, source_target_pairs={{0,4},{4,0},{8,12},{12,8},{16,20},{20,16},{24,28},{28,24},{32,36},... | collective-permute-start | bytes 1769480 | tf_op jit(solution)/shard_map/ppermute | solution.py:33
  435.6 27.3 %collective-permute-start.23 = (bf16[2,192,768]{2,1,0:T(8,128)(2,1)S(1)}, bf16[2,192,768]{2,1,0:T(8,128)(2,1)S(1)}, u32[]{:S(2)}, u32[]{:S(2)}) collective-permute-start(bf16[2,192,768]{2,1,0:T(8,128)(2,1)S(1)} %get-tuple-element.186), channel_id=1, source_target_pairs={{0,12},{4,8},{8,4},{12,0},{16,28},{20,24},{24,20},{28,16},{32,44},... | collective-permute-start | bytes 1769480 | tf_op jit(solution)/shard_map/ppermute | solution.py:33
  465.6 27.1 %collective-permute-start.24 = (f32[768,768]{1,0:T(8,128)S(1)}, f32[768,768]{1,0:T(8,128)}, u32[]{:S(2)}, u32[]{:S(2)}) collective-permute-start(f32[768,768]{1,0:T(8,128)S(1)} %convolution_add_fusion), channel_id=1, source_target_pairs={{0,1},{1,0},{2,3},{3,2},{4,5},{5,4},{6,7},{7,6},{8,9},{9,8},{10,11... | collective-permute-start | bytes 7077896 | tf_op jit(solution)/shard_map/ppermute | solution.py:37
  474.2 1.6 collective-permute-start.25
  476.5 7.8 %collective-permute-start.26 = (f32[24,10]{1,0:T(8,128)}, f32[24,10]{1,0:T(8,128)}, u32[]{:S(2)}, u32[]{:S(2)}) collective-permute-start(f32[24,10]{1,0:T(8,128)} %fusion.387), channel_id=1, source_target_pairs={{0,2},{1,3},{2,0},{3,1},{4,6},{5,7},{6,4},{7,5},{8,10},{9,11},{10,... | collective-permute-start | bytes 2888 | tf_op jit(solution)/shard_map/ppermute | solution.py:37
  551.0 13.5 %all-to-all-start.8 = ((bf16[32,24,220]{2,1,0:T(8,128)(2,1)}), bf16[32,24,220]{2,1,0:T(8,128)(2,1)S(1)}, u32[]{:S(2)}, u32[]{:S(2)}) async-start(bf16[32,24,220]{2,1,0:T(8,128)(2,1)} %pad_maximum_fusion.22), calls=%async_computation.8 | async-start | bytes 786432 | tf_op jit(solution)/shard_map/all_to_all | solution.py:271
  (123 other events, 763.3 us)

commit v2 on v1

v2 whole, which is shorter than its diff:
```python
import functools
import math

import jax
import jax.numpy as jnp
import numpy as np
from jax import lax
from jax.experimental import pallas as pl
from jax.experimental.pallas import tpu as pltpu
from jax.sharding import PartitionSpec as P

D = 768
FF = 3072
HD = 64
ROT = 16
CHUNK = 24
EPS_NORM = 1e-05
MOMENTUM = 0.95
STEP_SCALE = 0.4
RATE_VEC = 0.5
COLS = 192
HEADS_HERE = 3
NS_STEPS = 5
EPS_ORTH = 1e-07
COEF_A = 3.4445
COEF_B = -4.775
COEF_C = 2.0315
NEG_FILL = -1e30
BF = jnp.bfloat16
F32 = jnp.float32
VMEM = pltpu.VMEM


def dot_nn(a, b):
    return lax.dot_general(a, b, (((1,), (0,)), ((), ())), preferred_element_type=F32)


def dot_nt(a, b):
    return lax.dot_general(a, b, (((1,), (1,)), ((), ())), preferred_element_type=F32)


def dot_tn(a, b):
    return lax.dot_general(a, b, (((0,), (0,)), ((), ())), preferred_element_type=F32)


def call(kernel, outs, ins, scratch=(), grid=None, in_specs=None, out_specs=None, flops=0, limit=60):
    whole = pl.BlockSpec(memory_space=VMEM)
    kwargs = {} if grid is None else dict(grid=grid)
    return pl.pallas_call(
        kernel,
        out_shape=[jax.ShapeDtypeStruct(s, d) for s, d in outs],
        in_specs=in_specs or [whole] * len(ins),
        out_specs=out_specs or [whole] * len(outs),
        scratch_shapes=list(scratch),
        compiler_params=pltpu.CompilerParams(vmem_limit_bytes=limit * 1024 * 1024),
        cost_estimate=pl.CostEstimate(flops=flops, bytes_accessed=1 << 16, transcendentals=0),
        **kwargs,
    )(*ins)


SMEM_SPEC = pl.BlockSpec(memory_space=pltpu.SMEM)
NEAR_SPEC = pl.BlockSpec((D, D), lambda *_: (0, 2))
WIDE = 2304


def head_mask(h):
    lane = lax.broadcasted_iota(jnp.int32, (1, COLS), 1)
    return ((lane >= h * HD) & (lane < (h + 1) * HD)).astype(BF)


def allowed_t(start_row, i, width):
    key = lax.broadcasted_iota(jnp.int32, (width, 256), 0)
    query = lax.broadcasted_iota(jnp.int32, (width, 256), 1) + i * 256
    return (key >= start_row) & (key <= query)


def rope_at(cos_ref, sin_ref, there):
    lane = lax.broadcasted_iota(jnp.int32, (8, COLS), 1) % HD
    angle = lax.broadcasted_iota(jnp.int32, (8, COLS), 0)
    spread = ((lane < ROT) & (lane % (ROT // 2) == angle)).astype(F32)
    rest = (lax.broadcasted_iota(jnp.int32, (1, COLS), 1) % HD >= ROT).astype(F32)
    exact = dict(preferred_element_type=F32, precision=lax.Precision.HIGHEST)
    over = (((0,), (0,)), ((), ()))
    cosine = lax.dot_general(cos_ref[:, there], spread, over, **exact) + rest
    return cosine, lax.dot_general(sin_ref[:, there], spread, over, **exact)


def attend_forward_kernel(
    me_ref, first0_ref, first1_ref, first2_ref, first3_ref, w_ref, bias_ref, turn_ref, cos_ref, sin_ref, start_ref,
    q_ref, k_ref, v_ref, lse_ref, mixed_ref,
):
    me = me_ref[0]
    turn = turn_ref[...]
    wq, wk, wv = w_ref[:, COLS : 2 * COLS], w_ref[:, 2 * COLS : 3 * COLS], w_ref[:, 3 * COLS :]
    wqt = dot_nn(wq, turn).astype(BF)
    wkt = dot_nn(wk, turn).astype(BF)
    bias = bias_ref[:3]
    turned = lax.dot_general(
        bias[:2], turn.astype(F32), (((1,), (0,)), ((), ())),
        preferred_element_type=F32, precision=lax.Precision.HIGHEST,
    )
    for a in range(4):
        there = pl.ds(pl.multiple_of((me ^ a) * 256, 256), 256)
        x = (first0_ref, first1_ref, first2_ref, first3_ref)[a][...]
        cosine, sine = rope_at(cos_ref, sin_ref, there)
        q = (dot_nn(x, wq) + bias[0:1]) * cosine + (dot_nn(x, wqt) + turned[0:1]) * sine
        k = (dot_nn(x, wk) + bias[1:2]) * cosine + (dot_nn(x, wkt) + turned[1:2]) * sine
        q_ref[there, :] = q.astype(BF)
        k_ref[there, :] = k.astype(BF)
        v_ref[there, :] = (dot_nn(x, wv) + bias[2:3]).astype(BF)
    for i in range(4):
        n = (i + 1) * 256
        rows = slice(i * 256, n)
        q, k, v = q_ref[rows, :], k_ref[:n, :], v_ref[:n, :]
        allowed = allowed_t(start_ref[:, rows], i, n)
        mixed = jnp.zeros((256, COLS), F32)
        for h in range(HEADS_HERE):
            mask = head_mask(h)
            scores = dot_nt(k, q * (mask * BF(0.125)))
            scores = jnp.where(allowed, scores, NEG_FILL)
            top = jnp.max(scores, 0, keepdims=True)
            shifted = jnp.exp(scores - top)
            total = jnp.sum(shifted, 0, keepdims=True)
            probability = (shifted * (1.0 / total)).astype(BF)
            mixed = mixed + dot_tn(probability, v) * mask.astype(F32)
            lse_ref[h : h + 1, rows] = top + jnp.log(total)
        there = pl.ds(pl.multiple_of((me ^ i) * 256, 256), 256)
        mixed_ref[there, :] = mixed.astype(BF)


def attend_forward(me, first, w, bias, turn, cosine, sine, start):
    whole = pl.BlockSpec(memory_space=VMEM)
    ins = (me, *first, w, bias, turn, cosine, sine, start)
    outs = [((1024, COLS), BF)] * 3 + [((8, 1024), F32), ((1024, COLS), BF)]
    return call(
        attend_forward_kernel, outs, ins, in_specs=[SMEM_SPEC] + [whole] * 4 + [NEAR_SPEC] + [whole] * 5,
        grid=(1,), flops=10**7,
    )


def gelu_and_slope(pre):
    below = 0.5 * (1.0 + lax.erf(pre * 0.7071067811865476))
    return pre * below, below + pre * jnp.exp(-0.5 * pre * pre) * 0.3989422804014327


def forward_out_kernel(keep_in_ref, send_in_ref, mixed_ref, rest_ref, bias_ref, hidden_ref, slope_ref, keep_ref, send_ref):
    up_bias = jnp.concatenate([bias_ref[3 + r : 4 + r, :] for r in range(4)], 1)
    for a in range(2):
        rows = slice(a * 256, (a + 1) * 256)
        pre = dot_nn((keep_in_ref, send_in_ref)[a][...], rest_ref[:, :D]) + up_bias
        hidden, slope = gelu_and_slope(pre)
        hidden = hidden.astype(BF)
        hidden_ref[rows, :] = hidden
        slope_ref[rows, :] = slope
        out = dot_nt(hidden, rest_ref[:, D : 2 * D]) + dot_nt(mixed_ref[rows, :], rest_ref[:, 2 * D : 2 * D + COLS])
        if a == 0:
            keep_ref[...] = out
        else:
            send_ref[...] = out.astype(BF)


def forward_out(second, mixed, rest, bias, half):
    part = lambda n: pl.BlockSpec((512, n), lambda i, half=half: (half, 0))
    full = lambda *s: pl.BlockSpec(s, lambda i: (0,) * len(s))
    return pl.pallas_call(
        forward_out_kernel,
        grid=(1,),
        out_shape=[jax.ShapeDtypeStruct(s, d) for s, d in (((512, D), BF), ((512, D), F32), ((256, D), F32), ((256, D), BF))],
        in_specs=[full(256, D), full(256, D), part(COLS), full(D, WIDE), full(7, COLS)],
        out_specs=[full(512, D), full(512, D), full(256, D), full(256, D)],
        compiler_params=pltpu.CompilerParams(vmem_limit_bytes=60 << 20),
        cost_estimate=pl.CostEstimate(flops=10**7, bytes_accessed=1 << 16, transcendentals=0),
    )(second[2 * half], second[2 * half + 1], mixed, rest, bias)


def backward_rest_kernel(*refs):
    slots, refs = refs[:12], refs[12:]
    hidden_ref, hidden_far_ref, mixed_ref, slope_ref, slope_far_ref, rest_ref, gain_ref = refs[:7]
    grad_ref, d_mixed_ref, w_ref, sums_ref, acc_ref = refs[7:]
    step = pl.program_id(0)

    def one(slot):
        outer, second, scaled = slots[slot][...], slots[4 + slot][...], slots[8 + slot][...]
        hidden = (hidden_ref if slot < 2 else hidden_far_ref)[...]
        slope = (slope_ref if slot < 2 else slope_far_ref)[...]
        d_hidden = dot_nn(outer, rest_ref[:, D : 2 * D])
        d_mixed_ref[...] = dot_nn(outer, rest_ref[:, 2 * D : 2 * D + COLS]).astype(BF)
        d_pre = (d_hidden * slope).astype(BF)
        d_second = dot_nt(d_pre, rest_ref[:, :D])
        w_ref[...] = d_second * gain_ref[2:3, :]
        sums = jnp.concatenate(
            [
                jnp.sum(d_second * scaled.astype(F32), 0, keepdims=True),
                jnp.sum(d_second, 0, keepdims=True),
                jnp.sum(d_pre.astype(F32), 0, keepdims=True),
                jnp.zeros((5, D), F32),
            ],
            0,
        )
        up, down, out = dot_tn(second, d_pre), dot_tn(outer, hidden), dot_tn(outer, mixed_ref[...])
        if slot == 0:
            acc_ref[:, :D] = up
            acc_ref[:, D : 2 * D] = down
            acc_ref[:, 2 * D :] = out
            sums_ref[...] = sums
        elif slot < 3:
            acc_ref[:, :D] += up
            acc_ref[:, D : 2 * D] += down
            acc_ref[:, 2 * D :] += out
            sums_ref[...] += sums
        else:
            for total, first, last in ((up, 0, D), (down, D, 2 * D), (out, 2 * D, 1728)):
                total = acc_ref[:, first:last] + total
                for x in range(2):
                    for plane in range(16):
                        row = x * 384 + plane * CHUNK
                        grad_ref[plane, x, :, first:last] = total[row : row + CHUNK].astype(BF)
            sums_ref[...] += sums

    for slot in range(4):
        pl.when(step == slot)(lambda slot=slot: one(slot))


def backward_rest(outer, second, scaled, hidden, hidden_far, mixed, slope, slope_far, rest, gain):
    part = lambda n: pl.BlockSpec((256, n), lambda i: (i, 0))
    early = lambda n: pl.BlockSpec((256, n), lambda i: (jnp.minimum(i, 1), 0))
    late = lambda n: pl.BlockSpec((256, n), lambda i: (jnp.maximum(i, 2) - 2, 0))
    full = lambda *s: pl.BlockSpec(s, lambda i: (0,) * len(s))
    return pl.pallas_call(
        backward_rest_kernel,
        grid=(4,),
        out_shape=[
            jax.ShapeDtypeStruct(s, d)
            for s, d in (((16, 2, CHUNK, 1728), BF), ((1024, COLS), BF), ((1024, D), F32), ((8, D), F32))
        ],
        in_specs=[full(256, D)] * 12 + [early(D), late(D), part(COLS), early(D), late(D), full(D, WIDE), full(6, D)],
        out_specs=[full(16, 2, CHUNK, 1728), part(COLS), part(D), full(8, D)],
        scratch_shapes=[pltpu.VMEM((D, 1728), F32)],
        compiler_params=pltpu.CompilerParams(vmem_limit_bytes=60 << 20),
        cost_estimate=pl.CostEstimate(flops=10**7, bytes_accessed=1 << 16, transcendentals=0),
    )(*outer, *second, *scaled, hidden, hidden_far, mixed, slope, slope_far, rest, gain)


def attend_backward_kernel(
    me_ref, q_ref, k_ref, v_ref, lse_ref, d_mixed_ref, start_ref, cos_ref, sin_ref, turn_ref,
    w_ref, gain_ref, scaled0_ref, scaled1_ref, scaled2_ref, scaled3_ref, part_ref,
    proj_ref, keep_ref, send_ref, sums_ref, bias_ref, dq_ref, dk_ref, dv_ref,
):
    me = me_ref[0]
    dk_ref[...] = jnp.zeros((1024, COLS), F32)
    dv_ref[...] = jnp.zeros((1024, COLS), F32)
    for i in range(4):
        n = (i + 1) * 256
        rows = slice(i * 256, n)
        there = pl.ds(pl.multiple_of((me ^ i) * 256, 256), 256)
        d_mixed = d_mixed_ref[there, :]
        q, k, v = q_ref[rows, :], k_ref[:n, :], v_ref[:n, :]
        allowed = allowed_t(start_ref[:, rows], i, n)
        dq = jnp.zeros((256, COLS), F32)
        for h in range(HEADS_HERE):
            mask = head_mask(h)
            q_here = q * (mask * BF(0.125))
            d_here = d_mixed * mask
            scores = dot_nt(k, q_here)
            probability = jnp.where(allowed, jnp.exp(scores - lse_ref[h : h + 1, rows]), 0.0)
            d_prob = dot_nt(v, d_here)
            row = jnp.sum(probability * d_prob, 0, keepdims=True)
            d_score = (probability * (d_prob - row)).astype(BF)
            dq = dq + dot_tn(d_score, k) * (mask.astype(F32) * 0.125)
            dk_ref[:n, :] += dot_nn(d_score, q_here)
            dv_ref[:n, :] += dot_nn(probability.astype(BF), d_here)
        dq_ref[rows, :] = dq
    turn = turn_ref[...]

    def back(value, cosine, sine):
        upper = value.astype(BF)
        lower = (value - upper.astype(F32)).astype(BF)
        return value * cosine - (dot_nn(upper, turn) + dot_nn(lower, turn)) * sine

    sums = jnp.zeros((8, D), F32)
    bias = jnp.zeros((8, 576), F32)
    for a in range(4):
        there = pl.ds(pl.multiple_of((me ^ a) * 256, 256), 256)
        rows = slice(a * 256, (a + 1) * 256)
        cosine, sine = rope_at(cos_ref, sin_ref, there)
        dq = back(dq_ref[there, :], cosine, sine)
        dk = back(dk_ref[there, :], cosine, sine)
        proj = jnp.concatenate([dq, dk, dv_ref[there, :]], 1).astype(BF)
        proj_ref[rows, :] = proj
        d_first = dot_nt(proj, w_ref[:, COLS:])
        scaled = (scaled0_ref, scaled1_ref, scaled2_ref, scaled3_ref)[a][...]
        weighted = d_first * gain_ref[0:1, :] + part_ref[rows, :]
        if a % 2 == 0:
            keep_ref[a // 2] = weighted
        else:
            send_ref[a // 2] = weighted.astype(BF)
        sums = sums + jnp.concatenate(
            [
                jnp.sum(d_first * scaled.astype(F32), 0, keepdims=True),
                jnp.sum(d_first, 0, keepdims=True),
                jnp.zeros((6, D), F32),
            ],
            0,
        )
        bias = bias + jnp.concatenate(
            [jnp.sum(proj.astype(F32), 0, keepdims=True), jnp.zeros((7, 576), F32)], 0
        )
    sums_ref[...] = sums
    bias_ref[...] = bias


def attend_backward(me, q, k, v, lse, d_mixed, start, cosine, sine, turn, w, gain, scaled, part):
    whole = pl.BlockSpec(memory_space=VMEM)
    ins = (me, q, k, v, lse, d_mixed, start, cosine, sine, turn, w, gain, *scaled, part)
    outs = [((1024, 576), BF), ((2, 256, D), F32), ((2, 256, D), BF), ((8, D), F32), ((8, 576), F32)]
    return call(
        attend_backward_kernel, outs, ins, in_specs=[SMEM_SPEC] + [whole] * 9 + [NEAR_SPEC] + [whole] * 6,
        grid=(1,), scratch=[pltpu.VMEM((1024, COLS), F32)] * 3, flops=10**7,
    )


def grad_near_kernel(
    direct, first0_ref, first1_ref, first2_ref, first3_ref, proj_ref, sums_ref, sums_rest_ref, bias_ref, upstream_ref, out_ref
):
    total = dot_tn(first0_ref[...], proj_ref[:256, :])
    for a, ref in ((1, first1_ref), (2, first2_ref), (3, first3_ref)):
        total = total + dot_tn(ref[...], proj_ref[a * 256 : (a + 1) * 256, :])
    pre = sums_rest_ref[2:3, :]
    upper, lower = split(
        jnp.concatenate(
            [
                sums_ref[:2, :],
                sums_rest_ref[:2, :],
                jnp.sum(upstream_ref[...], 0, keepdims=True),
                jnp.concatenate([bias_ref[:1, :], pre[:, :COLS]], 1),
                jnp.concatenate([pre[:, COLS:], jnp.zeros((1, COLS), F32)], 1),
                jnp.zeros((1, D), F32),
            ],
            0,
        )
    )
    row = lax.broadcasted_iota(jnp.int32, (8, 16), 0)
    lane = lax.broadcasted_iota(jnp.int32, (8, 16), 1)
    small = dot_tn(upper, (row == lane).astype(BF)) + dot_tn(lower, (row + 8 == lane).astype(BF))
    for x in range(2):
        for plane in range(16):
            here = slice(x * 384 + plane * CHUNK, x * 384 + (plane + 1) * CHUNK)
            place = (x * 16 + plane,) if direct else (plane, x)
            out_ref[(*place, slice(None), slice(0, 576))] = total[here].astype(BF)
            out_ref[(*place, slice(None), slice(576, 592))] = small[here].astype(BF)


def grad_near(first, proj, parts, direct):
    shape = (32, CHUNK, 592) if direct else (16, 2, CHUNK, 592)
    return call(functools.partial(grad_near_kernel, direct), [(shape, BF)], (*first, proj, *parts), flops=10**7)[0]


def split(value):
    upper = value.astype(BF)
    return upper, (value - upper.astype(F32)).astype(BF)


def newton_schulz_kernel(
    place_ref, p0, p1, p2, p3, q0, q1, q2, q3, small_ref, out_ref,
    m_ref, g_ref, h_ref, gs_ref, ss_ref, hs_ref, x_ref, xs_ref,
):
    x, y = place_ref[0], place_ref[1]
    lane = lax.broadcasted_iota(jnp.int32, (1, D), 1)
    half = y // 2
    used = (x == 0) | ((lane >= half * COLS) & (lane < (half + 1) * COLS))
    for s, (p, q) in enumerate(((p0, q0), (p1, q1), (p2, q2), (p3, q3))):
        for b, ref in enumerate((p, q)):
            for c in range(2):
                m_ref[2 * b + c, s * 192 : (s + 1) * 192, :] = jnp.where(used, ref[c], jnp.zeros((), BF))

    def store(pair, lower, i, j, value):
        r, c = slice(i * 256, (i + 1) * 256), slice(j * 256, (j + 1) * 256)
        upper_part, lower_part = split(value)
        pair[0, r, c] = upper_part
        pair[1, r, c] = lower_part
        if i != j and lower:
            upper_part, lower_part = split(value.T)
            pair[0, c, r] = upper_part
            pair[1, c, r] = lower_part

    def product(a, b, finish):
        for j in range(3):
            n, c = (j + 1) * 256, slice(j * 256, (j + 1) * 256)
            value = dot_nn(a[0, :n, :], b[0, :, c]) + dot_nn(a[0, :n, :], b[1, :, c]) + dot_nn(a[1, :n, :], b[0, :, c])
            for i in range(j + 1):
                finish(i, j, value[i * 256 : (i + 1) * 256])

    def at(ref, i, j):
        return ref[i * 256 : (i + 1) * 256, j * 256 : (j + 1) * 256]

    def put(ref, i, j, value):
        ref[i * 256 : (i + 1) * 256, j * 256 : (j + 1) * 256] = value

    for j in range(3):
        n, c = (j + 1) * 256, slice(j * 256, (j + 1) * 256)
        value = dot_nt(m_ref[0, :n, :], m_ref[0, c, :])
        for b in range(1, 4):
            value = value + dot_nt(m_ref[b, :n, :], m_ref[b, c, :])
        g_ref[:n, c] = value
    trace = jnp.zeros((1, 1), F32)
    same = lax.broadcasted_iota(jnp.int32, (256, 256), 0) == lax.broadcasted_iota(jnp.int32, (256, 256), 1)
    for i in range(3):
        diagonal = jnp.where(same, at(g_ref, i, i), 0.0)
        trace = trace + jnp.sum(jnp.sum(diagonal, 1, keepdims=True), 0, keepdims=True)
    scale = 1.0 / (jnp.sqrt(trace) + EPS_ORTH)
    for j in range(3):
        for i in range(j + 1):
            value = at(g_ref, i, j) * (scale * scale)
            put(g_ref, i, j, value)
            store(gs_ref, True, i, j, value)
    which = jnp.where(x == 0, y, half)
    block = jnp.zeros((D, COLS), BF)
    for i in range(4):
        block = jnp.where(which == i, m_ref[0, :, i * COLS : (i + 1) * COLS], block)
    current = block.astype(F32) * scale
    x_ref[...] = current
    xs_ref[0], xs_ref[1] = split(current)

    def mix():
        def finish(i, j, value):
            store(ss_ref, True, i, j, COEF_B * at(g_ref, i, j) + COEF_C * value)

        product(gs_ref, gs_ref, finish)

    def advance():
        s0, s1 = ss_ref[0], ss_ref[1]
        return COEF_A * x_ref[...] + dot_nn(s0, xs_ref[0]) + dot_nn(s0, xs_ref[1]) + dot_nn(s1, xs_ref[0])

    def step(_, carry):
        mix()
        current = advance()
        x_ref[...] = current
        xs_ref[0], xs_ref[1] = split(current)

        def finish_h(i, j, value):
            value = COEF_A * at(g_ref, i, j) + value
            put(h_ref, i, j, value)
            store(hs_ref, True, i, j, value)

        product(ss_ref, gs_ref, finish_h)

        def finish_g(i, j, value):
            value = COEF_A * at(h_ref, i, j) + value
            put(g_ref, i, j, value)
            store(gs_ref, True, i, j, value)

        product(hs_ref, ss_ref, finish_g)
        return carry

    lax.fori_loop(0, NS_STEPS - 1, step, 0)
    mix()
    current = advance()
    for s in range(4):
        for group in range(8):
            row = s * 192 + group * 24
            out_ref[group, y ^ s, :, :COLS] = current[row : row + 24].astype(BF)
            out_ref[group, y ^ s, :, COLS:] = small_ref[...]


def newton_schulz(place, pieces, small):
    pair = pltpu.VMEM((2, D, D), BF)
    whole = pl.BlockSpec(memory_space=VMEM)
    return call(
        newton_schulz_kernel, [((8, 4, CHUNK, 224), BF)], (place, *pieces, small),
        in_specs=[SMEM_SPEC] + [whole] * 9,
        scratch=[pltpu.VMEM((4, D, D), BF)] + [pltpu.VMEM((D, D), F32)] * 2 + [pair] * 3
        + [pltpu.VMEM((D, COLS), F32), pltpu.VMEM((2, D, COLS), BF)],
        flops=10**7,
    )[0]


def pack_kernel(attn_ref, mlp_ref, out_ref):
    for layer in range(2):
        for m in range(2):
            parts = [mlp_ref[layer, m, :, r, :] for r in range(4)]
            out_ref[layer, :, m * D : (m + 1) * D] = jnp.concatenate(parts, 1).astype(BF)
        parts = [attn_ref[layer, m] for m in (3, 0, 1, 2)]
        out_ref[layer, :, 2 * D :] = jnp.concatenate(parts, 1).astype(BF)


def pack(attn_w, mlp_w):
    return call(pack_kernel, [((2, CHUNK, WIDE), BF)], (attn_w, mlp_w))[0]


def assemble_kernel(place_ref, a0, a1, a2, a2_more, a3, b0, b1, b2, b2_more, b3, out_ref):
    x, z, y = place_ref[0], place_ref[1], place_ref[2]
    for other, blocks in enumerate(((a0, a1, (a2, a2_more), a3), (b0, b1, (b2, b2_more), b3))):
        for outer, block in enumerate(blocks):
            for inner in range(4):
                value = block[inner // 2][inner % 2] if outer == 2 else block[inner]
                zr, yr = (outer, inner) if other else (inner, outer)
                out_ref[(x ^ other) * 16 + (z ^ zr) * 4 + (y ^ yr)] = value


def assemble(place, blocks):
    whole = pl.BlockSpec(memory_space=VMEM)
    return call(
        assemble_kernel, [((32, CHUNK, WIDE), BF)], (place, *blocks), in_specs=[SMEM_SPEC] + [whole] * 10
    )[0]


def momenta_kernel(
    attn_ref, mlp_ref, rest0_ref, rest1_ref, near1_ref, near0_ref, new_attn_ref, new_mlp_ref, sends_ref, small_ref
):
    total = jnp.sum(near0_ref[...].astype(F32), 0)
    near1 = near1_ref[...]
    none = jnp.zeros((CHUNK, 2 * COLS), BF)
    for layer, rest_ref, near in ((0, rest0_ref, total), (1, rest1_ref, near1)):
        for m in range(2):
            parts = []
            for r in range(4):
                first = m * D + r * COLS
                mom = MOMENTUM * mlp_ref[layer, m, :, r, :] + rest_ref[:, first : first + COLS]
                new_mlp_ref[layer, m, :, r, :] = mom
                parts.append(mom.astype(BF))
            sends_ref[2 * layer + m] = jnp.concatenate(parts, 1)
        parts = []
        for m in range(4):
            grad = near[:, m * COLS : (m + 1) * COLS] if m < 3 else rest_ref[:, 2 * D :]
            mom = MOMENTUM * attn_ref[layer, m] + grad
            new_attn_ref[layer, m] = mom
            parts.append(mom.astype(BF))
        sends_ref[4 + 2 * layer] = jnp.concatenate([*parts[:2], none], 1)
        sends_ref[5 + 2 * layer] = jnp.concatenate([*parts[2:], none], 1)
    here = total[:, 576:583] + total[:, 584:591]
    last = near1[:, 576:583] + near1[:, 584:591]
    small_ref[...] = jnp.concatenate([here[:, :5], last[:, :5], here[:, 5:], last[:, 5:]], 1)


def momenta(mom_attn, mom_mlp, *ins):
    outs = [(mom_attn.shape, F32), (mom_mlp.shape, F32), ((8, CHUNK, D), BF), ((CHUNK, 14), F32)]
    return call(momenta_kernel, outs, (mom_attn, mom_mlp, *ins))


def new_weights_kernel(back_ref, attn_ref, mlp_ref, new_attn_ref, new_mlp_ref, small_ref):
    def block(x, z, y):
        return back_ref[x * 16 + z * 4 + y, :, :COLS].astype(F32)

    for layer in range(2):
        for m in range(4):
            step = STEP_SCALE * math.sqrt(D) * block(1, 2 * layer + m // 2, 2 * (m % 2))
            new_attn_ref[layer, m] = attn_ref[layer, m] - step
        for m in range(2):
            for r in range(4):
                step = STEP_SCALE * math.sqrt(FF) * block(0, 2 * layer + m, r)
                new_mlp_ref[layer, m, :, r, :] = mlp_ref[layer, m, :, r, :] - step
    for i in range(32):
        part = back_ref[i, :, COLS:].astype(F32)
        small_ref[i] = part[:, :14] + part[:, 14:28]


def new_weights(back, attn_w, mlp_w):
    outs = [(attn_w.shape, F32), (mlp_w.shape, F32), ((32, CHUNK, 14), F32)]
    attn, mlp, small = call(new_weights_kernel, outs, (back, attn_w, mlp_w))
    return attn, mlp, small.reshape(D, 14)


def dp_swap(value, mask):
    return lax.ppermute(value, "dp", [(i, i ^ mask) for i in range(32)])


def tensor_swap(value, mask):
    return lax.ppermute(value, "tensor", [(i, i ^ mask) for i in range(4)])


def dp_place():
    me = lax.axis_index("dp")
    return me // 16, (me // 4) % 4, me % 4


def swap_four(pieces, unit):
    return [pieces[0]] + [dp_swap(pieces[s], s * unit) for s in (1, 2, 3)]


PLANE = [[x * 16 + i for i in range(16)] for x in range(2)]


def by_x(own, other):
    x = dp_place()[0]
    return jnp.stack([jnp.where(x == 0, own, other), jnp.where(x == 0, other, own)])


def spread_rows(shard, other):
    return jnp.concatenate([by_x(shard, other)[None]] * 16, 0)


def gather_rows(spread):
    return lax.all_to_all(spread, "dp", 0, 0, tiled=True, axis_index_groups=PLANE)


def gather_by_rings(shard):
    x, z, y = dp_place()
    other = dp_swap(shard, 16)
    halves = []
    for mine, unit, then in ((shard, 4, 1), (other, 1, 4)):
        block = jnp.stack(swap_four([mine] * 4, unit))
        left, right = dp_swap(block, then), dp_swap(block, 3 * then)
        halves += [block, left, dp_swap(right[:2], then), dp_swap(left[2:], 3 * then), right]
    return assemble(jnp.stack([x, z, y]).astype(jnp.int32), halves).reshape(D, WIDE)


def in_order(arrived):
    return arrived.transpose(1, 0, 2, 3).reshape(D, arrived.shape[3])


def scatter_rows(partial):
    return lax.all_to_all(partial, "dp", 0, 0, tiled=True, axis_index_groups=PLANE)


def add_arrived(arrived):
    sums = jnp.sum(arrived.astype(F32), 0)
    x = dp_place()[0]
    other = jnp.where(x == 0, sums[1], sums[0]).astype(BF)
    return jnp.where(x == 0, sums[0], sums[1]) + dp_swap(other, 16).astype(F32)


def gather_tokens(mine, beside=None):
    far = tensor_swap(mine, 2)
    near = tensor_swap(mine, 1)
    if beside is not None:
        far, beside = lax.optimization_barrier((far, beside))
    return [mine, near, far, tensor_swap(far, 1)], beside


def standardize(stream):
    center = stream - jnp.mean(stream, -1, keepdims=True)
    inverse = lax.rsqrt(jnp.mean(center * center, -1, keepdims=True) + EPS_NORM)
    return center * inverse, inverse


def rope_tables(labels):
    kinds = jnp.arange(8, dtype=jnp.int32)
    below = jnp.sum((labels[None, :] < kinds[:, None]).astype(jnp.int32), 1)
    start = jnp.sum(jnp.where(labels[None, :] == kinds[:, None], below[:, None], 0), 0)
    places = jnp.arange(labels.shape[0], dtype=jnp.int32) - start
    frequency = 10000.0 ** (jnp.arange(ROT // 2, dtype=F32) * (-2.0 / ROT))
    angles = places.astype(F32)[None, :] * frequency[:, None]
    cosine, sine = jnp.cos(angles), jnp.sin(angles)
    return jnp.cos(angles), jnp.sin(angles), start[None, :]


def turn_matrix():
    turn = np.zeros((COLS, COLS), np.float32)
    for head in range(HEADS_HERE):
        for i in range(ROT // 2):
            turn[head * HD + i + ROT // 2, head * HD + i] = -1.0
            turn[head * HD + i, head * HD + i + ROT // 2] = 1.0
    return turn


def normalized(stream, vector_rows, beside=None):
    scaled, inverse = standardize(stream)
    first, second, scaled_all = [], [], []
    slots, beside = gather_tokens(scaled.astype(jnp.float16), beside)
    for slot in slots:
        wide = slot.astype(F32)
        first.append((wide * vector_rows[0] + vector_rows[1]).astype(BF))
        second.append((wide * vector_rows[2] + vector_rows[3]).astype(BF))
        scaled_all.append(wide.astype(BF))
    return (scaled, inverse, first, second, scaled_all), beside


def forward_layer(stream, norms, weights, bias_rows, vector_rows, common):
    me, cosine, sine, start, turn = common
    scaled, inverse, first, second, scaled_all = norms
    q, k, v, lse, mixed = attend_forward(
        me, first, weights, bias_rows, turn, cosine, sine, start
    )
    hidden_far, slope_far, keep_far, send_far = forward_out(second, mixed, weights, bias_rows, 1)
    pair = (keep_far + tensor_swap(send_far, 1).astype(F32)).astype(BF)
    mixed, pair = lax.optimization_barrier((mixed, pair))
    hidden, slope, keep, send = forward_out(second, mixed, weights, bias_rows, 0)
    branch = keep + tensor_swap(send, 1).astype(F32) + tensor_swap(pair, 2).astype(F32)
    record = (q, k, v, lse, mixed, hidden, hidden_far, slope, slope_far)
    return record, stream + branch + vector_rows[4] + vector_rows[5]


def backward_layer(upstream, outer, record, weights, vector_rows, common, ready, last):
    me, cosine, sine, start, turn = common
    scaled, inverse, first, second, scaled_all, q, k, v, lse, mixed, hidden, hidden_far, slope, slope_far = record
    grad_rest, d_mixed, part, sums_rest = backward_rest(
        outer, second, scaled_all, hidden, hidden_far, mixed, slope, slope_far, weights, vector_rows
    )
    grad_rest = scatter_rows(grad_rest)
    d_mixed, ready = lax.optimization_barrier((d_mixed, ready))
    proj, keep, send, sums, bias = attend_backward(
        me, q, k, v, lse, d_mixed, start, cosine, sine, turn, weights, vector_rows, scaled_all, part
    )
    pair = keep + tensor_swap(send, 1).astype(F32)
    weighted = pair[0] + tensor_swap(pair[1].astype(BF), 2).astype(F32)
    new_upstream = upstream + inverse * (
        weighted
        - jnp.mean(weighted, -1, keepdims=True)
        - scaled * jnp.mean(weighted * scaled, -1, keepdims=True)
    )
    grad_near_here, grad_rest = lax.optimization_barrier((grad_near(first, proj, (sums, sums_rest, bias, upstream), last), grad_rest))
    grad_near_here = (
        lax.all_to_all(grad_near_here, "dp", 0, 0, tiled=True) if last else scatter_rows(grad_near_here)
    )
    return new_upstream, grad_rest, grad_near_here, ready


def two_terms(value):
    upper = value.astype(BF)
    return jnp.concatenate([upper, (value - upper.astype(F32)).astype(BF)], 1)


def orthogonal_blocks(sends, small):
    x, z, y = dp_place()
    groups = [[i + y_place for i in range(0, 32, 4)] for y_place in range(4)]
    rows = lax.all_to_all(sends, "dp", 0, 0, tiled=True, axis_index_groups=groups).reshape(192, D)
    shared = small[:, :10]
    shared = shared + tensor_swap(shared, 1)
    shared = shared + tensor_swap(shared, 2)
    pieces = swap_four([jnp.stack([rows, tensor_swap(rows, 2)])] * 4, 1)
    pieces[1], shared = lax.optimization_barrier((pieces[1], shared))
    pieces = pieces + [tensor_swap(piece, 1) for piece in pieces]
    small = two_terms(jnp.concatenate([shared, small[:, 10:]], 1))
    small = jnp.pad(small, ((0, 0), (0, 4)))
    result = newton_schulz(jnp.stack([x, y]).astype(jnp.int32), pieces, small)
    return lax.all_to_all(result.reshape(32, CHUNK, 224), "dp", 0, 0, tiled=True)


def per_device(
    x_in, segments, attn_w, mlp_w, in_bias, vectors, mom_attn, mom_mlp, mom_bias, mom_vec, cotangent
):
    cosine, sine, start = rope_tables(segments[0])
    me = lax.axis_index("tensor").astype(jnp.int32).reshape(1)
    common = (me, cosine, sine, start, jnp.asarray(turn_matrix(), BF))
    shards = pack(attn_w, mlp_w)
    arrived = gather_by_rings(shards[0])
    later = spread_rows(shards[1], dp_swap(shards[1], 16))
    stream = x_in[0].astype(F32)
    upstream = cotangent[0]
    norms, _ = normalized(stream, vectors[0])
    arrived, later, norms, common = lax.optimization_barrier((arrived, later, norms, common))
    weights = [arrived]
    arrived = gather_rows(later)
    record, stream = forward_layer(stream, norms, weights[0], in_bias[0], vectors[0], common)
    saved = [norms + record]
    stream, arrived = lax.optimization_barrier((stream, arrived))
    norms, last = normalized(stream, vectors[1], in_order(arrived))
    weights.append(last)
    record, stream = forward_layer(stream, norms, weights[1], in_bias[1], vectors[1], common)
    saved.append(norms + record)
    rests, nears = [None, None], [None, None]
    outer, _ = gather_tokens(upstream.astype(BF))
    upstream, rests[1], nears[1], stream = backward_layer(
        upstream, outer, saved[1], weights[1], vectors[1], common, stream, False
    )
    outer, _ = gather_tokens(upstream.astype(BF))
    upstream, rests[0], nears[0], nears[1] = backward_layer(
        upstream, outer, saved[0], weights[0], vectors[0], common, nears[1], True
    )
    rests, last_near = [add_arrived(rest) for rest in rests], add_arrived(nears[1])
    new_mom_attn, new_mom_mlp, sends, small = momenta(mom_attn, mom_mlp, rests[0], rests[1], last_near, nears[0])
    result = orthogonal_blocks(sends, small)
    new_attn_w, new_mlp_w, small = new_weights(result, attn_w, mlp_w)
    vec_total = small[:, :10].T.reshape(2, 5, D)
    vec_total = jnp.concatenate([vec_total, vec_total[:, 4:]], 1)
    bias_total = small[:, 10:].T.reshape(2, 2 * D)[:, :1344].reshape(2, 7, COLS)
    new_mom_bias = MOMENTUM * mom_bias + bias_total
    new_mom_vec = MOMENTUM * mom_vec + vec_total
    vec_rate = RATE_VEC / math.sqrt(32768)
    return (
        stream[None],
        upstream[None],
        new_mom_attn,
        new_attn_w,
        new_mom_mlp,
        new_mlp_w,
        new_mom_bias,
        in_bias - vec_rate * new_mom_bias,
        new_mom_vec,
        vectors - vec_rate * new_mom_vec,
    )


def solution(mesh):
    placed = (
        P("dp", "tensor", None),
        P("dp", None),
        P(None, None, "dp", "tensor"),
        P(None, None, "dp", None, "tensor"),
        P(None, None, "tensor"),
        P(),
        P(None, None, "dp", "tensor"),
        P(None, None, "dp", None, "tensor"),
        P(None, None, "tensor"),
        P(),
        P("dp", "tensor", None),
    )
    return jax.shard_map(
        per_device,
        mesh=mesh,
        in_specs=placed,
        out_specs=(
            P("dp", "tensor", None),
            P("dp", "tensor", None),
            P(None, None, "dp", "tensor"),
            P(None, None, "dp", "tensor"),
            P(None, None, "dp", None, "tensor"),
            P(None, None, "dp", None, "tensor"),
            P(None, None, "tensor"),
            P(None, None, "tensor"),
            P(),
            P(),
        ),
        check_vma=False,
    )
```

time: 580 us -> 461 us (0.79)
  Pallas kernels: 0 us -> 169 us
  matrix products: 160 us -> 0 us
  local copies, waits for them, and re-layouts: 88.3 us -> 20.7 us
  waiting for transfers between devices: 136 us -> 77.8 us
  other arithmetic: 85.2 us -> 40.1 us
  starting transfers between devices: 97.1 us -> 133 us
  blocking collectives: 0 us -> 10.4 us
    pallas_call x0 -> x17, Pallas kernels: none -> 169 us  [the longest x11 121 us: call(): pl.pallas_call(kernel, out_shape=[jax.ShapeDtypeStruct(s, d) for s, d in...]
    dot_general x62 -> x0, matrix products: 160 us -> none  [the longest x44 108 us: mm(): return jnp.einsum(spec, left, right, preferred_element_type=F32)]
    ppermute x24 -> x29, starting transfers between devices: 28.8 us -> 70.6 us  [tensor_swap(): return lax.ppermute(value, 'tensor', [(i, i ^ mask) for i in range(4)])]
    all_to_all x9 -> x6, waiting for transfers between devices: 59.8 us -> 18.3 us  [the longest x3 10.8 us: scatter_rows(): lax.all_to_all(partial, 'dp', 0, 0, tiled=True, axis_index_groups=PLANE)]
    all_to_all x9 -> x6, starting transfers between devices: 64.6 us -> 35.8 us  [the longest x3 22 us: scatter_rows(): lax.all_to_all(partial, 'dp', 0, 0, tiled=True, axis_index_groups=PLANE)]
    ppermute x3 -> x22, starting transfers between devices: 3.72 us -> 27 us  [dp_swap(): return lax.ppermute(value, 'dp', [(i, i ^ mask) for i in range(32)])]
    reduce_sum x14 -> x3, other arithmetic: 25.7 us -> 3.99 us  [add_arrived(): sums = jnp.sum(arrived.astype(F32), 0)]
    slice x36 -> x5, local copies, waits for them, and re-layouts: 18 us -> 0.13 us  [the longest x1 0.07 us: orthogonal_blocks(): small = two_terms(jnp.concatenate([shared, small[:, 10:]], 1))]
  transfers between devices with their start and end apart: 36 -> 57, of which waited for: 20 -> 23; matrix products, arithmetic and copies ran while one was open for 34% -> 10% of each run, Pallas kernels for 0% -> 26%
where the time goes in v2:
time: 461 us; the launch traced here: 453 us
  Pallas kernels  169 us (37%)
  starting transfers between devices  133 us (29%)
  waiting for transfers between devices  77.8 us (17%)
  other arithmetic  40.1 us (9%)
  local copies, waits for them, and re-layouts  20.7 us (4%)
  blocking collectives  10.4 us (2%)
    pallas_call x11, Pallas kernels, call(): pl.pallas_call(kernel, out_shape=[jax.ShapeDtypeStruct(s, d) for s, d in...  121 us
    ppermute x29, starting transfers between devices, tensor_swap(): return lax.ppermute(value, 'tensor', [(i, i ^ mask) for i in range(4)])  70.6 us
    ppermute x29, waiting for transfers between devices, tensor_swap(): return lax.ppermute(value, 'tensor', [(i, i ^ mask) for i in range(4)])  37 us
    ppermute x22, starting transfers between devices, dp_swap(): return lax.ppermute(value, 'dp', [(i, i ^ mask) for i in range(32)])  27 us
    pallas_call x2, Pallas kernels, backward_rest(): pl.pallas_call(backward_rest_kernel, grid=(4,), out_shape=[jax.ShapeDtype...  26.3 us
    ppermute x22, waiting for transfers between devices, dp_swap(): return lax.ppermute(value, 'dp', [(i, i ^ mask) for i in range(32)])  22.5 us
    all_to_all x3, starting transfers between devices, scatter_rows(): lax.all_to_all(partial, 'dp', 0, 0, tiled=True, axis_index_groups=PLANE)  22 us
    pallas_call x4, Pallas kernels, forward_out(): pl.pallas_call(forward_out_kernel, grid=(1,), out_shape=[jax.ShapeDtypeSt...  21.1 us
  transfers between devices with their start and end apart: 57, of which 23 were waited for; matrix products, arithmetic and copies ran while one was open for 10% of the time, Pallas kernels for 26%

profile of v2, /device:TPU:1, one launch (start us, length us, event | category | flops | bytes accessed | tf_op | source)
XLA Modules:
  0.0 452.8 jit_solution(15854585487263900624)
XLA Ops:
  7.4 3.3 collective-permute-start.4
  20.5 2.6 collective-permute-start.12
  24.7 2.7 collective-permute-start.13
  30.0 3.0 collective-permute-start.15
  33.1 4.1 collective-permute-start.21
  50.6 4.0 shard_map.196
  56.6 4.9 %all-to-all-start = ((bf16[16,2,24,2304]{3,2,1,0:T(8,128)(2,1)}), bf16[16,2,24,2304]{3,2,1,0:T(8,128)(2,1)}, u32[]{:S(2)}, u32[]{:S(2)}) async-start(bf16[16,2,24,2304]{3,2,1,0:T(8,128)(2,1)} %concatenate.12), calls=%async_computation | async-start | bytes 7077888 | tf_op jit(solution)/shard_map/all_to_all | solution.py:593
  62.1 10.2 %shard_map.197 = (bf16[1024,192]{1,0:T(8,128)(2,1)}, bf16[1024,192]{1,0:T(8,128)(2,1)}, bf16[1024,192]{1,0:T(8,128)(2,1)}, f32[8,1024]{1,0:T(8,128)}, bf16[1024,192]{1,0:T(8,128)(2,1)}) custom-call(s32[1]{0:T(128)} %bitcast.18.me_ref, bf16[256,768]{1,0:T(8,128)(2,1)} %get-tuple-element.103.first0_ref, bf16[256,768]{1,0:T(8,128)(2,1)} %get-tuple-element.104.first1_ref, ...), custom_call_target="tpu_custom_call" | custom-call | flops 10000000 | bytes 65536 | tf_op jit(solution)/shard_map/pallas_call | solution.py:49
  72.3 5.3 %shard_map.198 = (bf16[512,768]{1,0:T(8,128)(2,1)}, f32[512,768]{1,0:T(8,128)}, f32[256,768]{1,0:T(8,128)}, bf16[256,768]{1,0:T(8,128)(2,1)}) custom-call(bf16[256,768]{1,0:T(8,128)(2,1)} %get-tuple-element.113.keep_in_ref.refs_6_, bf16[256,768]{1,0:T(8,128)(2,1)} %get-tuple-element.114.send_in_ref.refs_7_, ...), custom_call_target="tpu_custom_call" | custom-call | flops 10000000 | bytes 65536 | tf_op jit(solution)/shard_map/pallas_call | solution.py:165
  77.6 4.8 %collective-permute-start.22 = (bf16[256,768]{1,0:T(8,128)(2,1)}, bf16[256,768]{1,0:T(8,128)(2,1)S(1)}, u32[]{:S(2)}, u32[]{:S(2)}) collective-permute-start(bf16[256,768]{1,0:T(8,128)(2,1)} %get-tuple-element.116), channel_id=1, source_target_pairs={{0,1},{1,0},{2,3},{3,2},{4,5},{5,4},{6,7},{7,6},{8,9},{9,8},{10,11... | collective-permute-start | bytes 1179656 | tf_op jit(solution)/shard_map/ppermute | solution.py:568
  85.2 5.3 %shard_map.199 = (bf16[512,768]{1,0:T(8,128)(2,1)}, f32[512,768]{1,0:T(8,128)}, f32[256,768]{1,0:T(8,128)}, bf16[256,768]{1,0:T(8,128)(2,1)}) custom-call(bf16[256,768]{1,0:T(8,128)(2,1)} %get-tuple-element.100.keep_in_ref.refs_4_, bf16[256,768]{1,0:T(8,128)(2,1)} %get-tuple-element.101.send_in_ref.refs_5_, ...), custom_call_target="tpu_custom_call" | custom-call | flops 10000000 | bytes 65536 | tf_op jit(solution)/shard_map/pallas_call | solution.py:165
  92.4 10.5 %collective-permute-done.24 = bf16[256,768]{1,0:T(8,128)(2,1)S(1)} collective-permute-done((bf16[256,768]{1,0:T(8,128)(2,1)S(1)}, bf16[256,768]{1,0:T(8,128)(2,1)S(1)}, u32[]{:S(2)}, u32[]{:S(2)}) %collective-permute-start.24) | collective-permute-done | bytes 393248 | tf_op jit(solution)/shard_map/ppermute | solution.py:568
  108.8 6.4 %collective-permute-start.25 = (f16[256,768]{1,0:T(8,128)(2,1)S(1)}, f16[256,768]{1,0:T(8,128)(2,1)S(1)}, u32[]{:S(2)}, u32[]{:S(2)}) collective-permute-start(f16[256,768]{1,0:T(8,128)(2,1)S(1)} %get-tuple-element.243), channel_id=1, source_target_pairs={{0,1},{1,0},{2,3},{3,2},{4,5},{5,4},{6,7},{7,6},{8,9},{9,8},{10,11... | collective-permute-start | bytes 1179656 | tf_op jit(solution)/shard_map/ppermute | solution.py:568
  115.2 4.0 copy.56
  119.1 3.8 collective-permute-start.27
  123.6 3.9 collective-permute-start.2
  129.5 10.1 %shard_map.200 = (bf16[1024,192]{1,0:T(8,128)(2,1)}, bf16[1024,192]{1,0:T(8,128)(2,1)}, bf16[1024,192]{1,0:T(8,128)(2,1)}, f32[8,1024]{1,0:T(8,128)}, bf16[1024,192]{1,0:T(8,128)(2,1)}) custom-call(s32[1]{0:T(128)} %bitcast.18.me_ref, bf16[256,768]{1,0:T(8,128)(2,1)} %get-tuple-element.242.first0_ref, bf16[256,768]{1,0:T(8,128)(2,1)} %get-tuple-element.251.first1_ref, ...), custom_call_target="tpu_custom_call" | custom-call | flops 10000000 | bytes 65536 | tf_op jit(solution)/shard_map/pallas_call | solution.py:49
  139.6 5.3 %shard_map.201 = (bf16[512,768]{1,0:T(8,128)(2,1)}, f32[512,768]{1,0:T(8,128)}, f32[256,768]{1,0:T(8,128)}, bf16[256,768]{1,0:T(8,128)(2,1)}) custom-call(bf16[256,768]{1,0:T(8,128)(2,1)} %get-tuple-element.276.keep_in_ref.refs_6_, bf16[256,768]{1,0:T(8,128)(2,1)} %get-tuple-element.274.send_in_ref.refs_7_, ...), custom_call_target="tpu_custom_call" | custom-call | flops 10000000 | bytes 65536 | tf_op jit(solution)/shard_map/pallas_call | solution.py:165
  147.7 5.3 %shard_map.202 = (bf16[512,768]{1,0:T(8,128)(2,1)}, f32[512,768]{1,0:T(8,128)}, f32[256,768]{1,0:T(8,128)}, bf16[256,768]{1,0:T(8,128)(2,1)}) custom-call(bf16[256,768]{1,0:T(8,128)(2,1)} %get-tuple-element.280.keep_in_ref.refs_4_, bf16[256,768]{1,0:T(8,128)(2,1)} %get-tuple-element.252.send_in_ref.refs_5_, ...), custom_call_target="tpu_custom_call" | custom-call | flops 10000000 | bytes 65536 | tf_op jit(solution)/shard_map/pallas_call | solution.py:165
  157.2 13.2 %shard_map.203 = (bf16[16,2,24,1728]{3,2,1,0:T(8,128)(2,1)}, bf16[1024,192]{1,0:T(8,128)(2,1)}, f32[1024,768]{1,0:T(8,128)}, f32[8,768]{1,0:T(8,128)}) custom-call(bf16[256,768]{1,0:T(8,128)(2,1)} %copy-done.10, bf16[256,768]{1,0:T(8,128)(2,1)} %copy-done.27, bf16[256,768]{1,0:T(8,128)(2,1)} %copy-done.26, bf16[256,768]{1,0:T(8,128)(2,1)} %copy-done.28, ...), custom_call_target="tpu_custom_call" | custom-call | flops 10000000 | bytes 65536 | tf_op jit(solution)/shard_map/pallas_call | solution.py:229
  170.4 8.4 %all-to-all-start.1 = ((bf16[16,2,24,1728]{3,2,1,0:T(8,128)(2,1)}), bf16[16,2,24,1728]{3,2,1,0:T(8,128)(2,1)S(1)}, u32[]{:S(2)}, u32[]{:S(2)}) async-start(bf16[16,2,24,1728]{3,2,1,0:T(8,128)(2,1)} %get-tuple-element.165), calls=%async_computation.1 | async-start | bytes 5505024 | tf_op jit(solution)/shard_map/all_to_all | solution.py:612
  181.2 18.2 %shard_map.204 = (bf16[1024,576]{1,0:T(8,128)(2,1)}, f32[2,256,768]{2,1,0:T(8,128)}, bf16[2,256,768]{2,1,0:T(8,128)(2,1)}, f32[8,768]{1,0:T(8,128)}, f32[8,576]{1,0:T(8,128)}) custom-call(s32[1]{0:T(128)} %bitcast.18.me_ref, bf16[1024,192]{1,0:T(8,128)(2,1)} %get-tuple-element.139.q_ref, bf16[1024,192]{1,0:T(8,128)(2,1)} %get-tuple-element.140.k_ref, ...), custom_call_target="tpu_custom_call" | custom-call | flops 10000000 | bytes 65536 | tf_op jit(solution)/shard_map/pallas_call | solution.py:49
  207.5 4.6 %shard_map.206 = bf16[16,2,24,592]{3,2,1,0:T(8,128)(2,1)} custom-call(bf16[256,768]{1,0:T(8,128)(2,1)} %get-tuple-element.242.first0_ref, bf16[256,768]{1,0:T(8,128)(2,1)} %get-tuple-element.251.first1_ref, bf16[256,768]{1,0:T(8,128)(2,1)} %get-tuple-element.277.first2_ref, bf16[256,768]{1,0:T(8,128)(2,1)} %get-tuple-element.275.first3_ref, ...), custom_call_target="tpu_custom_call" | custom-call | flops 10000000 | bytes 65536 | tf_op jit(solution)/shard_map/pallas_call | solution.py:49
  212.1 5.9 %collective-permute-done.32 = bf16[256,768]{1,0:T(8,128)(2,1)S(1)} collective-permute-done((bf16[256,768]{1,0:T(8,128)(2,1)}, bf16[256,768]{1,0:T(8,128)(2,1)S(1)}, u32[]{:S(2)}, u32[]{:S(2)}) %collective-permute-start.32) | collective-permute-done | bytes 393248 | tf_op jit(solution)/shard_map/ppermute | solution.py:568
  220.2 7.0 %all-to-all-start.2 = ((bf16[16,2,24,592]{3,2,1,0:T(8,128)(2,1)}), bf16[16,2,24,592]{3,2,1,0:T(8,128)(2,1)}, u32[]{:S(2)}, u32[]{:S(2)}) async-start(bf16[16,2,24,592]{3,2,1,0:T(8,128)(2,1)} %shard_map.206), calls=%async_computation.2 | async-start | bytes 1966080 | tf_op jit(solution)/shard_map/all_to_all | solution.py:612
  227.2 2.8 fusion.56
  233.2 7.5 %collective-permute-done.34.refs_2_ = bf16[256,768]{1,0:T(8,128)(2,1)S(1)} collective-permute-done((bf16[256,768]{1,0:T(8,128)(2,1)S(1)}, bf16[256,768]{1,0:T(8,128)(2,1)S(1)}, u32[]{:S(2)}, u32[]{:S(2)}) %collective-permute-start.34) | collective-permute-done | bytes 393248 | tf_op jit(solution)/shard_map/ppermute | solution.py:568
  245.1 13.2 %shard_map.205 = (bf16[16,2,24,1728]{3,2,1,0:T(8,128)(2,1)}, bf16[1024,192]{1,0:T(8,128)(2,1)}, f32[1024,768]{1,0:T(8,128)}, f32[8,768]{1,0:T(8,128)}) custom-call(bf16[256,768]{1,0:T(8,128)(2,1)} %copy-done.9, bf16[256,768]{1,0:T(8,128)(2,1)} %copy-done.30, bf16[256,768]{1,0:T(8,128)(2,1)} %copy-done.29, bf16[256,768]{1,0:T(8,128)(2,1)} %copy-done.31, ...), custom_call_target="tpu_custom_call" | custom-call | flops 10000000 | bytes 65536 | tf_op jit(solution)/shard_map/pallas_call | solution.py:229
  258.3 6.7 %all-to-all-start.3 = ((bf16[16,2,24,1728]{3,2,1,0:T(8,128)(2,1)}), bf16[16,2,24,1728]{3,2,1,0:T(8,128)(2,1)}, u32[]{:S(2)}, u32[]{:S(2)}) async-start(bf16[16,2,24,1728]{3,2,1,0:T(8,128)(2,1)} %get-tuple-element.176), calls=%async_computation.3 | async-start | bytes 5505024 | tf_op jit(solution)/shard_map/all_to_all | solution.py:612
  265.6 3.2 collective-permute-done.39
  271.2 17.9 %shard_map.207 = (bf16[1024,576]{1,0:T(8,128)(2,1)}, f32[2,256,768]{2,1,0:T(8,128)}, bf16[2,256,768]{2,1,0:T(8,128)(2,1)}, f32[8,768]{1,0:T(8,128)}, f32[8,576]{1,0:T(8,128)}) custom-call(s32[1]{0:T(128)} %bitcast.18.me_ref, bf16[1024,192]{1,0:T(8,128)(2,1)} %get-tuple-element.148.q_ref, bf16[1024,192]{1,0:T(8,128)(2,1)} %get-tuple-element.149.k_ref, ...), custom_call_target="tpu_custom_call" | custom-call | flops 10000000 | bytes 65536 | tf_op jit(solution)/shard_map/pallas_call | solution.py:49
  291.2 4.7 %shard_map.208 = bf16[32,24,592]{2,1,0:T(8,128)(2,1)} custom-call(bf16[256,768]{1,0:T(8,128)(2,1)} %get-tuple-element.103.first0_ref, bf16[256,768]{1,0:T(8,128)(2,1)} %get-tuple-element.104.first1_ref, bf16[256,768]{1,0:T(8,128)(2,1)} %get-tuple-element.105.first2_ref, bf16[256,768]{1,0:T(8,128)(2,1)} %get-tuple-element.106.first3_ref, ...), custom_call_target="tpu_custom_call" | custom-call | flops 10000000 | bytes 65536 | tf_op jit(solution)/shard_map/pallas_call | solution.py:49
  295.9 10.8 %all-to-all-done.3 = bf16[16,2,24,1728]{3,2,1,0:T(8,128)(2,1)} async-done(((bf16[16,2,24,1728]{3,2,1,0:T(8,128)(2,1)}), bf16[16,2,24,1728]{3,2,1,0:T(8,128)(2,1)}, u32[]{:S(2)}, u32[]{:S(2)}) %all-to-all-start.3) | async-done | bytes 2654240 | tf_op jit(solution)/shard_map/all_to_all | solution.py:612
  308.9 4.3 all-to-all-start.4
  315.2 10.7 %collective-permute-done.38 = bf16[24,1728]{1,0:T(8,128)(2,1)S(1)} collective-permute-done((bf16[24,1728]{1,0:T(8,128)(2,1)S(1)}, bf16[24,1728]{1,0:T(8,128)(2,1)S(1)}, u32[]{:S(2)}, u32[]{:S(2)}) %collective-permute-start.38) | collective-permute-done | bytes 82976 | tf_op jit(solution)/shard_map/ppermute | solution.py:564
  327.7 3.2 shard_map.209
  331.0 10.4 %all_to_all.35 = bf16[8,24,768]{2,1,0:T(8,128)(2,1)S(1)} all-to-all(bf16[8,24,768]{2,1,0:T(8,128)(2,1)} %get-tuple-element.182), channel_id=1, replica_groups={{0,16,32,48,64,80,96,112},{4,20,36,52,68,84,100,116},{8,24,40,56,72,88,..., dimensions={0} | all-to-all | bytes 589824 | tf_op jit(solution)/shard_map/all_to_all | solution.py:716
  341.4 3.4 collective-permute-start.41
  346.1 2.8 collective-permute-done.41
  353.0 3.0 collective-permute-start.37
  356.0 8.8 %collective-permute-start.43 = (f32[24,10]{1,0:T(8,128)S(1)}, f32[24,10]{1,0:T(8,128)S(1)}, u32[]{:S(2)}, u32[]{:S(2)}) collective-permute-start(f32[24,10]{1,0:T(8,128)S(1)} %bitcast.141), channel_id=1, source_target_pairs={{0,1},{1,0},{2,3},{3,2},{4,5},{5,4},{6,7},{7,6},{8,9},{9,8},{10,11... | collective-permute-start | bytes 2888 | tf_op jit(solution)/shard_map/ppermute | solution.py:568
  366.3 4.0 collective-permute-done.44
  372.1 7.5 %collective-permute-start.49 = (bf16[2,192,768]{2,1,0:T(8,128)(2,1)S(1)}, bf16[2,192,768]{2,1,0:T(8,128)(2,1)S(1)}, u32[]{:S(2)}, u32[]{:S(2)}) collective-permute-start(bf16[2,192,768]{2,1,0:T(8,128)(2,1)S(1)} %collective-permute-done.45.p2), channel_id=1, source_target_pairs={{0,1},{1,0},{2,3},{3,2},{4,5},{5,4},{6,7},{7,6},{8,9},{9,8},{10,11... | collective-permute-start | bytes 1769480 | tf_op jit(solution)/shard_map/ppermute | solution.py:568
  379.6 2.8 collective-permute-start.50
  386.6 43.2 %shard_map.210 = bf16[8,4,24,224]{3,2,1,0:T(8,128)(2,1)} custom-call(s32[2]{0:T(128)} %pad_add_fusion.1.place_ref, bf16[2,192,768]{2,1,0:T(8,128)(2,1)} %copy-done.6, bf16[2,192,768]{2,1,0:T(8,128)(2,1)} %copy-done.20, bf16[2,192,768]{2,1,0:T(8,128)(2,1)} %copy-done.21, bf16[2,192,768]{2,1,0:T(8,128)(2,1)} %copy-done.22, bf16[2,192,768]{2,1,0:T(8,128)(2,1)} %copy-done.23, ...), custom_call_target="tpu_custom_call" | custom-call | flops 10000000 | bytes 65536 | tf_op jit(solution)/shard_map/pallas_call | solution.py:49
  429.7 4.6 %all-to-all-start.6 = ((bf16[32,24,224]{2,1,0:T(8,128)(2,1)}), bf16[32,24,224]{2,1,0:T(8,128)(2,1)}, u32[]{:S(2)}, u32[]{:S(2)}) async-start(bf16[32,24,224]{2,1,0:T(8,128)(2,1)} %bitcast.121), calls=%async_computation.6 | async-start | bytes 786432 | tf_op jit(solution)/shard_map/all_to_all | solution.py:726
  436.8 7.4 %all-to-all-done.6.back_ref = bf16[32,24,224]{2,1,0:T(8,128)(2,1)} async-done(((bf16[32,24,224]{2,1,0:T(8,128)(2,1)}), bf16[32,24,224]{2,1,0:T(8,128)(2,1)}, u32[]{:S(2)}, u32[]{:S(2)}) %all-to-all-start.6) | async-done | bytes 344096 | tf_op jit(solution)/shard_map/all_to_all | solution.py:726
  444.2 3.0 shard_map.211
  (276 shorter events, 108.3 us)
Async XLA Ops:
  3.6 15.5 %collective-permute-start.10 = (bf16[24,2304]{1,0:T(8,128)(2,1)S(1)}, bf16[24,2304]{1,0:T(8,128)(2,1)S(1)}, u32[]{:S(2)}, u32[]{:S(2)}) collective-permute-start(bf16[24,2304]{1,0:T(8,128)(2,1)S(1)} %get-tuple-element.264), channel_id=1, source_target_pairs={{0,64},{4,68},{8,72},{12,76},{16,80},{20,84},{24,88},{28,92},{32,9... | collective-permute-start | bytes 331784 | tf_op jit(solution)/shard_map/ppermute | solution.py:564
  5.7 11.4 %collective-permute-start.3 = (bf16[24,2304]{1,0:T(8,128)(2,1)S(1)}, bf16[24,2304]{1,0:T(8,128)(2,1)S(1)}, u32[]{:S(2)}, u32[]{:S(2)}) collective-permute-start(bf16[24,2304]{1,0:T(8,128)(2,1)S(1)} %get-tuple-element.264), channel_id=1, source_target_pairs={{0,16},{4,20},{8,24},{12,28},{16,0},{20,4},{24,8},{28,12},{32,48},... | collective-permute-start | bytes 331784 | tf_op jit(solution)/shard_map/ppermute | solution.py:564
  7.4 11.6 %collective-permute-start.4 = (bf16[24,2304]{1,0:T(8,128)(2,1)S(1)}, bf16[24,2304]{1,0:T(8,128)(2,1)S(1)}, u32[]{:S(2)}, u32[]{:S(2)}) collective-permute-start(bf16[24,2304]{1,0:T(8,128)(2,1)S(1)} %get-tuple-element.264), channel_id=1, source_target_pairs={{0,32},{4,36},{8,40},{12,44},{16,48},{20,52},{24,56},{28,60},{32,0... | collective-permute-start | bytes 331784 | tf_op jit(solution)/shard_map/ppermute | solution.py:564
  10.7 8.3 %collective-permute-start.5 = (bf16[24,2304]{1,0:T(8,128)(2,1)S(1)}, bf16[24,2304]{1,0:T(8,128)(2,1)S(1)}, u32[]{:S(2)}, u32[]{:S(2)}) collective-permute-start(bf16[24,2304]{1,0:T(8,128)(2,1)S(1)} %get-tuple-element.264), channel_id=1, source_target_pairs={{0,48},{4,52},{8,56},{12,60},{16,32},{20,36},{24,40},{28,44},{32,1... | collective-permute-start | bytes 331784 | tf_op jit(solution)/shard_map/ppermute | solution.py:564
  12.4 20.7 %collective-permute-start.20 = (f16[256,768]{1,0:T(8,128)(2,1)S(1)}, f16[256,768]{1,0:T(8,128)(2,1)S(1)}, u32[]{:S(2)}, u32[]{:S(2)}) collective-permute-start(f16[256,768]{1,0:T(8,128)(2,1)S(1)} %get-tuple-element.245), channel_id=1, source_target_pairs={{0,2},{1,3},{2,0},{3,1},{4,6},{5,7},{6,4},{7,5},{8,10},{9,11},{10,... | collective-permute-start | bytes 1179656 | tf_op jit(solution)/shard_map/ppermute | solution.py:568
  17.2 15.9 %collective-permute-start.19 = (f16[256,768]{1,0:T(8,128)(2,1)S(1)}, f16[256,768]{1,0:T(8,128)(2,1)S(1)}, u32[]{:S(2)}, u32[]{:S(2)}) collective-permute-start(f16[256,768]{1,0:T(8,128)(2,1)S(1)} %get-tuple-element.245), channel_id=1, source_target_pairs={{0,1},{1,0},{2,3},{3,2},{4,5},{5,4},{6,7},{7,6},{8,9},{9,8},{10,11... | collective-permute-start | bytes 1179656 | tf_op jit(solution)/shard_map/ppermute | solution.py:568
  19.1 9.1 %collective-permute-start.11 = (bf16[24,2304]{1,0:T(8,128)(2,1)S(1)}, bf16[24,2304]{1,0:T(8,128)(2,1)S(1)}, u32[]{:S(2)}, u32[]{:S(2)}) collective-permute-start(bf16[24,2304]{1,0:T(8,128)(2,1)S(1)} %collective-permute-done.10), channel_id=1, source_target_pairs={{0,4},{4,0},{8,12},{12,8},{16,20},{20,16},{24,28},{28,24},{32,36},... | collective-permute-start | bytes 331784 | tf_op jit(solution)/shard_map/ppermute | solution.py:564
  20.5 7.9 %collective-permute-start.12 = (bf16[24,2304]{1,0:T(8,128)(2,1)S(1)}, bf16[24,2304]{1,0:T(8,128)(2,1)S(1)}, u32[]{:S(2)}, u32[]{:S(2)}) collective-permute-start(bf16[24,2304]{1,0:T(8,128)(2,1)S(1)} %collective-permute-done.10), channel_id=1, source_target_pairs={{0,8},{4,12},{8,0},{12,4},{16,24},{20,28},{24,16},{28,20},{32,40},... | collective-permute-start | bytes 331784 | tf_op jit(solution)/shard_map/ppermute | solution.py:564
  28.2 11.3 %collective-permute-start.7 = (bf16[4,24,2304]{2,1,0:T(8,128)(2,1)S(1)}, bf16[4,24,2304]{2,1,0:T(8,128)(2,1)S(1)}, u32[]{:S(2)}, u32[]{:S(2)}) collective-permute-start(bf16[4,24,2304]{2,1,0:T(8,128)(2,1)S(1)} %pad_maximum_fusion.1.a0), channel_id=1, source_target_pairs={{0,12},{4,8},{8,4},{12,0},{16,28},{20,24},{24,20},{28,16},{32,44},... | collective-permute-start | bytes 1327112 | tf_op jit(solution)/shard_map/ppermute | solution.py:564
  28.4 11.3 %collective-permute-start.6 = (bf16[4,24,2304]{2,1,0:T(8,128)(2,1)S(1)}, bf16[4,24,2304]{2,1,0:T(8,128)(2,1)S(1)}, u32[]{:S(2)}, u32[]{:S(2)}) collective-permute-start(bf16[4,24,2304]{2,1,0:T(8,128)(2,1)S(1)} %pad_maximum_fusion.1.a0), channel_id=1, source_target_pairs={{0,4},{4,0},{8,12},{12,8},{16,20},{20,16},{24,28},{28,24},{32,36},... | collective-permute-start | bytes 1327112 | tf_op jit(solution)/shard_map/ppermute | solution.py:564
  30.0 12.2 %collective-permute-start.15 = (bf16[4,24,2304]{2,1,0:T(8,128)(2,1)S(1)}, bf16[4,24,2304]{2,1,0:T(8,128)(2,1)S(1)}, u32[]{:S(2)}, u32[]{:S(2)}) collective-permute-start(bf16[4,24,2304]{2,1,0:T(8,128)(2,1)S(1)} %pad_maximum_fusion.2.b0), channel_id=1, source_target_pairs={{0,48},{4,52},{8,56},{12,60},{16,32},{20,36},{24,40},{28,44},{32,1... | collective-permute-start | bytes 1327112 | tf_op jit(solution)/shard_map/ppermute | solution.py:564
  33.1 10.9 %collective-permute-start.14 = (bf16[4,24,2304]{2,1,0:T(8,128)(2,1)S(1)}, bf16[4,24,2304]{2,1,0:T(8,128)(2,1)S(1)}, u32[]{:S(2)}, u32[]{:S(2)}) collective-permute-start(bf16[4,24,2304]{2,1,0:T(8,128)(2,1)S(1)} %pad_maximum_fusion.2.b0), channel_id=1, source_target_pairs={{0,16},{4,20},{8,24},{12,28},{16,0},{20,4},{24,8},{28,12},{32,48},... | collective-permute-start | bytes 1327112 | tf_op jit(solution)/shard_map/ppermute | solution.py:564
  33.1 11.0 %collective-permute-start.21 = (f16[256,768]{1,0:T(8,128)(2,1)S(1)}, f16[256,768]{1,0:T(8,128)(2,1)S(1)}, u32[]{:S(2)}, u32[]{:S(2)}) collective-permute-start(f16[256,768]{1,0:T(8,128)(2,1)S(1)} %collective-permute-done.20), channel_id=1, source_target_pairs={{0,1},{1,0},{2,3},{3,2},{4,5},{5,4},{6,7},{7,6},{8,9},{9,8},{10,11... | collective-permute-start | bytes 1179656 | tf_op jit(solution)/shard_map/ppermute | solution.py:568
  39.6 7.5 %collective-permute-start.8 = (bf16[2,24,2304]{2,1,0:T(8,128)(2,1)S(1)}, bf16[2,24,2304]{2,1,0:T(8,128)(2,1)}, u32[]{:S(2)}, u32[]{:S(2)}) collective-permute-start(bf16[2,24,2304]{2,1,0:T(8,128)(2,1)S(1)} %slice.214), channel_id=1, source_target_pairs={{0,4},{4,0},{8,12},{12,8},{16,20},{20,16},{24,28},{28,24},{32,36},... | collective-permute-start | bytes 663560 | tf_op jit(solution)/shard_map/ppermute | solution.py:564
  39.7 7.3 %collective-permute-start.9 = (bf16[2,24,2304]{2,1,0:T(8,128)(2,1)S(1)}, bf16[2,24,2304]{2,1,0:T(8,128)(2,1)S(1)}, u32[]{:S(2)}, u32[]{:S(2)}) collective-permute-start(bf16[2,24,2304]{2,1,0:T(8,128)(2,1)S(1)} %slice.215), channel_id=1, source_target_pairs={{0,12},{4,8},{8,4},{12,0},{16,28},{20,24},{24,20},{28,16},{32,44},... | collective-permute-start | bytes 663560 | tf_op jit(solution)/shard_map/ppermute | solution.py:564
  44.0 6.6 %collective-permute-start.17 = (bf16[2,24,2304]{2,1,0:T(8,128)(2,1)S(1)}, bf16[2,24,2304]{2,1,0:T(8,128)(2,1)}, u32[]{:S(2)}, u32[]{:S(2)}) collective-permute-start(bf16[2,24,2304]{2,1,0:T(8,128)(2,1)S(1)} %slice.217), channel_id=1, source_target_pairs={{0,48},{4,52},{8,56},{12,60},{16,32},{20,36},{24,40},{28,44},{32,1... | collective-permute-start | bytes 663560 | tf_op jit(solution)/shard_map/ppermute | solution.py:564
  56.6 47.7 %all-to-all-start = ((bf16[16,2,24,2304]{3,2,1,0:T(8,128)(2,1)}), bf16[16,2,24,2304]{3,2,1,0:T(8,128)(2,1)}, u32[]{:S(2)}, u32[]{:S(2)}) async-start(bf16[16,2,24,2304]{3,2,1,0:T(8,128)(2,1)} %concatenate.12), calls=%async_computation | async-start | bytes 7077888 | tf_op jit(solution)/shard_map/all_to_all | solution.py:593
  77.6 6.4 %collective-permute-start.22 = (bf16[256,768]{1,0:T(8,128)(2,1)}, bf16[256,768]{1,0:T(8,128)(2,1)S(1)}, u32[]{:S(2)}, u32[]{:S(2)}) collective-permute-start(bf16[256,768]{1,0:T(8,128)(2,1)} %get-tuple-element.116), channel_id=1, source_target_pairs={{0,1},{1,0},{2,3},{3,2},{4,5},{5,4},{6,7},{7,6},{8,9},{9,8},{10,11... | collective-permute-start | bytes 1179656 | tf_op jit(solution)/shard_map/ppermute | solution.py:568
  90.8 12.1 %collective-permute-start.24 = (bf16[256,768]{1,0:T(8,128)(2,1)S(1)}, bf16[256,768]{1,0:T(8,128)(2,1)S(1)}, u32[]{:S(2)}, u32[]{:S(2)}) collective-permute-start(bf16[256,768]{1,0:T(8,128)(2,1)S(1)} %add_convert_fusion.1), channel_id=1, source_target_pairs={{0,2},{1,3},{2,0},{3,1},{4,6},{5,7},{6,4},{7,5},{8,10},{9,11},{10,... | collective-permute-start | bytes 1179656 | tf_op jit(solution)/shard_map/ppermute | solution.py:568
  105.7 13.5 %collective-permute-start.26 = (f16[256,768]{1,0:T(8,128)(2,1)S(1)}, f16[256,768]{1,0:T(8,128)(2,1)S(1)}, u32[]{:S(2)}, u32[]{:S(2)}) collective-permute-start(f16[256,768]{1,0:T(8,128)(2,1)S(1)} %get-tuple-element.243), channel_id=1, source_target_pairs={{0,2},{1,3},{2,0},{3,1},{4,6},{5,7},{6,4},{7,5},{8,10},{9,11},{10,... | collective-permute-start | bytes 1179656 | tf_op jit(solution)/shard_map/ppermute | solution.py:568
  107.2 16.4 %collective-permute-start.1 = (bf16[256,768]{1,0:T(8,128)(2,1)S(1)}, bf16[256,768]{1,0:T(8,128)(2,1)S(1)}, u32[]{:S(2)}, u32[]{:S(2)}) collective-permute-start(bf16[256,768]{1,0:T(8,128)(2,1)S(1)} %bitcast_convert_fusion.refs_0_), channel_id=1, source_target_pairs={{0,2},{1,3},{2,0},{3,1},{4,6},{5,7},{6,4},{7,5},{8,10},{9,11},{10,... | collective-permute-start | bytes 1179656 | tf_op jit(solution)/shard_map/ppermute | solution.py:568
  108.8 18.7 %collective-permute-start.25 = (f16[256,768]{1,0:T(8,128)(2,1)S(1)}, f16[256,768]{1,0:T(8,128)(2,1)S(1)}, u32[]{:S(2)}, u32[]{:S(2)}) collective-permute-start(f16[256,768]{1,0:T(8,128)(2,1)S(1)} %get-tuple-element.243), channel_id=1, source_target_pairs={{0,1},{1,0},{2,3},{3,2},{4,5},{5,4},{6,7},{7,6},{8,9},{9,8},{10,11... | collective-permute-start | bytes 1179656 | tf_op jit(solution)/shard_map/ppermute | solution.py:568
  119.1 8.4 %collective-permute-start.27 = (f16[256,768]{1,0:T(8,128)(2,1)S(1)}, f16[256,768]{1,0:T(8,128)(2,1)S(1)}, u32[]{:S(2)}, u32[]{:S(2)}) collective-permute-start(f16[256,768]{1,0:T(8,128)(2,1)S(1)} %collective-permute-done.26), channel_id=1, source_target_pairs={{0,1},{1,0},{2,3},{3,2},{4,5},{5,4},{6,7},{7,6},{8,9},{9,8},{10,11... | collective-permute-start | bytes 1179656 | tf_op jit(solution)/shard_map/ppermute | solution.py:568
  122.9 33.4 %collective-permute-start = (bf16[256,768]{1,0:T(8,128)(2,1)S(1)}, bf16[256,768]{1,0:T(8,128)(2,1)S(1)}, u32[]{:S(2)}, u32[]{:S(2)}) collective-permute-start(bf16[256,768]{1,0:T(8,128)(2,1)S(1)} %bitcast_convert_fusion.refs_0_), channel_id=1, source_target_pairs={{0,1},{1,0},{2,3},{3,2},{4,5},{5,4},{6,7},{7,6},{8,9},{9,8},{10,11... | collective-permute-start | bytes 1179656 | tf_op jit(solution)/shard_map/ppermute | solution.py:568
  123.6 32.8 %collective-permute-start.2 = (bf16[256,768]{1,0:T(8,128)(2,1)S(1)}, bf16[256,768]{1,0:T(8,128)(2,1)S(1)}, u32[]{:S(2)}, u32[]{:S(2)}) collective-permute-start(bf16[256,768]{1,0:T(8,128)(2,1)S(1)} %collective-permute-done.1.refs_2_), channel_id=1, source_target_pairs={{0,1},{1,0},{2,3},{3,2},{4,5},{5,4},{6,7},{7,6},{8,9},{9,8},{10,11... | collective-permute-start | bytes 1179656 | tf_op jit(solution)/shard_map/ppermute | solution.py:568
  153.0 25.8 %collective-permute-start.29 = (bf16[256,768]{1,0:T(8,128)(2,1)}, bf16[256,768]{1,0:T(8,128)(2,1)}, u32[]{:S(2)}, u32[]{:S(2)}) collective-permute-start(bf16[256,768]{1,0:T(8,128)(2,1)} %get-tuple-element.136), channel_id=1, source_target_pairs={{0,1},{1,0},{2,3},{3,2},{4,5},{5,4},{6,7},{7,6},{8,9},{9,8},{10,11... | collective-permute-start | bytes 1179656 | tf_op jit(solution)/shard_map/ppermute | solution.py:568
  153.2 25.6 %collective-permute-start.30 = (bf16[256,768]{1,0:T(8,128)(2,1)}, bf16[256,768]{1,0:T(8,128)(2,1)}, u32[]{:S(2)}, u32[]{:S(2)}) collective-permute-start(bf16[256,768]{1,0:T(8,128)(2,1)} %add_convert_fusion), channel_id=1, source_target_pairs={{0,2},{1,3},{2,0},{3,1},{4,6},{5,7},{6,4},{7,5},{8,10},{9,11},{10,... | collective-permute-start | bytes 1179656 | tf_op jit(solution)/shard_map/ppermute | solution.py:568
  170.4 49.8 %all-to-all-start.1 = ((bf16[16,2,24,1728]{3,2,1,0:T(8,128)(2,1)}), bf16[16,2,24,1728]{3,2,1,0:T(8,128)(2,1)S(1)}, u32[]{:S(2)}, u32[]{:S(2)}) async-start(bf16[16,2,24,1728]{3,2,1,0:T(8,128)(2,1)} %get-tuple-element.165), calls=%async_computation.1 | async-start | bytes 5505024 | tf_op jit(solution)/shard_map/all_to_all | solution.py:612
  206.0 12.0 %collective-permute-start.32 = (bf16[256,768]{1,0:T(8,128)(2,1)}, bf16[256,768]{1,0:T(8,128)(2,1)S(1)}, u32[]{:S(2)}, u32[]{:S(2)}) collective-permute-start(bf16[256,768]{1,0:T(8,128)(2,1)} %fusion.42), channel_id=1, source_target_pairs={{0,2},{1,3},{2,0},{3,1},{4,6},{5,7},{6,4},{7,5},{8,10},{9,11},{10,... | collective-permute-start | bytes 1179656 | tf_op jit(solution)/shard_map/ppermute | solution.py:568
  220.2 38.1 %all-to-all-start.2 = ((bf16[16,2,24,592]{3,2,1,0:T(8,128)(2,1)}), bf16[16,2,24,592]{3,2,1,0:T(8,128)(2,1)}, u32[]{:S(2)}, u32[]{:S(2)}) async-start(bf16[16,2,24,592]{3,2,1,0:T(8,128)(2,1)} %shard_map.206), calls=%async_computation.2 | async-start | bytes 1966080 | tf_op jit(solution)/shard_map/all_to_all | solution.py:612
  229.9 10.7 %collective-permute-start.34 = (bf16[256,768]{1,0:T(8,128)(2,1)S(1)}, bf16[256,768]{1,0:T(8,128)(2,1)S(1)}, u32[]{:S(2)}, u32[]{:S(2)}) collective-permute-start(bf16[256,768]{1,0:T(8,128)(2,1)S(1)} %get-tuple-element.240.refs_0_), channel_id=1, source_target_pairs={{0,2},{1,3},{2,0},{3,1},{4,6},{5,7},{6,4},{7,5},{8,10},{9,11},{10,... | collective-permute-start | bytes 1179656 | tf_op jit(solution)/shard_map/ppermute | solution.py:568
  231.4 11.6 %collective-permute-start.33 = (bf16[256,768]{1,0:T(8,128)(2,1)S(1)}, bf16[256,768]{1,0:T(8,128)(2,1)S(1)}, u32[]{:S(2)}, u32[]{:S(2)}) collective-permute-start(bf16[256,768]{1,0:T(8,128)(2,1)S(1)} %get-tuple-element.240.refs_0_), channel_id=1, source_target_pairs={{0,1},{1,0},{2,3},{3,2},{4,5},{5,4},{6,7},{7,6},{8,9},{9,8},{10,11... | collective-permute-start | bytes 1179656 | tf_op jit(solution)/shard_map/ppermute | solution.py:568
  258.3 48.4 %all-to-all-start.3 = ((bf16[16,2,24,1728]{3,2,1,0:T(8,128)(2,1)}), bf16[16,2,24,1728]{3,2,1,0:T(8,128)(2,1)}, u32[]{:S(2)}, u32[]{:S(2)}) async-start(bf16[16,2,24,1728]{3,2,1,0:T(8,128)(2,1)} %get-tuple-element.176), calls=%async_computation.3 | async-start | bytes 5505024 | tf_op jit(solution)/shard_map/all_to_all | solution.py:612
  270.9 43.7 %collective-permute-start.40 = (bf16[24,592]{1,0:T(8,128)(2,1)S(1)}, bf16[24,592]{1,0:T(8,128)(2,1)S(1)}, u32[]{:S(2)}, u32[]{:S(2)}) collective-permute-start(bf16[24,592]{1,0:T(8,128)(2,1)S(1)} %fusion.48), channel_id=1, source_target_pairs={{0,64},{4,68},{8,72},{12,76},{16,80},{20,84},{24,88},{28,92},{32,9... | collective-permute-start | bytes 85256 | tf_op jit(solution)/shard_map/ppermute | solution.py:564
  289.1 55.7 %collective-permute-start.36 = (bf16[2,256,768]{2,1,0:T(8,128)(2,1)}, bf16[2,256,768]{2,1,0:T(8,128)(2,1)}, u32[]{:S(2)}, u32[]{:S(2)}) collective-permute-start(bf16[2,256,768]{2,1,0:T(8,128)(2,1)} %get-tuple-element.170), channel_id=1, source_target_pairs={{0,1},{1,0},{2,3},{3,2},{4,5},{5,4},{6,7},{7,6},{8,9},{9,8},{10,11... | collective-permute-start | bytes 2359304 | tf_op jit(solution)/shard_map/ppermute | solution.py:568
  308.9 17.8 %all-to-all-start.4 = ((bf16[32,24,592]{2,1,0:T(8,128)(2,1)}), bf16[32,24,592]{2,1,0:T(8,128)(2,1)S(1)}, u32[]{:S(2)}, u32[]{:S(2)}) async-start(bf16[32,24,592]{2,1,0:T(8,128)(2,1)} %shard_map.208), calls=%async_computation.4 | async-start | bytes 1966080 | tf_op jit(solution)/shard_map/all_to_all | solution.py:703
  313.2 12.7 %collective-permute-start.38 = (bf16[24,1728]{1,0:T(8,128)(2,1)S(1)}, bf16[24,1728]{1,0:T(8,128)(2,1)S(1)}, u32[]{:S(2)}, u32[]{:S(2)}) collective-permute-start(bf16[24,1728]{1,0:T(8,128)(2,1)S(1)} %fusion.46), channel_id=1, source_target_pairs={{0,64},{4,68},{8,72},{12,76},{16,80},{20,84},{24,88},{28,92},{32,9... | collective-permute-start | bytes 248840 | tf_op jit(solution)/shard_map/ppermute | solution.py:564
  341.4 7.5 %collective-permute-start.41 = (bf16[192,768]{1,0:T(8,128)(2,1)S(1)}, bf16[192,768]{1,0:T(8,128)(2,1)S(1)}, u32[]{:S(2)}, u32[]{:S(2)}) collective-permute-start(bf16[192,768]{1,0:T(8,128)(2,1)S(1)} %bitcast.124), channel_id=1, source_target_pairs={{0,2},{1,3},{2,0},{3,1},{4,6},{5,7},{6,4},{7,5},{8,10},{9,11},{10,... | collective-permute-start | bytes 884744 | tf_op jit(solution)/shard_map/ppermute | solution.py:568
  349.0 22.3 %collective-permute-start.42 = (bf16[2,192,768]{2,1,0:T(8,128)(2,1)S(1)}, bf16[2,192,768]{2,1,0:T(8,128)(2,1)S(1)}, u32[]{:S(2)}, u32[]{:S(2)}) collective-permute-start(bf16[2,192,768]{2,1,0:T(8,128)(2,1)S(1)} %pad_maximum_fusion.p0), channel_id=1, source_target_pairs={{0,4},{4,0},{8,12},{12,8},{16,20},{20,16},{24,28},{28,24},{32,36},... | collective-permute-start | bytes 1769480 | tf_op jit(solution)/shard_map/ppermute | solution.py:564
  350.3 21.9 %collective-permute-start.45 = (bf16[2,192,768]{2,1,0:T(8,128)(2,1)S(1)}, bf16[2,192,768]{2,1,0:T(8,128)(2,1)S(1)}, u32[]{:S(2)}, u32[]{:S(2)}) collective-permute-start(bf16[2,192,768]{2,1,0:T(8,128)(2,1)S(1)} %pad_maximum_fusion.p0), channel_id=1, source_target_pairs={{0,8},{4,12},{8,0},{12,4},{16,24},{20,28},{24,16},{28,20},{32,40},... | collective-permute-start | bytes 1769480 | tf_op jit(solution)/shard_map/ppermute | solution.py:564
  352.7 27.0 %collective-permute-start.46 = (bf16[2,192,768]{2,1,0:T(8,128)(2,1)S(1)}, bf16[2,192,768]{2,1,0:T(8,128)(2,1)S(1)}, u32[]{:S(2)}, u32[]{:S(2)}) collective-permute-start(bf16[2,192,768]{2,1,0:T(8,128)(2,1)S(1)} %pad_maximum_fusion.p0), channel_id=1, source_target_pairs={{0,12},{4,8},{8,4},{12,0},{16,28},{20,24},{24,20},{28,16},{32,44},... | collective-permute-start | bytes 1769480 | tf_op jit(solution)/shard_map/ppermute | solution.py:564
  353.0 29.5 %collective-permute-start.37 = (bf16[256,768]{1,0:T(8,128)(2,1)S(1)}, bf16[256,768]{1,0:T(8,128)(2,1)S(1)}, u32[]{:S(2)}, u32[]{:S(2)}) collective-permute-start(bf16[256,768]{1,0:T(8,128)(2,1)S(1)} %fusion.43), channel_id=1, source_target_pairs={{0,2},{1,3},{2,0},{3,1},{4,6},{5,7},{6,4},{7,5},{8,10},{9,11},{10,... | collective-permute-start | bytes 1179656 | tf_op jit(solution)/shard_map/ppermute | solution.py:568
  356.0 9.7 %collective-permute-start.43 = (f32[24,10]{1,0:T(8,128)S(1)}, f32[24,10]{1,0:T(8,128)S(1)}, u32[]{:S(2)}, u32[]{:S(2)}) collective-permute-start(f32[24,10]{1,0:T(8,128)S(1)} %bitcast.141), channel_id=1, source_target_pairs={{0,1},{1,0},{2,3},{3,2},{4,5},{5,4},{6,7},{7,6},{8,9},{9,8},{10,11... | collective-permute-start | bytes 2888 | tf_op jit(solution)/shard_map/ppermute | solution.py:568
  370.2 14.5 %collective-permute-start.47 = (bf16[2,192,768]{2,1,0:T(8,128)(2,1)S(1)}, bf16[2,192,768]{2,1,0:T(8,128)(2,1)S(1)}, u32[]{:S(2)}, u32[]{:S(2)}) collective-permute-start(bf16[2,192,768]{2,1,0:T(8,128)(2,1)S(1)} %pad_maximum_fusion.p0), channel_id=1, source_target_pairs={{0,1},{1,0},{2,3},{3,2},{4,5},{5,4},{6,7},{7,6},{8,9},{9,8},{10,11... | collective-permute-start | bytes 1769480 | tf_op jit(solution)/shard_map/ppermute | solution.py:568
  371.3 13.5 %collective-permute-start.48 = (bf16[2,192,768]{2,1,0:T(8,128)(2,1)S(1)}, bf16[2,192,768]{2,1,0:T(8,128)(2,1)S(1)}, u32[]{:S(2)}, u32[]{:S(2)}) collective-permute-start(bf16[2,192,768]{2,1,0:T(8,128)(2,1)S(1)} %collective-permute-done.42.p1), channel_id=1, source_target_pairs={{0,1},{1,0},{2,3},{3,2},{4,5},{5,4},{6,7},{7,6},{8,9},{9,8},{10,11... | collective-permute-start | bytes 1769480 | tf_op jit(solution)/shard_map/ppermute | solution.py:568
  372.1 12.6 %collective-permute-start.49 = (bf16[2,192,768]{2,1,0:T(8,128)(2,1)S(1)}, bf16[2,192,768]{2,1,0:T(8,128)(2,1)S(1)}, u32[]{:S(2)}, u32[]{:S(2)}) collective-permute-start(bf16[2,192,768]{2,1,0:T(8,128)(2,1)S(1)} %collective-permute-done.45.p2), channel_id=1, source_target_pairs={{0,1},{1,0},{2,3},{3,2},{4,5},{5,4},{6,7},{7,6},{8,9},{9,8},{10,11... | collective-permute-start | bytes 1769480 | tf_op jit(solution)/shard_map/ppermute | solution.py:568
  379.6 6.9 %collective-permute-start.50 = (bf16[2,192,768]{2,1,0:T(8,128)(2,1)S(1)}, bf16[2,192,768]{2,1,0:T(8,128)(2,1)}, u32[]{:S(2)}, u32[]{:S(2)}) collective-permute-start(bf16[2,192,768]{2,1,0:T(8,128)(2,1)S(1)} %collective-permute-done.46.p3), channel_id=1, source_target_pairs={{0,1},{1,0},{2,3},{3,2},{4,5},{5,4},{6,7},{7,6},{8,9},{9,8},{10,11... | collective-permute-start | bytes 1769480 | tf_op jit(solution)/shard_map/ppermute | solution.py:568
  429.7 14.5 %all-to-all-start.6 = ((bf16[32,24,224]{2,1,0:T(8,128)(2,1)}), bf16[32,24,224]{2,1,0:T(8,128)(2,1)}, u32[]{:S(2)}, u32[]{:S(2)}) async-start(bf16[32,24,224]{2,1,0:T(8,128)(2,1)} %bitcast.121), calls=%async_computation.6 | async-start | bytes 786432 | tf_op jit(solution)/shard_map/all_to_all | solution.py:726
  (61 other events, 741.4 us)

commit v3 on v2

--- a/solution.py
+++ b/solution.py
@@ -26,6 +26,7 @@
 COEF_B = -4.775
 COEF_C = 2.0315
 NEG_FILL = -1e30
+F1_LIMIT, F2_LIMIT, B1_LIMIT, B2_LIMIT, GN_LIMIT, NS_LIMIT, OTHER_LIMIT = 10, 6, 14, 14, 8, 26, 6
 BF = jnp.bfloat16
 F32 = jnp.float32
 VMEM = pltpu.VMEM
@@ -43,7 +44,7 @@
     return lax.dot_general(a, b, (((0,), (0,)), ((), ())), preferred_element_type=F32)
 
 
-def call(kernel, outs, ins, scratch=(), grid=None, in_specs=None, out_specs=None, flops=0, limit=60):
+def call(kernel, outs, ins, scratch=(), grid=None, in_specs=None, out_specs=None, flops=0, limit=OTHER_LIMIT):
     whole = pl.BlockSpec(memory_space=VMEM)
     kwargs = {} if grid is None else dict(grid=grid)
     return pl.pallas_call(
@@ -59,7 +60,6 @@
 
 
 SMEM_SPEC = pl.BlockSpec(memory_space=pltpu.SMEM)
-NEAR_SPEC = pl.BlockSpec((D, D), lambda *_: (0, 2))
 WIDE = 2304
 
 
@@ -72,6 +72,21 @@
     key = lax.broadcasted_iota(jnp.int32, (width, 256), 0)
     query = lax.broadcasted_iota(jnp.int32, (width, 256), 1) + i * 256
     return (key >= start_row) & (key <= query)
+
+
+def by_heads(rows):
+    return jnp.concatenate([rows * head_mask(h) for h in range(HEADS_HERE)], 0)
+
+
+def own_lanes(stacked):
+    return sum(stacked[h * 256 : (h + 1) * 256] * head_mask(h).astype(F32) for h in range(HEADS_HERE))
+
+
+def blocked(start_row, i, width):
+    key = lax.broadcasted_iota(jnp.int32, (width, 256), 0)
+    query = lax.broadcasted_iota(jnp.int32, (width, 256), 1) + i * 256
+    once = jnp.where((key >= start_row) & (key <= query), 0.0, NEG_FILL)
+    return jnp.concatenate([once] * HEADS_HERE, 1)
 
 
 def rope_at(cos_ref, sin_ref, there):
@@ -91,7 +106,7 @@
 ):
     me = me_ref[0]
     turn = turn_ref[...]
-    wq, wk, wv = w_ref[:, COLS : 2 * COLS], w_ref[:, 2 * COLS : 3 * COLS], w_ref[:, 3 * COLS :]
+    wq, wk, wv = w_ref[:, 1728:1920], w_ref[:, 1920:2112], w_ref[:, 2112:]
     wqt = dot_nn(wq, turn).astype(BF)
     wkt = dot_nn(wk, turn).astype(BF)
     bias = bias_ref[:3]
@@ -133,8 +148,8 @@
     ins = (me, *first, w, bias, turn, cosine, sine, start)
     outs = [((1024, COLS), BF)] * 3 + [((8, 1024), F32), ((1024, COLS), BF)]
     return call(
-        attend_forward_kernel, outs, ins, in_specs=[SMEM_SPEC] + [whole] * 4 + [NEAR_SPEC] + [whole] * 5,
-        grid=(1,), flops=10**7,
+        attend_forward_kernel, outs, ins, in_specs=[SMEM_SPEC] + [whole] * 10,
+        flops=10**7, limit=F1_LIMIT,
     )
 
 
@@ -143,16 +158,17 @@
     return pre * below, below + pre * jnp.exp(-0.5 * pre * pre) * 0.3989422804014327
 
 
-def forward_out_kernel(keep_in_ref, send_in_ref, mixed_ref, rest_ref, bias_ref, hidden_ref, slope_ref, keep_ref, send_ref):
-    up_bias = jnp.concatenate([bias_ref[3 + r : 4 + r, :] for r in range(4)], 1)
+def up_bias(bias_ref):
+    return jnp.concatenate([bias_ref[3 + r : 4 + r, :] for r in range(4)], 1)
+
+
+def forward_out_kernel(half, keep_in_ref, send_in_ref, mixed_ref, rest_ref, bias_ref, keep_ref, send_ref):
+    bias = up_bias(bias_ref)
     for a in range(2):
-        rows = slice(a * 256, (a + 1) * 256)
-        pre = dot_nn((keep_in_ref, send_in_ref)[a][...], rest_ref[:, :D]) + up_bias
-        hidden, slope = gelu_and_slope(pre)
-        hidden = hidden.astype(BF)
-        hidden_ref[rows, :] = hidden
-        slope_ref[rows, :] = slope
-        out = dot_nt(hidden, rest_ref[:, D : 2 * D]) + dot_nt(mixed_ref[rows, :], rest_ref[:, 2 * D : 2 * D + COLS])
+        pre = dot_nn((keep_in_ref, send_in_ref)[a][...], rest_ref[:, :D]) + bias
+        hidden = gelu_and_slope(pre)[0].astype(BF)
+        mixed = mixed_ref[(2 * half + a) * 256 : (2 * half + a + 1) * 256, :]
+        out = dot_nt(hidden, rest_ref[:, D : 2 * D]) + dot_nt(mixed, rest_ref[:, 2 * D : 2 * D + COLS])
         if a == 0:
             keep_ref[...] = out
         else:
@@ -160,34 +176,25 @@
 
 
 def forward_out(second, mixed, rest, bias, half):
-    part = lambda n: pl.BlockSpec((512, n), lambda i, half=half: (half, 0))
-    full = lambda *s: pl.BlockSpec(s, lambda i: (0,) * len(s))
-    return pl.pallas_call(
-        forward_out_kernel,
-        grid=(1,),
-        out_shape=[jax.ShapeDtypeStruct(s, d) for s, d in (((512, D), BF), ((512, D), F32), ((256, D), F32), ((256, D), BF))],
-        in_specs=[full(256, D), full(256, D), part(COLS), full(D, WIDE), full(7, COLS)],
-        out_specs=[full(512, D), full(512, D), full(256, D), full(256, D)],
-        compiler_params=pltpu.CompilerParams(vmem_limit_bytes=60 << 20),
-        cost_estimate=pl.CostEstimate(flops=10**7, bytes_accessed=1 << 16, transcendentals=0),
-    )(second[2 * half], second[2 * half + 1], mixed, rest, bias)
+    ins = (second[2 * half], second[2 * half + 1], mixed, rest, bias)
+    return call(
+        functools.partial(forward_out_kernel, half), [((256, D), F32), ((256, D), BF)], ins, flops=10**7, limit=F2_LIMIT
+    )
 
 
 def backward_rest_kernel(*refs):
     slots, refs = refs[:12], refs[12:]
-    hidden_ref, hidden_far_ref, mixed_ref, slope_ref, slope_far_ref, rest_ref, gain_ref = refs[:7]
-    grad_ref, d_mixed_ref, w_ref, sums_ref, acc_ref = refs[7:]
-    step = pl.program_id(0)
-
-    def one(slot):
+    mixed_ref, rest_ref, gain_ref, bias_ref, grad_ref, d_mixed_ref, w_ref, sums_ref, acc_ref = refs
+    bias = up_bias(bias_ref)
+    for slot in range(4):
+        rows = slice(slot * 256, (slot + 1) * 256)
         outer, second, scaled = slots[slot][...], slots[4 + slot][...], slots[8 + slot][...]
-        hidden = (hidden_ref if slot < 2 else hidden_far_ref)[...]
-        slope = (slope_ref if slot < 2 else slope_far_ref)[...]
+        hidden, slope = gelu_and_slope(dot_nn(second, rest_ref[:, :D]) + bias)
         d_hidden = dot_nn(outer, rest_ref[:, D : 2 * D])
-        d_mixed_ref[...] = dot_nn(outer, rest_ref[:, 2 * D : 2 * D + COLS]).astype(BF)
+        d_mixed_ref[rows, :] = dot_nn(outer, rest_ref[:, 2 * D : 2 * D + COLS]).astype(BF)
         d_pre = (d_hidden * slope).astype(BF)
         d_second = dot_nt(d_pre, rest_ref[:, :D])
-        w_ref[...] = d_second * gain_ref[2:3, :]
+        w_ref[rows, :] = (d_second * gain_ref[2:3, :]).astype(BF)
         sums = jnp.concatenate(
             [
                 jnp.sum(d_second * scaled.astype(F32), 0, keepdims=True),
@@ -197,48 +204,32 @@
             ],
             0,
         )
-        up, down, out = dot_tn(second, d_pre), dot_tn(outer, hidden), dot_tn(outer, mixed_ref[...])
+        up, down, out = dot_tn(second, d_pre), dot_tn(outer, hidden.astype(BF)), dot_tn(outer, mixed_ref[rows, :])
         if slot == 0:
             acc_ref[:, :D] = up
             acc_ref[:, D : 2 * D] = down
             acc_ref[:, 2 * D :] = out
             sums_ref[...] = sums
-        elif slot < 3:
-            acc_ref[:, :D] += up
-            acc_ref[:, D : 2 * D] += down
-            acc_ref[:, 2 * D :] += out
+        else:
+            if slot < 3:
+                acc_ref[:, :D] += up
+                acc_ref[:, D : 2 * D] += down
+                acc_ref[:, 2 * D :] += out
             sums_ref[...] += sums
-        else:
-            for total, first, last in ((up, 0, D), (down, D, 2 * D), (out, 2 * D, 1728)):
-                total = acc_ref[:, first:last] + total
-                for x in range(2):
-                    for plane in range(16):
-                        row = x * 384 + plane * CHUNK
-                        grad_ref[plane, x, :, first:last] = total[row : row + CHUNK].astype(BF)
-            sums_ref[...] += sums
-
-    for slot in range(4):
-        pl.when(step == slot)(lambda slot=slot: one(slot))
-
-
-def backward_rest(outer, second, scaled, hidden, hidden_far, mixed, slope, slope_far, rest, gain):
-    part = lambda n: pl.BlockSpec((256, n), lambda i: (i, 0))
-    early = lambda n: pl.BlockSpec((256, n), lambda i: (jnp.minimum(i, 1), 0))
-    late = lambda n: pl.BlockSpec((256, n), lambda i: (jnp.maximum(i, 2) - 2, 0))
-    full = lambda *s: pl.BlockSpec(s, lambda i: (0,) * len(s))
-    return pl.pallas_call(
-        backward_rest_kernel,
-        grid=(4,),
-        out_shape=[
-            jax.ShapeDtypeStruct(s, d)
-            for s, d in (((16, 2, CHUNK, 1728), BF), ((1024, COLS), BF), ((1024, D), F32), ((8, D), F32))
-        ],
-        in_specs=[full(256, D)] * 12 + [early(D), late(D), part(COLS), early(D), late(D), full(D, WIDE), full(6, D)],
-        out_specs=[full(16, 2, CHUNK, 1728), part(COLS), part(D), full(8, D)],
-        scratch_shapes=[pltpu.VMEM((D, 1728), F32)],
-        compiler_params=pltpu.CompilerParams(vmem_limit_bytes=60 << 20),
-        cost_estimate=pl.CostEstimate(flops=10**7, bytes_accessed=1 << 16, transcendentals=0),
-    )(*outer, *second, *scaled, hidden, hidden_far, mixed, slope, slope_far, rest, gain)
+    for total, first, last in ((up, 0, D), (down, D, 2 * D), (out, 2 * D, 1728)):
+        total = acc_ref[:, first:last] + total
+        for to_x in range(2):
+            for plane in range(16):
+                row = to_x * 384 + plane * CHUNK
+                grad_ref[plane, to_x, :, first:last] = total[row : row + CHUNK].astype(BF)
+
+
+def backward_rest(outer, second, scaled, mixed, rest, gain, bias):
+    outs = [((16, 2, CHUNK, 1728), BF), ((1024, COLS), BF), ((1024, D), BF), ((8, D), F32)]
+    return call(
+        backward_rest_kernel, outs, (*outer, *second, *scaled, mixed, rest, gain, bias),
+        scratch=[pltpu.VMEM((D, 1728), F32)], flops=10**7, limit=B1_LIMIT,
+    )
 
 
 def attend_backward_kernel(
@@ -247,29 +238,27 @@
     proj_ref, keep_ref, send_ref, sums_ref, bias_ref, dq_ref, dk_ref, dv_ref,
 ):
     me = me_ref[0]
-    dk_ref[...] = jnp.zeros((1024, COLS), F32)
-    dv_ref[...] = jnp.zeros((1024, COLS), F32)
-    for i in range(4):
+    for i in reversed(range(4)):
         n = (i + 1) * 256
         rows = slice(i * 256, n)
         there = pl.ds(pl.multiple_of((me ^ i) * 256, 256), 256)
-        d_mixed = d_mixed_ref[there, :]
-        q, k, v = q_ref[rows, :], k_ref[:n, :], v_ref[:n, :]
-        allowed = allowed_t(start_ref[:, rows], i, n)
-        dq = jnp.zeros((256, COLS), F32)
-        for h in range(HEADS_HERE):
-            mask = head_mask(h)
-            q_here = q * (mask * BF(0.125))
-            d_here = d_mixed * mask
-            scores = dot_nt(k, q_here)
-            probability = jnp.where(allowed, jnp.exp(scores - lse_ref[h : h + 1, rows]), 0.0)
-            d_prob = dot_nt(v, d_here)
-            row = jnp.sum(probability * d_prob, 0, keepdims=True)
-            d_score = (probability * (d_prob - row)).astype(BF)
-            dq = dq + dot_tn(d_score, k) * (mask.astype(F32) * 0.125)
-            dk_ref[:n, :] += dot_nn(d_score, q_here)
-            dv_ref[:n, :] += dot_nn(probability.astype(BF), d_here)
-        dq_ref[rows, :] = dq
+        queries = by_heads(q_ref[rows, :] * BF(0.125))
+        upstream = by_heads(d_mixed_ref[there, :])
+        k, v = k_ref[:n, :], v_ref[:n, :]
+        lse = jnp.concatenate([lse_ref[h : h + 1, rows] for h in range(HEADS_HERE)], 1)
+        probability = jnp.exp(dot_nt(k, queries) - lse + blocked(start_ref[:, rows], i, n))
+        d_prob = dot_nt(v, upstream)
+        row = jnp.sum(probability * d_prob, 0, keepdims=True)
+        d_score = (probability * (d_prob - row)).astype(BF)
+        dq_ref[rows, :] = own_lanes(dot_tn(d_score, k)) * 0.125
+        dk = dot_nn(d_score, queries)
+        dv = dot_nn(probability.astype(BF), upstream)
+        if i == 3:
+            dk_ref[...] = dk
+            dv_ref[...] = dv
+        else:
+            dk_ref[:n, :] += dk
+            dv_ref[:n, :] += dv
     turn = turn_ref[...]
 
     def back(value, cosine, sine):
@@ -287,9 +276,9 @@
         dk = back(dk_ref[there, :], cosine, sine)
         proj = jnp.concatenate([dq, dk, dv_ref[there, :]], 1).astype(BF)
         proj_ref[rows, :] = proj
-        d_first = dot_nt(proj, w_ref[:, COLS:])
+        d_first = dot_nt(proj, w_ref[:, 1728:])
         scaled = (scaled0_ref, scaled1_ref, scaled2_ref, scaled3_ref)[a][...]
-        weighted = d_first * gain_ref[0:1, :] + part_ref[rows, :]
+        weighted = d_first * gain_ref[0:1, :] + part_ref[rows, :].astype(F32)
         if a % 2 == 0:
             keep_ref[a // 2] = weighted
         else:
@@ -314,17 +303,16 @@
     ins = (me, q, k, v, lse, d_mixed, start, cosine, sine, turn, w, gain, *scaled, part)
     outs = [((1024, 576), BF), ((2, 256, D), F32), ((2, 256, D), BF), ((8, D), F32), ((8, 576), F32)]
     return call(
-        attend_backward_kernel, outs, ins, in_specs=[SMEM_SPEC] + [whole] * 9 + [NEAR_SPEC] + [whole] * 6,
-        grid=(1,), scratch=[pltpu.VMEM((1024, COLS), F32)] * 3, flops=10**7,
-    )
-
-
-def grad_near_kernel(
-    direct, first0_ref, first1_ref, first2_ref, first3_ref, proj_ref, sums_ref, sums_rest_ref, bias_ref, upstream_ref, out_ref
+        attend_backward_kernel, outs, ins, in_specs=[SMEM_SPEC] + [whole] * 16,
+        scratch=[pltpu.VMEM((1024, COLS), F32)] * 3, flops=10**7, limit=B2_LIMIT,
+    )
+
+
+def all_grads_kernel(
+    rings, place_ref, first0_ref, first1_ref, first2_ref, first3_ref, proj_ref, sums_ref, sums_rest_ref, bias_ref, upstream_ref, rest_ref, out_ref
 ):
-    total = dot_tn(first0_ref[...], proj_ref[:256, :])
-    for a, ref in ((1, first1_ref), (2, first2_ref), (3, first3_ref)):
-        total = total + dot_tn(ref[...], proj_ref[a * 256 : (a + 1) * 256, :])
+    first = jnp.concatenate([first0_ref[...], first1_ref[...], first2_ref[...], first3_ref[...]], 0)
+    total = dot_tn(first, proj_ref[...])
     pre = sums_rest_ref[2:3, :]
     upper, lower = split(
         jnp.concatenate(
@@ -342,17 +330,26 @@
     row = lax.broadcasted_iota(jnp.int32, (8, 16), 0)
     lane = lax.broadcasted_iota(jnp.int32, (8, 16), 1)
     small = dot_tn(upper, (row == lane).astype(BF)) + dot_tn(lower, (row + 8 == lane).astype(BF))
-    for x in range(2):
+    x, z, y = place_ref[0], place_ref[1], place_ref[2]
+    for to_x in range(2):
         for plane in range(16):
-            here = slice(x * 384 + plane * CHUNK, x * 384 + (plane + 1) * CHUNK)
-            place = (x * 16 + plane,) if direct else (plane, x)
-            out_ref[(*place, slice(None), slice(0, 576))] = total[here].astype(BF)
-            out_ref[(*place, slice(None), slice(576, 592))] = small[here].astype(BF)
-
-
-def grad_near(first, proj, parts, direct):
-    shape = (32, CHUNK, 592) if direct else (16, 2, CHUNK, 592)
-    return call(functools.partial(grad_near_kernel, direct), [(shape, BF)], (*first, proj, *parts), flops=10**7)[0]
+            here = slice(to_x * 384 + plane * CHUNK, to_x * 384 + (plane + 1) * CHUNK)
+            place = (plane, to_x)
+            if rings:
+                half, zr, yr = to_x ^ x, (plane // 4) ^ z, (plane % 4) ^ y
+                place = (half, jnp.where(half == 0, yr, zr), jnp.where(half == 0, zr, yr))
+            out_ref[(*place, slice(None), slice(0, 1728))] = rest_ref[plane, to_x]
+            out_ref[(*place, slice(None), slice(1728, 2304))] = total[here].astype(BF)
+            out_ref[(*place, slice(None), slice(2304, 2320))] = small[here].astype(BF)
+
+
+def all_grads(place, first, proj, parts, rings):
+    shape = (2, 4, 4, CHUNK, 2320) if rings else (16, 2, CHUNK, 2320)
+    whole = pl.BlockSpec(memory_space=VMEM)
+    return call(
+        functools.partial(all_grads_kernel, rings), [(shape, BF)], (place, *first, proj, *parts),
+        in_specs=[SMEM_SPEC] + [whole] * 10, flops=10**7, limit=GN_LIMIT,
+    )[0]
 
 
 def split(value):
@@ -361,17 +358,17 @@
 
 
 def newton_schulz_kernel(
-    place_ref, p0, p1, p2, p3, q0, q1, q2, q3, small_ref, out_ref,
-    m_ref, g_ref, h_ref, gs_ref, ss_ref, hs_ref, x_ref, xs_ref,
+    place_ref, *refs
 ):
+    rows, (small_ref, out_ref, m_ref, g_ref, h_ref, gs_ref, ss_ref, hs_ref, x_ref, xs_ref) = refs[:16], refs[16:]
     x, y = place_ref[0], place_ref[1]
     lane = lax.broadcasted_iota(jnp.int32, (1, D), 1)
     half = y // 2
     used = (x == 0) | ((lane >= half * COLS) & (lane < (half + 1) * COLS))
-    for s, (p, q) in enumerate(((p0, q0), (p1, q1), (p2, q2), (p3, q3))):
-        for b, ref in enumerate((p, q)):
+    for s in range(4):
+        for b in range(2):
             for c in range(2):
-                m_ref[2 * b + c, s * 192 : (s + 1) * 192, :] = jnp.where(used, ref[c], jnp.zeros((), BF))
+                m_ref[2 * b + c, s * 192 : (s + 1) * 192, :] = jnp.where(used, rows[8 * b + 2 * s + c][...], jnp.zeros((), BF))
 
     def store(pair, lower, i, j, value):
         r, c = slice(i * 256, (i + 1) * 256), slice(j * 256, (j + 1) * 256)
@@ -402,12 +399,16 @@
         for b in range(1, 4):
             value = value + dot_nt(m_ref[b, :n, :], m_ref[b, c, :])
         g_ref[:n, c] = value
-    trace = jnp.zeros((1, 1), F32)
     same = lax.broadcasted_iota(jnp.int32, (256, 256), 0) == lax.broadcasted_iota(jnp.int32, (256, 256), 1)
-    for i in range(3):
-        diagonal = jnp.where(same, at(g_ref, i, i), 0.0)
-        trace = trace + jnp.sum(jnp.sum(diagonal, 1, keepdims=True), 0, keepdims=True)
-    scale = 1.0 / (jnp.sqrt(trace) + EPS_ORTH)
+
+    def trace_of(ref):
+        trace = jnp.zeros((1, 1), F32)
+        for i in range(3):
+            diagonal = jnp.where(same, at(ref, i, i), 0.0)
+            trace = trace + jnp.sum(jnp.sum(diagonal, 1, keepdims=True), 0, keepdims=True)
+        return trace
+
+    scale = 1.0 / (jnp.sqrt(trace_of(g_ref)) + EPS_ORTH)
     for j in range(3):
         for i in range(j + 1):
             value = at(g_ref, i, j) * (scale * scale)
@@ -431,7 +432,7 @@
         s0, s1 = ss_ref[0], ss_ref[1]
         return COEF_A * x_ref[...] + dot_nn(s0, xs_ref[0]) + dot_nn(s0, xs_ref[1]) + dot_nn(s1, xs_ref[0])
 
-    def step(_, carry):
+    def step():
         mix()
         current = advance()
         x_ref[...] = current
@@ -450,11 +451,68 @@
             store(gs_ref, True, i, j, value)
 
         product(hs_ref, ss_ref, finish_g)
+
+    def repeated(_, carry):
+        step()
         return carry
 
-    lax.fori_loop(0, NS_STEPS - 1, step, 0)
-    mix()
-    current = advance()
+    lax.fori_loop(0, NS_STEPS - 2, repeated, 0)
+
+    def once(a, b, finish):
+        for j in range(3):
+            n, c = (j + 1) * 256, slice(j * 256, (j + 1) * 256)
+            value = dot_nn(a[0, :n, :], b[0, :, c])
+            for i in range(j + 1):
+                finish(i, j, value[i * 256 : (i + 1) * 256])
+
+    def store_once(pair, i, j, value):
+        r, c = slice(i * 256, (i + 1) * 256), slice(j * 256, (j + 1) * 256)
+        pair[0, r, c] = value.astype(BF)
+        if i != j:
+            pair[0, c, r] = value.T.astype(BF)
+
+    m = trace_of(g_ref) * (1.0 / D)
+    for i in range(3):
+        value = at(g_ref, i, i) - jnp.where(same, m, 0.0)
+        put(g_ref, i, i, value)
+        store_once(gs_ref, i, i, value)
+
+    def mix_once(m):
+        def finish(i, j, value):
+            store(ss_ref, True, i, j, (COEF_B + 2.0 * COEF_C * m) * at(g_ref, i, j) + COEF_C * value)
+
+        once(gs_ref, gs_ref, finish)
+        return (COEF_B + COEF_C * m) * m
+
+    def advance_once(p):
+        s0, s1 = ss_ref[0], ss_ref[1]
+        return (COEF_A + p) * x_ref[...] + dot_nn(s0, xs_ref[0]) + dot_nn(s0, xs_ref[1]) + dot_nn(s1, xs_ref[0])
+
+    p = mix_once(m)
+    current = advance_once(p)
+    x_ref[...] = current
+    xs_ref[0], xs_ref[1] = split(current)
+
+    def mixer_at(i, j):
+        r, c = slice(i * 256, (i + 1) * 256), slice(j * 256, (j + 1) * 256)
+        return ss_ref[0, r, c].astype(F32) + ss_ref[1, r, c].astype(F32)
+
+    def finish_h_once(i, j, value):
+        value = (COEF_A + p) * at(g_ref, i, j) + m * mixer_at(i, j) + value
+        put(h_ref, i, j, value)
+        store_once(hs_ref, i, j, value)
+
+    once(ss_ref, gs_ref, finish_h_once)
+    q = (COEF_A + p) * m
+
+    def finish_g_once(i, j, value):
+        value = (COEF_A + p) * at(h_ref, i, j) + q * mixer_at(i, j) + value
+        put(g_ref, i, j, value)
+        store_once(gs_ref, i, j, value)
+
+    once(hs_ref, ss_ref, finish_g_once)
+    p = mix_once((COEF_A + p) * q)
+    current = advance_once(p)
     for s in range(4):
         for group in range(8):
             row = s * 192 + group * 24
@@ -467,10 +525,10 @@
     whole = pl.BlockSpec(memory_space=VMEM)
     return call(
         newton_schulz_kernel, [((8, 4, CHUNK, 224), BF)], (place, *pieces, small),
-        in_specs=[SMEM_SPEC] + [whole] * 9,
+        in_specs=[SMEM_SPEC] + [whole] * 17,
         scratch=[pltpu.VMEM((4, D, D), BF)] + [pltpu.VMEM((D, D), F32)] * 2 + [pair] * 3
         + [pltpu.VMEM((D, COLS), F32), pltpu.VMEM((2, D, COLS), BF)],
-        flops=10**7,
+        flops=10**7, limit=NS_LIMIT,
     )[0]
 
 
@@ -504,13 +562,9 @@
     )[0]
 
 
-def momenta_kernel(
-    attn_ref, mlp_ref, rest0_ref, rest1_ref, near1_ref, near0_ref, new_attn_ref, new_mlp_ref, sends_ref, small_ref
-):
-    total = jnp.sum(near0_ref[...].astype(F32), 0)
-    near1 = near1_ref[...]
+def momenta_kernel(attn_ref, mlp_ref, grads0_ref, grads1_ref, new_attn_ref, new_mlp_ref, sends_ref, small_ref):
     none = jnp.zeros((CHUNK, 2 * COLS), BF)
-    for layer, rest_ref, near in ((0, rest0_ref, total), (1, rest1_ref, near1)):
+    for layer, rest_ref in ((0, grads0_ref), (1, grads1_ref)):
         for m in range(2):
             parts = []
             for r in range(4):
@@ -521,14 +575,15 @@
             sends_ref[2 * layer + m] = jnp.concatenate(parts, 1)
         parts = []
         for m in range(4):
-            grad = near[:, m * COLS : (m + 1) * COLS] if m < 3 else rest_ref[:, 2 * D :]
+            first = 1728 + m * COLS if m < 3 else 2 * D
+            grad = rest_ref[:, first : first + COLS]
             mom = MOMENTUM * attn_ref[layer, m] + grad
             new_attn_ref[layer, m] = mom
             parts.append(mom.astype(BF))
         sends_ref[4 + 2 * layer] = jnp.concatenate([*parts[:2], none], 1)
         sends_ref[5 + 2 * layer] = jnp.concatenate([*parts[2:], none], 1)
-    here = total[:, 576:583] + total[:, 584:591]
-    last = near1[:, 576:583] + near1[:, 584:591]
+    here = grads0_ref[:, 2304:2311] + grads0_ref[:, 2312:2319]
+    last = grads1_ref[:, 2304:2311] + grads1_ref[:, 2312:2319]
     small_ref[...] = jnp.concatenate([here[:, :5], last[:, :5], here[:, 5:], last[:, 5:]], 1)
 
 
@@ -537,7 +592,10 @@
     return call(momenta_kernel, outs, (mom_attn, mom_mlp, *ins))
 
 
-def new_weights_kernel(back_ref, attn_ref, mlp_ref, new_attn_ref, new_mlp_ref, small_ref):
+def new_weights_kernel(
+    back_ref, attn_ref, mlp_ref, mom_bias_ref, bias_ref, mom_vec_ref, vec_ref,
+    new_attn_ref, new_mlp_ref, new_mom_bias_ref, new_bias_ref, new_mom_vec_ref, new_vec_ref,
+):
     def block(x, z, y):
         return back_ref[x * 16 + z * 4 + y, :, :COLS].astype(F32)
 
@@ -549,15 +607,29 @@
             for r in range(4):
                 step = STEP_SCALE * math.sqrt(FF) * block(0, 2 * layer + m, r)
                 new_mlp_ref[layer, m, :, r, :] = mlp_ref[layer, m, :, r, :] - step
+    parts = []
     for i in range(32):
-        part = back_ref[i, :, COLS:].astype(F32)
-        small_ref[i] = part[:, :14] + part[:, 14:28]
-
-
-def new_weights(back, attn_w, mlp_w):
-    outs = [(attn_w.shape, F32), (mlp_w.shape, F32), ((32, CHUNK, 14), F32)]
-    attn, mlp, small = call(new_weights_kernel, outs, (back, attn_w, mlp_w))
-    return attn, mlp, small.reshape(D, 14)
+        row = lax.broadcasted_iota(jnp.int32, (CHUNK, D), 0)
+        lane = lax.broadcasted_iota(jnp.int32, (CHUNK, D), 1)
+        parts.append(dot_tn(back_ref[i, :, COLS:], (row + i * CHUNK == lane).astype(BF)))
+    lying = sum(parts)
+    total = lying[:14] + lying[14:28]
+    rate = RATE_VEC / math.sqrt(32768)
+    for layer in range(2):
+        for row in range(6):
+            grad = total[5 * layer + min(row, 4) : 5 * layer + min(row, 4) + 1]
+            mom = MOMENTUM * mom_vec_ref[layer, row : row + 1, :] + grad
+            new_mom_vec_ref[layer, row : row + 1, :] = mom
+            new_vec_ref[layer, row : row + 1, :] = vec_ref[layer, row : row + 1, :] - rate * mom
+        grads = jnp.concatenate([total[10 + 2 * layer : 11 + 2 * layer], total[11 + 2 * layer : 12 + 2 * layer]], 1)
+        for row in range(7):
+            mom = MOMENTUM * mom_bias_ref[layer, row : row + 1, :] + grads[:, row * COLS : (row + 1) * COLS]
+            new_mom_bias_ref[layer, row : row + 1, :] = mom
+            new_bias_ref[layer, row : row + 1, :] = bias_ref[layer, row : row + 1, :] - rate * mom
+
+
+def new_weights(*ins):
+    return call(new_weights_kernel, [(part.shape, F32) for part in ins[1:]], ins)
 
 
 def dp_swap(value, mask):
@@ -612,6 +684,20 @@
     return lax.all_to_all(partial, "dp", 0, 0, tiled=True, axis_index_groups=PLANE)
 
 
+def add_by_rings(partial, ready):
+    def total(pieces):
+        pieces = [piece.astype(F32) for piece in pieces]
+        return (pieces[0] + pieces[1]) + (pieces[2] + pieces[3])
+
+    first = [swap_four([partial[half, s] for s in range(4)], unit) for half, unit in ((0, 1), (1, 4))]
+    first, ready = lax.optimization_barrier((first, ready))
+    halves = []
+    for pieces, then in zip(first, (4, 1)):
+        block = total(pieces).astype(BF)
+        halves.append(total(swap_four([block[s] for s in range(4)], then)))
+    return halves[0] + dp_swap(halves[1].astype(BF), 16).astype(F32), ready
+
+
 def add_arrived(arrived):
     sums = jnp.sum(arrived.astype(F32), 0)
     x = dp_place()[0]
@@ -656,7 +742,11 @@
 def normalized(stream, vector_rows, beside=None):
     scaled, inverse = standardize(stream)
     first, second, scaled_all = [], [], []
-    slots, beside = gather_tokens(scaled.astype(jnp.float16), beside)
+    sent = scaled.astype(jnp.float16)
+    if beside is not None:
+        sent, beside = lax.optimization_barrier((sent, beside))
+        beside = in_order(beside)
+    slots, beside = gather_tokens(sent, beside)
     for slot in slots:
         wide = slot.astype(F32)
         first.append((wide * vector_rows[0] + vector_rows[1]).astype(BF))
@@ -671,38 +761,48 @@
     q, k, v, lse, mixed = attend_forward(
         me, first, weights, bias_rows, turn, cosine, sine, start
     )
-    hidden_far, slope_far, keep_far, send_far = forward_out(second, mixed, weights, bias_rows, 1)
+    keep_far, send_far = forward_out(second, mixed, weights, bias_rows, 1)
     pair = (keep_far + tensor_swap(send_far, 1).astype(F32)).astype(BF)
     mixed, pair = lax.optimization_barrier((mixed, pair))
-    hidden, slope, keep, send = forward_out(second, mixed, weights, bias_rows, 0)
-    branch = keep + tensor_swap(send, 1).astype(F32) + tensor_swap(pair, 2).astype(F32)
-    record = (q, k, v, lse, mixed, hidden, hidden_far, slope, slope_far)
-    return record, stream + branch + vector_rows[4] + vector_rows[5]
-
-
-def backward_layer(upstream, outer, record, weights, vector_rows, common, ready, last):
+    keep, send = forward_out(second, mixed, weights, bias_rows, 0)
+    parts = (keep, tensor_swap(send, 1), tensor_swap(pair, 2))
+    record = (q, k, v, lse, mixed)
+    return record, parts
+
+
+def add_parts(stream, parts, vector_rows):
+    branch = parts[0] + parts[1].astype(F32) + parts[2].astype(F32)
+    return stream + branch + vector_rows[4] + vector_rows[5]
+
+
+def backward_layer(upstream, outer, record, weights, bias_rows, vector_rows, common, ready, last):
     me, cosine, sine, start, turn = common
-    scaled, inverse, first, second, scaled_all, q, k, v, lse, mixed, hidden, hidden_far, slope, slope_far = record
+    scaled, inverse, first, second, scaled_all, q, k, v, lse, mixed = record
     grad_rest, d_mixed, part, sums_rest = backward_rest(
-        outer, second, scaled_all, hidden, hidden_far, mixed, slope, slope_far, weights, vector_rows
-    )
-    grad_rest = scatter_rows(grad_rest)
-    d_mixed, ready = lax.optimization_barrier((d_mixed, ready))
+        outer, second, scaled_all, mixed, weights, vector_rows, bias_rows
+    )
+    if not last:
+        d_mixed, ready = lax.optimization_barrier((d_mixed, ready))
     proj, keep, send, sums, bias = attend_backward(
         me, q, k, v, lse, d_mixed, start, cosine, sine, turn, weights, vector_rows, scaled_all, part
     )
     pair = keep + tensor_swap(send, 1).astype(F32)
-    weighted = pair[0] + tensor_swap(pair[1].astype(BF), 2).astype(F32)
+    pair = (pair[0], pair[1].astype(BF))
+    weighted = pair[0] + tensor_swap(pair[1], 2).astype(F32)
     new_upstream = upstream + inverse * (
         weighted
         - jnp.mean(weighted, -1, keepdims=True)
         - scaled * jnp.mean(weighted * scaled, -1, keepdims=True)
     )
-    grad_near_here, grad_rest = lax.optimization_barrier((grad_near(first, proj, (sums, sums_rest, bias, upstream), last), grad_rest))
-    grad_near_here = (
-        lax.all_to_all(grad_near_here, "dp", 0, 0, tiled=True) if last else scatter_rows(grad_near_here)
-    )
-    return new_upstream, grad_rest, grad_near_here, ready
+    place = jnp.stack(dp_place()).astype(jnp.int32)
+    if not last:
+        proj, pair = lax.optimization_barrier((proj, pair))
+    grads = all_grads(place, first, proj, (sums, sums_rest, bias, upstream, grad_rest), last)
+    if last:
+        grads, ready = add_by_rings(grads, ready)
+    else:
+        grads = scatter_rows(grads)
+    return new_upstream, grads, ready
 
 
 def two_terms(value):
@@ -717,8 +817,10 @@
     shared = small[:, :10]
     shared = shared + tensor_swap(shared, 1)
     shared = shared + tensor_swap(shared, 2)
-    pieces = swap_four([jnp.stack([rows, tensor_swap(rows, 2)])] * 4, 1)
-    pieces[1], shared = lax.optimization_barrier((pieces[1], shared))
+    both = jnp.stack([rows, tensor_swap(rows, 2)])
+    left, right = dp_swap(both, 1), dp_swap(both, 3)
+    left, shared = lax.optimization_barrier((left, shared))
+    pieces = [both[0], both[1], left[0], left[1], dp_swap(right[0], 1), dp_swap(left[1], 3), right[0], right[1]]
     pieces = pieces + [tensor_swap(piece, 1) for piece in pieces]
     small = two_terms(jnp.concatenate([shared, small[:, 10:]], 1))
     small = jnp.pad(small, ((0, 0), (0, 4)))
@@ -741,32 +843,27 @@
     arrived, later, norms, common = lax.optimization_barrier((arrived, later, norms, common))
     weights = [arrived]
     arrived = gather_rows(later)
-    record, stream = forward_layer(stream, norms, weights[0], in_bias[0], vectors[0], common)
+    record, parts = forward_layer(stream, norms, weights[0], in_bias[0], vectors[0], common)
+    stream = add_parts(stream, parts, vectors[0])
     saved = [norms + record]
-    stream, arrived = lax.optimization_barrier((stream, arrived))
-    norms, last = normalized(stream, vectors[1], in_order(arrived))
+    norms, last = normalized(stream, vectors[1], arrived)
     weights.append(last)
-    record, stream = forward_layer(stream, norms, weights[1], in_bias[1], vectors[1], common)
+    record, parts = forward_layer(stream, norms, weights[1], in_bias[1], vectors[1], common)
     saved.append(norms + record)
-    rests, nears = [None, None], [None, None]
     outer, _ = gather_tokens(upstream.astype(BF))
-    upstream, rests[1], nears[1], stream = backward_layer(
-        upstream, outer, saved[1], weights[1], vectors[1], common, stream, False
-    )
+    upstream, grads_last, ready = backward_layer(
+        upstream, outer, saved[1], weights[1], in_bias[1], vectors[1], common, parts, False
+    )
+    stream = add_parts(stream, ready, vectors[1])
     outer, _ = gather_tokens(upstream.astype(BF))
-    upstream, rests[0], nears[0], nears[1] = backward_layer(
-        upstream, outer, saved[0], weights[0], vectors[0], common, nears[1], True
-    )
-    rests, last_near = [add_arrived(rest) for rest in rests], add_arrived(nears[1])
-    new_mom_attn, new_mom_mlp, sends, small = momenta(mom_attn, mom_mlp, rests[0], rests[1], last_near, nears[0])
+    upstream, grads_first, grads_last = backward_layer(
+        upstream, outer, saved[0], weights[0], in_bias[0], vectors[0], common, grads_last, True
+    )
+    new_mom_attn, new_mom_mlp, sends, small = momenta(mom_attn, mom_mlp, grads_first, add_arrived(grads_last))
     result = orthogonal_blocks(sends, small)
-    new_attn_w, new_mlp_w, small = new_weights(result, attn_w, mlp_w)
-    vec_total = small[:, :10].T.reshape(2, 5, D)
-    vec_total = jnp.concatenate([vec_total, vec_total[:, 4:]], 1)
-    bias_total = small[:, 10:].T.reshape(2, 2 * D)[:, :1344].reshape(2, 7, COLS)
-    new_mom_bias = MOMENTUM * mom_bias + bias_total
-    new_mom_vec = MOMENTUM * mom_vec + vec_total
-    vec_rate = RATE_VEC / math.sqrt(32768)
+    new_attn_w, new_mlp_w, new_mom_bias, new_in_bias, new_mom_vec, new_vectors = new_weights(
+        result, attn_w, mlp_w, mom_bias, in_bias, mom_vec, vectors
+    )
     return (
         stream[None],
         upstream[None],
@@ -775,9 +872,9 @@
         new_mom_mlp,
         new_mlp_w,
         new_mom_bias,
-        in_bias - vec_rate * new_mom_bias,
+        new_in_bias,
         new_mom_vec,
-        vectors - vec_rate * new_mom_vec,
+        new_vectors,
     )
 
 

time: 461 us -> 396 us (0.86)
  Pallas kernels: 169 us -> 105 us
  other arithmetic: 40.1 us -> 24 us
  local copies, waits for them, and re-layouts: 20.7 us -> 26.7 us
  starting transfers between devices: 133 us -> 138 us
    pallas_call x6 -> x0, Pallas kernels: 47.5 us -> none  [the longest x2 26.3 us: backward_rest(): pl.pallas_call(backward_rest_kernel, grid=(4,), out_shape=[jax.ShapeDtype...]
    ppermute x22 -> x34, starting transfers between devices: 27 us -> 49.3 us  [dp_swap(): return lax.ppermute(value, 'dp', [(i, i ^ mask) for i in range(32)])]
    ppermute x22 -> x34, waiting for transfers between devices: 22.5 us -> 42.4 us  [dp_swap(): return lax.ppermute(value, 'dp', [(i, i ^ mask) for i in range(32)])]
    pallas_call x11 -> x17, Pallas kernels: 121 us -> 105 us  [call(): pl.pallas_call(kernel, out_shape=[jax.ShapeDtypeStruct(s, d) for s, d in...]
    all_to_all x3 -> x1, starting transfers between devices: 22 us -> 10.2 us  [scatter_rows(): lax.all_to_all(partial, 'dp', 0, 0, tiled=True, axis_index_groups=PLANE)]
    all_to_all x3 -> x1, waiting for transfers between devices: 10.8 us -> 0.01 us  [scatter_rows(): lax.all_to_all(partial, 'dp', 0, 0, tiled=True, axis_index_groups=PLANE)]
    unnamed x112 -> x206, local copies, waits for them, and re-layouts: 9.59 us -> 19.7 us
    ppermute x29 -> x33, waiting for transfers between devices: 37 us -> 32.8 us  [tensor_swap(): return lax.ppermute(value, 'tensor', [(i, i ^ mask) for i in range(4)])]
  transfers between devices with their start and end apart: 57 -> 70, of which waited for: 23 -> 23; matrix products, arithmetic and copies ran while one was open for 10% -> 7% of each run, Pallas kernels for 26% -> 14%
where the time goes in v3:
time: 396 us; the launch traced here: 388 us
  starting transfers between devices  138 us (35%)
  Pallas kernels  105 us (27%)
  waiting for transfers between devices  82.2 us (21%)
  local copies, waits for them, and re-layouts  26.7 us (7%)
  other arithmetic  24 us (6%)
  blocking collectives  9.16 us (2%)
    pallas_call x17, Pallas kernels, call(): pl.pallas_call(kernel, out_shape=[jax.ShapeDtypeStruct(s, d) for s, d in...  105 us
    ppermute x33, starting transfers between devices, tensor_swap(): return lax.ppermute(value, 'tensor', [(i, i ^ mask) for i in range(4)])  67.1 us
    ppermute x34, starting transfers between devices, dp_swap(): return lax.ppermute(value, 'dp', [(i, i ^ mask) for i in range(32)])  49.3 us
    ppermute x34, waiting for transfers between devices, dp_swap(): return lax.ppermute(value, 'dp', [(i, i ^ mask) for i in range(32)])  42.4 us
    ppermute x33, waiting for transfers between devices, tensor_swap(): return lax.ppermute(value, 'tensor', [(i, i ^ mask) for i in range(4)])  32.8 us
    unnamed x206, local copies, waits for them, and re-layouts  19.7 us
    all_to_all x1, starting transfers between devices, scatter_rows(): lax.all_to_all(partial, 'dp', 0, 0, tiled=True, axis_index_groups=PLANE)  10.2 us
    all_to_all x1, blocking collectives, orthogonal_blocks(): lax.all_to_all(sends, 'dp', 0, 0, tiled=True, axis_index_groups=groups)  9.16 us
  transfers between devices with their start and end apart: 70, of which 23 were waited for; matrix products, arithmetic and copies ran while one was open for 7% of the time, Pallas kernels for 14%

profile of v3, /device:TPU:1, one launch (start us, length us, event | category | flops | bytes accessed | tf_op | source)
XLA Modules:
  0.0 388.0 jit_solution(170362717579478170)
XLA Ops:
  6.5 3.3 collective-permute-start.1
  11.6 2.5 collective-permute-start.17
  17.8 3.0 collective-permute-start.9
  21.6 2.4 collective-permute-done.15
  28.1 3.0 collective-permute-start.12
  31.2 4.2 %collective-permute-start.18 = (f16[256,768]{1,0:T(8,128)(2,1)S(1)}, f16[256,768]{1,0:T(8,128)(2,1)S(1)}, u32[]{:S(2)}, u32[]{:S(2)}) collective-permute-start(f16[256,768]{1,0:T(8,128)(2,1)S(1)} %collective-permute-done.17), channel_id=1, source_target_pairs={{0,1},{1,0},{2,3},{3,2},{4,5},{5,4},{6,7},{7,6},{8,9},{9,8},{10,11... | collective-permute-start | bytes 1179656 | tf_op jit(solution)/shard_map/ppermute | solution.py:640
  38.4 3.3 collective-permute-start.6
  42.3 2.6 collective-permute-start.14
  51.2 4.9 %all-to-all-start = ((bf16[16,2,24,2304]{3,2,1,0:T(8,128)(2,1)}), bf16[16,2,24,2304]{3,2,1,0:T(8,128)(2,1)}, u32[]{:S(2)}, u32[]{:S(2)}) async-start(bf16[16,2,24,2304]{3,2,1,0:T(8,128)(2,1)} %concatenate.9), calls=%async_computation | async-start | bytes 7077888 | tf_op jit(solution)/shard_map/all_to_all | solution.py:665
  63.8 7.6 %shard_map.197 = (bf16[1024,192]{1,0:T(8,128)(2,1)S(1)}, bf16[1024,192]{1,0:T(8,128)(2,1)S(1)}, bf16[1024,192]{1,0:T(8,128)(2,1)S(1)}, f32[8,1024]{1,0:T(8,128)S(1)}, bf16[1024,192]{1,0:T(8,128)(2,1)S(1)}) custom-call(s32[1]{0:T(128)} %bitcast.17.me_ref, bf16[256,768]{1,0:T(8,128)(2,1)S(1)} %copy-done.11, bf16[256,768]{1,0:T(8,128)(2,1)S(1)} %copy-done.17, ...), custom_call_target="tpu_custom_call" | custom-call | flops 10000000 | bytes 65536 | tf_op jit(solution)/shard_map/pallas_call | solution.py:50
  73.1 4.9 %collective-permute-start.19 = (bf16[256,768]{1,0:T(8,128)(2,1)S(1)}, bf16[256,768]{1,0:T(8,128)(2,1)S(1)}, u32[]{:S(2)}, u32[]{:S(2)}) collective-permute-start(bf16[256,768]{1,0:T(8,128)(2,1)S(1)} %get-tuple-element.117), channel_id=1, source_target_pairs={{0,1},{1,0},{2,3},{3,2},{4,5},{5,4},{6,7},{7,6},{8,9},{9,8},{10,11... | collective-permute-start | bytes 1179656 | tf_op jit(solution)/shard_map/ppermute | solution.py:640
  83.0 10.7 %collective-permute-done.21 = bf16[256,768]{1,0:T(8,128)(2,1)S(1)} collective-permute-done((bf16[256,768]{1,0:T(8,128)(2,1)S(1)}, bf16[256,768]{1,0:T(8,128)(2,1)S(1)}, u32[]{:S(2)}, u32[]{:S(2)}) %collective-permute-start.21) | collective-permute-done | bytes 393248 | tf_op jit(solution)/shard_map/ppermute | solution.py:640
  101.4 8.7 %collective-permute-start.25 = (f16[256,768]{1,0:T(8,128)(2,1)}, f16[256,768]{1,0:T(8,128)(2,1)S(1)}, u32[]{:S(2)}, u32[]{:S(2)}) collective-permute-start(f16[256,768]{1,0:T(8,128)(2,1)} %fusion.40), channel_id=1, source_target_pairs={{0,1},{1,0},{2,3},{3,2},{4,5},{5,4},{6,7},{7,6},{8,9},{9,8},{10,11... | collective-permute-start | bytes 1179656 | tf_op jit(solution)/shard_map/ppermute | solution.py:640
  110.1 2.3 copy.60
  115.0 3.6 collective-permute-start.24
  119.5 7.7 %shard_map.200 = (bf16[1024,192]{1,0:T(8,128)(2,1)S(1)}, bf16[1024,192]{1,0:T(8,128)(2,1)S(1)}, bf16[1024,192]{1,0:T(8,128)(2,1)S(1)}, f32[8,1024]{1,0:T(8,128)S(1)}, bf16[1024,192]{1,0:T(8,128)(2,1)S(1)}) custom-call(s32[1]{0:T(128)} %bitcast.17.me_ref, bf16[256,768]{1,0:T(8,128)(2,1)S(1)} %get-tuple-element.280.first0_ref, ...), custom_call_target="tpu_custom_call" | custom-call | flops 10000000 | bytes 65536 | tf_op jit(solution)/shard_map/pallas_call | solution.py:50
  135.0 7.8 %shard_map.202 = (bf16[16,2,24,1728]{3,2,1,0:T(8,128)(2,1)S(1)}, bf16[1024,192]{1,0:T(8,128)(2,1)S(1)}, bf16[1024,768]{1,0:T(8,128)(2,1)S(1)}, f32[8,768]{1,0:T(8,128)S(1)}) custom-call(bf16[256,768]{1,0:T(8,128)(2,1)S(1)} %bitcast_convert_fusion.refs_0_, bf16[256,768]{1,0:T(8,128)(2,1)S(1)} %collective-permute-done.22.refs_1_, ...), custom_call_target="tpu_custom_call" | custom-call | flops 10000000 | bytes 65536 | tf_op jit(solution)/shard_map/pallas_call | solution.py:50
  142.8 2.5 collective-permute-done.30
  146.1 10.9 %shard_map.204 = (bf16[1024,576]{1,0:T(8,128)(2,1)S(1)}, f32[2,256,768]{2,1,0:T(8,128)S(1)}, bf16[2,256,768]{2,1,0:T(8,128)(2,1)S(1)}, f32[8,768]{1,0:T(8,128)S(1)}, f32[8,576]{1,0:T(8,128)S(1)}) custom-call(s32[1]{0:T(128)} %bitcast.17.me_ref, bf16[1024,192]{1,0:T(8,128)(2,1)S(1)} %get-tuple-element.138.q_ref, ...), custom_call_target="tpu_custom_call" | custom-call | flops 10000000 | bytes 65536 | tf_op jit(solution)/shard_map/pallas_call | solution.py:50
  162.6 2.3 shard_map.208
  166.8 10.2 %all-to-all-start.1 = ((bf16[16,2,24,2320]{3,2,1,0:T(8,128)(2,1)}), bf16[16,2,24,2320]{3,2,1,0:T(8,128)(2,1)}, u32[]{:S(2)}, u32[]{:S(2)}) async-start(bf16[16,2,24,2320]{3,2,1,0:T(8,128)(2,1)} %copy-done), calls=%async_computation.1 | async-start | bytes 7471104 | tf_op jit(solution)/shard_map/all_to_all | solution.py:684
  179.2 3.0 fusion.55
  184.8 8.6 %collective-permute-done.34.refs_2_ = bf16[256,768]{1,0:T(8,128)(2,1)S(1)} collective-permute-done((bf16[256,768]{1,0:T(8,128)(2,1)S(1)}, bf16[256,768]{1,0:T(8,128)(2,1)S(1)}, u32[]{:S(2)}, u32[]{:S(2)}) %collective-permute-start.34) | collective-permute-done | bytes 393248 | tf_op jit(solution)/shard_map/ppermute | solution.py:640
  197.1 7.7 %shard_map.205 = (bf16[16,2,24,1728]{3,2,1,0:T(8,128)(2,1)S(1)}, bf16[1024,192]{1,0:T(8,128)(2,1)S(1)}, bf16[1024,768]{1,0:T(8,128)(2,1)S(1)}, f32[8,768]{1,0:T(8,128)S(1)}) custom-call(bf16[256,768]{1,0:T(8,128)(2,1)S(1)} %get-tuple-element.248.refs_0_, bf16[256,768]{1,0:T(8,128)(2,1)S(1)} %collective-permute-done.33.refs_1_, ...), custom_call_target="tpu_custom_call" | custom-call | flops 10000000 | bytes 65536 | tf_op jit(solution)/shard_map/pallas_call | solution.py:50
  204.9 12.2 %shard_map.206 = (bf16[1024,576]{1,0:T(8,128)(2,1)S(1)}, f32[2,256,768]{2,1,0:T(8,128)S(1)}, bf16[2,256,768]{2,1,0:T(8,128)(2,1)}, f32[8,768]{1,0:T(8,128)S(1)}, f32[8,576]{1,0:T(8,128)S(1)}) custom-call(s32[1]{0:T(128)} %bitcast.17.me_ref, bf16[1024,192]{1,0:T(8,128)(2,1)S(1)} %copy-done.45, bf16[1024,192]{1,0:T(8,128)(2,1)S(1)} %copy-done.47, ...), custom_call_target="tpu_custom_call" | custom-call | flops 10000000 | bytes 65536 | tf_op jit(solution)/shard_map/pallas_call | solution.py:50
  218.2 2.3 shard_map.207
  222.2 2.4 collective-permute-start.39
  226.1 2.4 collective-permute-start.42
  228.5 12.0 %collective-permute-done.38 = bf16[4,24,2320]{2,1,0:T(8,128)(2,1)S(1)} collective-permute-done((bf16[4,24,2320]{2,1,0:T(8,128)(2,1)S(1)}, bf16[4,24,2320]{2,1,0:T(8,128)(2,1)S(1)}, u32[]{:S(2)}, u32[]{:S(2)}) %collective-permute-start.38) | collective-permute-done | bytes 445472 | tf_op jit(solution)/shard_map/ppermute | solution.py:636
  242.2 9.1 %collective-permute-done.39 = bf16[4,24,2320]{2,1,0:T(8,128)(2,1)S(1)} collective-permute-done((bf16[4,24,2320]{2,1,0:T(8,128)(2,1)S(1)}, bf16[4,24,2320]{2,1,0:T(8,128)(2,1)S(1)}, u32[]{:S(2)}, u32[]{:S(2)}) %collective-permute-start.39) | collective-permute-done | bytes 445472 | tf_op jit(solution)/shard_map/ppermute | solution.py:636
  254.6 8.9 %collective-permute-done.43 = bf16[4,24,2320]{2,1,0:T(8,128)(2,1)} collective-permute-done((bf16[4,24,2320]{2,1,0:T(8,128)(2,1)S(1)}, bf16[4,24,2320]{2,1,0:T(8,128)(2,1)}, u32[]{:S(2)}, u32[]{:S(2)}) %collective-permute-start.43) | collective-permute-done | bytes 445472 | tf_op jit(solution)/shard_map/ppermute | solution.py:636
  263.5 2.7 convert_reduce_fusion
  269.2 3.9 %collective-permute-start.49 = (bf16[24,2320]{1,0:T(8,128)(2,1)S(1)}, bf16[24,2320]{1,0:T(8,128)(2,1)S(1)}, u32[]{:S(2)}, u32[]{:S(2)}) collective-permute-start(bf16[24,2320]{1,0:T(8,128)(2,1)S(1)} %get-tuple-element.271), channel_id=1, source_target_pairs={{0,12},{4,8},{8,4},{12,0},{16,28},{20,24},{24,20},{28,16},{32,44},... | collective-permute-start | bytes 334088 | tf_op jit(solution)/shard_map/ppermute | solution.py:636
  275.5 2.7 collective-permute-done.49
  280.7 3.5 collective-permute-done.46
  285.8 9.2 %all_to_all.20 = bf16[8,24,768]{2,1,0:T(8,128)(2,1)S(1)} all-to-all(bf16[8,24,768]{2,1,0:T(8,128)(2,1)S(1)} %get-tuple-element.181), channel_id=1, replica_groups={{0,16,32,48,64,80,96,112},{4,20,36,52,68,84,100,116},{8,24,40,56,72,88,..., dimensions={0} | all-to-all | bytes 589824 | tf_op jit(solution)/shard_map/all_to_all | solution.py:816
  295.0 2.6 collective-permute-start.52
  297.6 2.5 collective-permute-start.54
  300.2 2.3 collective-permute-done.52.refs_1_
  302.9 4.3 %collective-permute-start.56 = (bf16[2,192,768]{2,1,0:T(8,128)(2,1)S(1)}, bf16[2,192,768]{2,1,0:T(8,128)(2,1)S(1)}, u32[]{:S(2)}, u32[]{:S(2)}) collective-permute-start(bf16[2,192,768]{2,1,0:T(8,128)(2,1)S(1)} %pad_maximum_fusion), channel_id=1, source_target_pairs={{0,12},{4,8},{8,4},{12,0},{16,28},{20,24},{24,20},{28,16},{32,44},... | collective-permute-start | bytes 1769480 | tf_op jit(solution)/shard_map/ppermute | solution.py:636
  311.3 4.5 %collective-permute-start.59 = (bf16[192,768]{1,0:T(8,128)(2,1)S(1)}, bf16[192,768]{1,0:T(8,128)(2,1)S(1)}, u32[]{:S(2)}, u32[]{:S(2)}) collective-permute-start(bf16[192,768]{1,0:T(8,128)(2,1)S(1)} %bitcast.157), channel_id=1, source_target_pairs={{0,1},{1,0},{2,3},{3,2},{4,5},{5,4},{6,7},{7,6},{8,9},{9,8},{10,11... | collective-permute-start | bytes 884744 | tf_op jit(solution)/shard_map/ppermute | solution.py:640
  315.9 3.0 collective-permute-start.58
  319.0 5.7 %collective-permute-start.61 = (bf16[192,768]{1,0:T(8,128)(2,1)S(1)}, bf16[192,768]{1,0:T(8,128)(2,1)S(1)}, u32[]{:S(2)}, u32[]{:S(2)}) collective-permute-start(bf16[192,768]{1,0:T(8,128)(2,1)S(1)} %get-tuple-element.266.refs_2_), channel_id=1, source_target_pairs={{0,1},{1,0},{2,3},{3,2},{4,5},{5,4},{6,7},{7,6},{8,9},{9,8},{10,11... | collective-permute-start | bytes 884744 | tf_op jit(solution)/shard_map/ppermute | solution.py:640
  325.6 2.2 collective-permute-start.66
  331.5 36.2 %shard_map.210 = bf16[8,4,24,224]{3,2,1,0:T(8,128)(2,1)} custom-call(s32[2]{0:T(128)S(1)} %pad_add_fusion.1.place_ref, bf16[192,768]{1,0:T(8,128)(2,1)S(1)} %bitcast.158, bf16[192,768]{1,0:T(8,128)(2,1)S(1)} %collective-permute-done.52.refs_1_, bf16[192,768]{1,0:T(8,128)(2,1)S(1)} %get-tuple-element.266.refs_2_, ...), custom_call_target="tpu_custom_call" | custom-call | flops 10000000 | bytes 65536 | tf_op jit(solution)/shard_map/pallas_call | solution.py:50
  367.6 6.3 %all-to-all-start.3 = ((bf16[32,24,224]{2,1,0:T(8,128)(2,1)}), bf16[32,24,224]{2,1,0:T(8,128)(2,1)S(1)}, u32[]{:S(2)}, u32[]{:S(2)}) async-start(bf16[32,24,224]{2,1,0:T(8,128)(2,1)} %bitcast.59), calls=%async_computation.3 | async-start | bytes 786432 | tf_op jit(solution)/shard_map/all_to_all | solution.py:828
  374.1 2.4 add_bitcast_fusion
  376.5 6.7 %all-to-all-done.3.back_ref = bf16[32,24,224]{2,1,0:T(8,128)(2,1)S(1)} async-done(((bf16[32,24,224]{2,1,0:T(8,128)(2,1)}), bf16[32,24,224]{2,1,0:T(8,128)(2,1)S(1)}, u32[]{:S(2)}, u32[]{:S(2)}) %all-to-all-start.3) | async-done | bytes 344096 | tf_op jit(solution)/shard_map/all_to_all | solution.py:828
  (389 shorter events, 107.7 us)
Async XLA Ops:
  2.8 15.0 %collective-permute-start.7 = (bf16[24,2304]{1,0:T(8,128)(2,1)S(1)}, bf16[24,2304]{1,0:T(8,128)(2,1)S(1)}, u32[]{:S(2)}, u32[]{:S(2)}) collective-permute-start(bf16[24,2304]{1,0:T(8,128)(2,1)S(1)} %get-tuple-element.293), channel_id=1, source_target_pairs={{0,64},{4,68},{8,72},{12,76},{16,80},{20,84},{24,88},{28,92},{32,9... | collective-permute-start | bytes 331784 | tf_op jit(solution)/shard_map/ppermute | solution.py:636
  4.9 11.0 %collective-permute-start = (bf16[24,2304]{1,0:T(8,128)(2,1)S(1)}, bf16[24,2304]{1,0:T(8,128)(2,1)S(1)}, u32[]{:S(2)}, u32[]{:S(2)}) collective-permute-start(bf16[24,2304]{1,0:T(8,128)(2,1)S(1)} %get-tuple-element.293), channel_id=1, source_target_pairs={{0,16},{4,20},{8,24},{12,28},{16,0},{20,4},{24,8},{28,12},{32,48},... | collective-permute-start | bytes 331784 | tf_op jit(solution)/shard_map/ppermute | solution.py:636
  6.5 11.2 %collective-permute-start.1 = (bf16[24,2304]{1,0:T(8,128)(2,1)S(1)}, bf16[24,2304]{1,0:T(8,128)(2,1)S(1)}, u32[]{:S(2)}, u32[]{:S(2)}) collective-permute-start(bf16[24,2304]{1,0:T(8,128)(2,1)S(1)} %get-tuple-element.293), channel_id=1, source_target_pairs={{0,32},{4,36},{8,40},{12,44},{16,48},{20,52},{24,56},{28,60},{32,0... | collective-permute-start | bytes 331784 | tf_op jit(solution)/shard_map/ppermute | solution.py:636
  9.8 7.9 %collective-permute-start.2 = (bf16[24,2304]{1,0:T(8,128)(2,1)S(1)}, bf16[24,2304]{1,0:T(8,128)(2,1)S(1)}, u32[]{:S(2)}, u32[]{:S(2)}) collective-permute-start(bf16[24,2304]{1,0:T(8,128)(2,1)S(1)} %get-tuple-element.293), channel_id=1, source_target_pairs={{0,48},{4,52},{8,56},{12,60},{16,32},{20,36},{24,40},{28,44},{32,1... | collective-permute-start | bytes 331784 | tf_op jit(solution)/shard_map/ppermute | solution.py:636
  11.6 19.6 %collective-permute-start.17 = (f16[256,768]{1,0:T(8,128)(2,1)S(1)}, f16[256,768]{1,0:T(8,128)(2,1)S(1)}, u32[]{:S(2)}, u32[]{:S(2)}) collective-permute-start(f16[256,768]{1,0:T(8,128)(2,1)S(1)} %get-tuple-element.253), channel_id=1, source_target_pairs={{0,2},{1,3},{2,0},{3,1},{4,6},{5,7},{6,4},{7,5},{8,10},{9,11},{10,... | collective-permute-start | bytes 1179656 | tf_op jit(solution)/shard_map/ppermute | solution.py:640
  15.9 15.3 %collective-permute-start.16 = (f16[256,768]{1,0:T(8,128)(2,1)S(1)}, f16[256,768]{1,0:T(8,128)(2,1)S(1)}, u32[]{:S(2)}, u32[]{:S(2)}) collective-permute-start(f16[256,768]{1,0:T(8,128)(2,1)S(1)} %get-tuple-element.253), channel_id=1, source_target_pairs={{0,1},{1,0},{2,3},{3,2},{4,5},{5,4},{6,7},{7,6},{8,9},{9,8},{10,11... | collective-permute-start | bytes 1179656 | tf_op jit(solution)/shard_map/ppermute | solution.py:640
  17.8 7.5 %collective-permute-start.9 = (bf16[24,2304]{1,0:T(8,128)(2,1)S(1)}, bf16[24,2304]{1,0:T(8,128)(2,1)S(1)}, u32[]{:S(2)}, u32[]{:S(2)}) collective-permute-start(bf16[24,2304]{1,0:T(8,128)(2,1)S(1)} %collective-permute-done.7), channel_id=1, source_target_pairs={{0,8},{4,12},{8,0},{12,4},{16,24},{20,28},{24,16},{28,20},{32,40},... | collective-permute-start | bytes 331784 | tf_op jit(solution)/shard_map/ppermute | solution.py:636
  20.8 6.5 %collective-permute-start.10 = (bf16[24,2304]{1,0:T(8,128)(2,1)S(1)}, bf16[24,2304]{1,0:T(8,128)(2,1)S(1)}, u32[]{:S(2)}, u32[]{:S(2)}) collective-permute-start(bf16[24,2304]{1,0:T(8,128)(2,1)S(1)} %collective-permute-done.7), channel_id=1, source_target_pairs={{0,12},{4,8},{8,4},{12,0},{16,28},{20,24},{24,20},{28,16},{32,44},... | collective-permute-start | bytes 331784 | tf_op jit(solution)/shard_map/ppermute | solution.py:636
  25.3 11.6 %collective-permute-start.4 = (bf16[4,24,2304]{2,1,0:T(8,128)(2,1)S(1)}, bf16[4,24,2304]{2,1,0:T(8,128)(2,1)S(1)}, u32[]{:S(2)}, u32[]{:S(2)}) collective-permute-start(bf16[4,24,2304]{2,1,0:T(8,128)(2,1)S(1)} %pad_maximum_fusion.1.a0), channel_id=1, source_target_pairs={{0,12},{4,8},{8,4},{12,0},{16,28},{20,24},{24,20},{28,16},{32,44},... | collective-permute-start | bytes 1327112 | tf_op jit(solution)/shard_map/ppermute | solution.py:636
  27.3 11.0 %collective-permute-start.3 = (bf16[4,24,2304]{2,1,0:T(8,128)(2,1)S(1)}, bf16[4,24,2304]{2,1,0:T(8,128)(2,1)S(1)}, u32[]{:S(2)}, u32[]{:S(2)}) collective-permute-start(bf16[4,24,2304]{2,1,0:T(8,128)(2,1)S(1)} %pad_maximum_fusion.1.a0), channel_id=1, source_target_pairs={{0,4},{4,0},{8,12},{12,8},{16,20},{20,16},{24,28},{28,24},{32,36},... | collective-permute-start | bytes 1327112 | tf_op jit(solution)/shard_map/ppermute | solution.py:636
  28.1 13.6 %collective-permute-start.12 = (bf16[4,24,2304]{2,1,0:T(8,128)(2,1)S(1)}, bf16[4,24,2304]{2,1,0:T(8,128)(2,1)S(1)}, u32[]{:S(2)}, u32[]{:S(2)}) collective-permute-start(bf16[4,24,2304]{2,1,0:T(8,128)(2,1)S(1)} %pad_maximum_fusion.2.b0), channel_id=1, source_target_pairs={{0,48},{4,52},{8,56},{12,60},{16,32},{20,36},{24,40},{28,44},{32,1... | collective-permute-start | bytes 1327112 | tf_op jit(solution)/shard_map/ppermute | solution.py:636
  31.1 11.1 %collective-permute-start.11 = (bf16[4,24,2304]{2,1,0:T(8,128)(2,1)S(1)}, bf16[4,24,2304]{2,1,0:T(8,128)(2,1)S(1)}, u32[]{:S(2)}, u32[]{:S(2)}) collective-permute-start(bf16[4,24,2304]{2,1,0:T(8,128)(2,1)S(1)} %pad_maximum_fusion.2.b0), channel_id=1, source_target_pairs={{0,16},{4,20},{8,24},{12,28},{16,0},{20,4},{24,8},{28,12},{32,48},... | collective-permute-start | bytes 1327112 | tf_op jit(solution)/shard_map/ppermute | solution.py:636
  31.2 13.8 %collective-permute-start.18 = (f16[256,768]{1,0:T(8,128)(2,1)S(1)}, f16[256,768]{1,0:T(8,128)(2,1)S(1)}, u32[]{:S(2)}, u32[]{:S(2)}) collective-permute-start(f16[256,768]{1,0:T(8,128)(2,1)S(1)} %collective-permute-done.17), channel_id=1, source_target_pairs={{0,1},{1,0},{2,3},{3,2},{4,5},{5,4},{6,7},{7,6},{8,9},{9,8},{10,11... | collective-permute-start | bytes 1179656 | tf_op jit(solution)/shard_map/ppermute | solution.py:640
  37.0 10.9 %collective-permute-start.5 = (bf16[2,24,2304]{2,1,0:T(8,128)(2,1)S(1)}, bf16[2,24,2304]{2,1,0:T(8,128)(2,1)S(1)}, u32[]{:S(2)}, u32[]{:S(2)}) collective-permute-start(bf16[2,24,2304]{2,1,0:T(8,128)(2,1)S(1)} %slice.262), channel_id=1, source_target_pairs={{0,4},{4,0},{8,12},{12,8},{16,20},{20,16},{24,28},{28,24},{32,36},... | collective-permute-start | bytes 663560 | tf_op jit(solution)/shard_map/ppermute | solution.py:636
  38.4 9.6 %collective-permute-start.6 = (bf16[2,24,2304]{2,1,0:T(8,128)(2,1)S(1)}, bf16[2,24,2304]{2,1,0:T(8,128)(2,1)S(1)}, u32[]{:S(2)}, u32[]{:S(2)}) collective-permute-start(bf16[2,24,2304]{2,1,0:T(8,128)(2,1)S(1)} %slice.263), channel_id=1, source_target_pairs={{0,12},{4,8},{8,4},{12,0},{16,28},{20,24},{24,20},{28,16},{32,44},... | collective-permute-start | bytes 663560 | tf_op jit(solution)/shard_map/ppermute | solution.py:636
  51.2 45.5 %all-to-all-start = ((bf16[16,2,24,2304]{3,2,1,0:T(8,128)(2,1)}), bf16[16,2,24,2304]{3,2,1,0:T(8,128)(2,1)}, u32[]{:S(2)}, u32[]{:S(2)}) async-start(bf16[16,2,24,2304]{3,2,1,0:T(8,128)(2,1)} %concatenate.9), calls=%async_computation | async-start | bytes 7077888 | tf_op jit(solution)/shard_map/all_to_all | solution.py:665
  81.6 12.2 %collective-permute-start.21 = (bf16[256,768]{1,0:T(8,128)(2,1)S(1)}, bf16[256,768]{1,0:T(8,128)(2,1)S(1)}, u32[]{:S(2)}, u32[]{:S(2)}) collective-permute-start(bf16[256,768]{1,0:T(8,128)(2,1)S(1)} %add_convert_fusion.3), channel_id=1, source_target_pairs={{0,2},{1,3},{2,0},{3,1},{4,6},{5,7},{6,4},{7,5},{8,10},{9,11},{10,... | collective-permute-start | bytes 1179656 | tf_op jit(solution)/shard_map/ppermute | solution.py:640
  96.7 15.7 %collective-permute-start.26 = (f16[256,768]{1,0:T(8,128)(2,1)}, f16[256,768]{1,0:T(8,128)(2,1)S(1)}, u32[]{:S(2)}, u32[]{:S(2)}) collective-permute-start(f16[256,768]{1,0:T(8,128)(2,1)} %fusion.40), channel_id=1, source_target_pairs={{0,2},{1,3},{2,0},{3,1},{4,6},{5,7},{6,4},{7,5},{8,10},{9,11},{10,... | collective-permute-start | bytes 1179656 | tf_op jit(solution)/shard_map/ppermute | solution.py:640
  99.3 15.7 %collective-permute-start.23 = (bf16[256,768]{1,0:T(8,128)(2,1)S(1)}, bf16[256,768]{1,0:T(8,128)(2,1)S(1)}, u32[]{:S(2)}, u32[]{:S(2)}) collective-permute-start(bf16[256,768]{1,0:T(8,128)(2,1)S(1)} %bitcast_convert_fusion.refs_0_), channel_id=1, source_target_pairs={{0,2},{1,3},{2,0},{3,1},{4,6},{5,7},{6,4},{7,5},{8,10},{9,11},{10,... | collective-permute-start | bytes 1179656 | tf_op jit(solution)/shard_map/ppermute | solution.py:640
  101.4 17.1 %collective-permute-start.25 = (f16[256,768]{1,0:T(8,128)(2,1)}, f16[256,768]{1,0:T(8,128)(2,1)S(1)}, u32[]{:S(2)}, u32[]{:S(2)}) collective-permute-start(f16[256,768]{1,0:T(8,128)(2,1)} %fusion.40), channel_id=1, source_target_pairs={{0,1},{1,0},{2,3},{3,2},{4,5},{5,4},{6,7},{7,6},{8,9},{9,8},{10,11... | collective-permute-start | bytes 1179656 | tf_op jit(solution)/shard_map/ppermute | solution.py:640
  114.3 20.7 %collective-permute-start.22 = (bf16[256,768]{1,0:T(8,128)(2,1)S(1)}, bf16[256,768]{1,0:T(8,128)(2,1)S(1)}, u32[]{:S(2)}, u32[]{:S(2)}) collective-permute-start(bf16[256,768]{1,0:T(8,128)(2,1)S(1)} %bitcast_convert_fusion.refs_0_), channel_id=1, source_target_pairs={{0,1},{1,0},{2,3},{3,2},{4,5},{5,4},{6,7},{7,6},{8,9},{9,8},{10,11... | collective-permute-start | bytes 1179656 | tf_op jit(solution)/shard_map/ppermute | solution.py:640
  115.0 20.0 %collective-permute-start.24 = (bf16[256,768]{1,0:T(8,128)(2,1)S(1)}, bf16[256,768]{1,0:T(8,128)(2,1)S(1)}, u32[]{:S(2)}, u32[]{:S(2)}) collective-permute-start(bf16[256,768]{1,0:T(8,128)(2,1)S(1)} %collective-permute-done.23.refs_2_), channel_id=1, source_target_pairs={{0,1},{1,0},{2,3},{3,2},{4,5},{5,4},{6,7},{7,6},{8,9},{9,8},{10,11... | collective-permute-start | bytes 1179656 | tf_op jit(solution)/shard_map/ppermute | solution.py:640
  133.2 9.6 %collective-permute-start.29 = (bf16[256,768]{1,0:T(8,128)(2,1)S(1)}, bf16[256,768]{1,0:T(8,128)(2,1)S(1)}, u32[]{:S(2)}, u32[]{:S(2)}) collective-permute-start(bf16[256,768]{1,0:T(8,128)(2,1)S(1)} %get-tuple-element.133), channel_id=1, source_target_pairs={{0,1},{1,0},{2,3},{3,2},{4,5},{5,4},{6,7},{7,6},{8,9},{9,8},{10,11... | collective-permute-start | bytes 1179656 | tf_op jit(solution)/shard_map/ppermute | solution.py:640
  133.4 12.0 %collective-permute-start.30 = (bf16[256,768]{1,0:T(8,128)(2,1)S(1)}, bf16[256,768]{1,0:T(8,128)(2,1)S(1)}, u32[]{:S(2)}, u32[]{:S(2)}) collective-permute-start(bf16[256,768]{1,0:T(8,128)(2,1)S(1)} %add_convert_fusion.2), channel_id=1, source_target_pairs={{0,2},{1,3},{2,0},{3,1},{4,6},{5,7},{6,4},{7,5},{8,10},{9,11},{10,... | collective-permute-start | bytes 1179656 | tf_op jit(solution)/shard_map/ppermute | solution.py:640
  161.2 15.8 %collective-permute-start.32 = (bf16[256,768]{1,0:T(8,128)(2,1)}, bf16[256,768]{1,0:T(8,128)(2,1)}, u32[]{:S(2)}, u32[]{:S(2)}) collective-permute-start(bf16[256,768]{1,0:T(8,128)(2,1)} %fusion.41), channel_id=1, source_target_pairs={{0,2},{1,3},{2,0},{3,1},{4,6},{5,7},{6,4},{7,5},{8,10},{9,11},{10,... | collective-permute-start | bytes 1179656 | tf_op jit(solution)/shard_map/ppermute | solution.py:640
  166.8 96.8 %all-to-all-start.1 = ((bf16[16,2,24,2320]{3,2,1,0:T(8,128)(2,1)}), bf16[16,2,24,2320]{3,2,1,0:T(8,128)(2,1)}, u32[]{:S(2)}, u32[]{:S(2)}) async-start(bf16[16,2,24,2320]{3,2,1,0:T(8,128)(2,1)} %copy-done), calls=%async_computation.1 | async-start | bytes 7471104 | tf_op jit(solution)/shard_map/all_to_all | solution.py:684
  182.2 11.3 %collective-permute-start.34 = (bf16[256,768]{1,0:T(8,128)(2,1)S(1)}, bf16[256,768]{1,0:T(8,128)(2,1)S(1)}, u32[]{:S(2)}, u32[]{:S(2)}) collective-permute-start(bf16[256,768]{1,0:T(8,128)(2,1)S(1)} %get-tuple-element.248.refs_0_), channel_id=1, source_target_pairs={{0,2},{1,3},{2,0},{3,1},{4,6},{5,7},{6,4},{7,5},{8,10},{9,11},{10,... | collective-permute-start | bytes 1179656 | tf_op jit(solution)/shard_map/ppermute | solution.py:640
  183.6 12.0 %collective-permute-start.33 = (bf16[256,768]{1,0:T(8,128)(2,1)S(1)}, bf16[256,768]{1,0:T(8,128)(2,1)S(1)}, u32[]{:S(2)}, u32[]{:S(2)}) collective-permute-start(bf16[256,768]{1,0:T(8,128)(2,1)S(1)} %get-tuple-element.248.refs_0_), channel_id=1, source_target_pairs={{0,1},{1,0},{2,3},{3,2},{4,5},{5,4},{6,7},{7,6},{8,9},{9,8},{10,11... | collective-permute-start | bytes 1179656 | tf_op jit(solution)/shard_map/ppermute | solution.py:640
  220.8 19.7 %collective-permute-start.38 = (bf16[4,24,2320]{2,1,0:T(8,128)(2,1)S(1)}, bf16[4,24,2320]{2,1,0:T(8,128)(2,1)S(1)}, u32[]{:S(2)}, u32[]{:S(2)}) collective-permute-start(bf16[4,24,2320]{2,1,0:T(8,128)(2,1)S(1)} %get-tuple-element.260), channel_id=1, source_target_pairs={{0,4},{4,0},{8,12},{12,8},{16,20},{20,16},{24,28},{28,24},{32,36},... | collective-permute-start | bytes 1336328 | tf_op jit(solution)/shard_map/ppermute | solution.py:636
  222.2 29.0 %collective-permute-start.39 = (bf16[4,24,2320]{2,1,0:T(8,128)(2,1)S(1)}, bf16[4,24,2320]{2,1,0:T(8,128)(2,1)S(1)}, u32[]{:S(2)}, u32[]{:S(2)}) collective-permute-start(bf16[4,24,2320]{2,1,0:T(8,128)(2,1)S(1)} %get-tuple-element.259), channel_id=1, source_target_pairs={{0,8},{4,12},{8,0},{12,4},{16,24},{20,28},{24,16},{28,20},{32,40},... | collective-permute-start | bytes 1336328 | tf_op jit(solution)/shard_map/ppermute | solution.py:636
  224.6 28.4 %collective-permute-start.40 = (bf16[4,24,2320]{2,1,0:T(8,128)(2,1)S(1)}, bf16[4,24,2320]{2,1,0:T(8,128)(2,1)S(1)}, u32[]{:S(2)}, u32[]{:S(2)}) collective-permute-start(bf16[4,24,2320]{2,1,0:T(8,128)(2,1)S(1)} %get-tuple-element.258), channel_id=1, source_target_pairs={{0,12},{4,8},{8,4},{12,0},{16,28},{20,24},{24,20},{28,16},{32,44},... | collective-permute-start | bytes 1336328 | tf_op jit(solution)/shard_map/ppermute | solution.py:636
  224.8 28.3 %collective-permute-start.41 = (bf16[4,24,2320]{2,1,0:T(8,128)(2,1)S(1)}, bf16[4,24,2320]{2,1,0:T(8,128)(2,1)S(1)}, u32[]{:S(2)}, u32[]{:S(2)}) collective-permute-start(bf16[4,24,2320]{2,1,0:T(8,128)(2,1)S(1)} %get-tuple-element.256), channel_id=1, source_target_pairs={{0,16},{4,20},{8,24},{12,28},{16,0},{20,4},{24,8},{28,12},{32,48},... | collective-permute-start | bytes 1336328 | tf_op jit(solution)/shard_map/ppermute | solution.py:636
  226.1 27.3 %collective-permute-start.42 = (bf16[4,24,2320]{2,1,0:T(8,128)(2,1)S(1)}, bf16[4,24,2320]{2,1,0:T(8,128)(2,1)S(1)}, u32[]{:S(2)}, u32[]{:S(2)}) collective-permute-start(bf16[4,24,2320]{2,1,0:T(8,128)(2,1)S(1)} %get-tuple-element.255), channel_id=1, source_target_pairs={{0,32},{4,36},{8,40},{12,44},{16,48},{20,52},{24,56},{28,60},{32,0... | collective-permute-start | bytes 1336328 | tf_op jit(solution)/shard_map/ppermute | solution.py:636
  240.5 23.0 %collective-permute-start.43 = (bf16[4,24,2320]{2,1,0:T(8,128)(2,1)S(1)}, bf16[4,24,2320]{2,1,0:T(8,128)(2,1)}, u32[]{:S(2)}, u32[]{:S(2)}) collective-permute-start(bf16[4,24,2320]{2,1,0:T(8,128)(2,1)S(1)} %get-tuple-element.254), channel_id=1, source_target_pairs={{0,48},{4,52},{8,56},{12,60},{16,32},{20,36},{24,40},{28,44},{32,1... | collective-permute-start | bytes 1336328 | tf_op jit(solution)/shard_map/ppermute | solution.py:636
  251.3 51.4 %collective-permute-start.36 = (bf16[2,256,768]{2,1,0:T(8,128)(2,1)}, bf16[2,256,768]{2,1,0:T(8,128)(2,1)S(1)}, u32[]{:S(2)}, u32[]{:S(2)}) collective-permute-start(bf16[2,256,768]{2,1,0:T(8,128)(2,1)} %get-tuple-element.158), channel_id=1, source_target_pairs={{0,1},{1,0},{2,3},{3,2},{4,5},{5,4},{6,7},{7,6},{8,9},{9,8},{10,11... | collective-permute-start | bytes 2359304 | tf_op jit(solution)/shard_map/ppermute | solution.py:640
  266.3 12.0 %collective-permute-start.51 = (bf16[24,2320]{1,0:T(8,128)(2,1)S(1)}, bf16[24,2320]{1,0:T(8,128)(2,1)S(1)}, u32[]{:S(2)}, u32[]{:S(2)}) collective-permute-start(bf16[24,2320]{1,0:T(8,128)(2,1)S(1)} %fusion.49), channel_id=1, source_target_pairs={{0,64},{4,68},{8,72},{12,76},{16,80},{20,84},{24,88},{28,92},{32,9... | collective-permute-start | bytes 334088 | tf_op jit(solution)/shard_map/ppermute | solution.py:636
  269.2 9.0 %collective-permute-start.49 = (bf16[24,2320]{1,0:T(8,128)(2,1)S(1)}, bf16[24,2320]{1,0:T(8,128)(2,1)S(1)}, u32[]{:S(2)}, u32[]{:S(2)}) collective-permute-start(bf16[24,2320]{1,0:T(8,128)(2,1)S(1)} %get-tuple-element.271), channel_id=1, source_target_pairs={{0,12},{4,8},{8,4},{12,0},{16,28},{20,24},{24,20},{28,16},{32,44},... | collective-permute-start | bytes 334088 | tf_op jit(solution)/shard_map/ppermute | solution.py:636
  295.0 7.5 %collective-permute-start.52 = (bf16[192,768]{1,0:T(8,128)(2,1)S(1)}, bf16[192,768]{1,0:T(8,128)(2,1)S(1)}, u32[]{:S(2)}, u32[]{:S(2)}) collective-permute-start(bf16[192,768]{1,0:T(8,128)(2,1)S(1)} %bitcast.155), channel_id=1, source_target_pairs={{0,2},{1,3},{2,0},{3,1},{4,6},{5,7},{6,4},{7,5},{8,10},{9,11},{10,... | collective-permute-start | bytes 884744 | tf_op jit(solution)/shard_map/ppermute | solution.py:640
  297.6 9.5 %collective-permute-start.54 = (f32[24,10]{1,0:T(8,128)S(1)}, f32[24,10]{1,0:T(8,128)S(1)}, u32[]{:S(2)}, u32[]{:S(2)}) collective-permute-start(f32[24,10]{1,0:T(8,128)S(1)} %bitcast.164), channel_id=1, source_target_pairs={{0,1},{1,0},{2,3},{3,2},{4,5},{5,4},{6,7},{7,6},{8,9},{9,8},{10,11... | collective-permute-start | bytes 2888 | tf_op jit(solution)/shard_map/ppermute | solution.py:640
  302.6 13.3 %collective-permute-start.53 = (bf16[2,192,768]{2,1,0:T(8,128)(2,1)S(1)}, bf16[2,192,768]{2,1,0:T(8,128)(2,1)S(1)}, u32[]{:S(2)}, u32[]{:S(2)}) collective-permute-start(bf16[2,192,768]{2,1,0:T(8,128)(2,1)S(1)} %pad_maximum_fusion), channel_id=1, source_target_pairs={{0,4},{4,0},{8,12},{12,8},{16,20},{20,16},{24,28},{28,24},{32,36},... | collective-permute-start | bytes 1769480 | tf_op jit(solution)/shard_map/ppermute | solution.py:636
  302.9 16.0 %collective-permute-start.56 = (bf16[2,192,768]{2,1,0:T(8,128)(2,1)S(1)}, bf16[2,192,768]{2,1,0:T(8,128)(2,1)S(1)}, u32[]{:S(2)}, u32[]{:S(2)}) collective-permute-start(bf16[2,192,768]{2,1,0:T(8,128)(2,1)S(1)} %pad_maximum_fusion), channel_id=1, source_target_pairs={{0,12},{4,8},{8,4},{12,0},{16,28},{20,24},{24,20},{28,16},{32,44},... | collective-permute-start | bytes 1769480 | tf_op jit(solution)/shard_map/ppermute | solution.py:636
  308.7 10.3 %collective-permute-start.37 = (bf16[256,768]{1,0:T(8,128)(2,1)S(1)}, bf16[256,768]{1,0:T(8,128)(2,1)S(1)}, u32[]{:S(2)}, u32[]{:S(2)}) collective-permute-start(bf16[256,768]{1,0:T(8,128)(2,1)S(1)} %fusion.42), channel_id=1, source_target_pairs={{0,2},{1,3},{2,0},{3,1},{4,6},{5,7},{6,4},{7,5},{8,10},{9,11},{10,... | collective-permute-start | bytes 1179656 | tf_op jit(solution)/shard_map/ppermute | solution.py:640
  311.3 13.7 %collective-permute-start.59 = (bf16[192,768]{1,0:T(8,128)(2,1)S(1)}, bf16[192,768]{1,0:T(8,128)(2,1)S(1)}, u32[]{:S(2)}, u32[]{:S(2)}) collective-permute-start(bf16[192,768]{1,0:T(8,128)(2,1)S(1)} %bitcast.157), channel_id=1, source_target_pairs={{0,1},{1,0},{2,3},{3,2},{4,5},{5,4},{6,7},{7,6},{8,9},{9,8},{10,11... | collective-permute-start | bytes 884744 | tf_op jit(solution)/shard_map/ppermute | solution.py:640
  315.8 9.2 %collective-permute-start.60 = (bf16[192,768]{1,0:T(8,128)(2,1)S(1)}, bf16[192,768]{1,0:T(8,128)(2,1)S(1)}, u32[]{:S(2)}, u32[]{:S(2)}) collective-permute-start(bf16[192,768]{1,0:T(8,128)(2,1)S(1)} %collective-permute-done.52.refs_1_), channel_id=1, source_target_pairs={{0,1},{1,0},{2,3},{3,2},{4,5},{5,4},{6,7},{7,6},{8,9},{9,8},{10,11... | collective-permute-start | bytes 884744 | tf_op jit(solution)/shard_map/ppermute | solution.py:640
  315.9 9.7 %collective-permute-start.58 = (bf16[192,768]{1,0:T(8,128)(2,1)S(1)}, bf16[192,768]{1,0:T(8,128)(2,1)S(1)}, u32[]{:S(2)}, u32[]{:S(2)}) collective-permute-start(bf16[192,768]{1,0:T(8,128)(2,1)S(1)} %get-tuple-element.265.refs_3_), channel_id=1, source_target_pairs={{0,12},{4,8},{8,4},{12,0},{16,28},{20,24},{24,20},{28,16},{32,44},... | collective-permute-start | bytes 884744 | tf_op jit(solution)/shard_map/ppermute | solution.py:636
  318.9 8.8 %collective-permute-start.57 = (bf16[192,768]{1,0:T(8,128)(2,1)S(1)}, bf16[192,768]{1,0:T(8,128)(2,1)S(1)}, u32[]{:S(2)}, u32[]{:S(2)}) collective-permute-start(bf16[192,768]{1,0:T(8,128)(2,1)S(1)} %get-tuple-element.264.refs_6_), channel_id=1, source_target_pairs={{0,4},{4,0},{8,12},{12,8},{16,20},{20,16},{24,28},{28,24},{32,36},... | collective-permute-start | bytes 884744 | tf_op jit(solution)/shard_map/ppermute | solution.py:636
  319.0 10.8 %collective-permute-start.61 = (bf16[192,768]{1,0:T(8,128)(2,1)S(1)}, bf16[192,768]{1,0:T(8,128)(2,1)S(1)}, u32[]{:S(2)}, u32[]{:S(2)}) collective-permute-start(bf16[192,768]{1,0:T(8,128)(2,1)S(1)} %get-tuple-element.266.refs_2_), channel_id=1, source_target_pairs={{0,1},{1,0},{2,3},{3,2},{4,5},{5,4},{6,7},{7,6},{8,9},{9,8},{10,11... | collective-permute-start | bytes 884744 | tf_op jit(solution)/shard_map/ppermute | solution.py:640
  367.6 15.5 %all-to-all-start.3 = ((bf16[32,24,224]{2,1,0:T(8,128)(2,1)}), bf16[32,24,224]{2,1,0:T(8,128)(2,1)S(1)}, u32[]{:S(2)}, u32[]{:S(2)}) async-start(bf16[32,24,224]{2,1,0:T(8,128)(2,1)} %bitcast.59), calls=%async_computation.3 | async-start | bytes 786432 | tf_op jit(solution)/shard_map/all_to_all | solution.py:828
  (121 other events, 959.6 us)
